TPU v7x, 32 devices: a whole 2x2x4 slice. The times are simulated.
32 devices in a mesh: speech: 4 (over y, core), text: 8 (over z, x).
Axes of the slice: x: 2, y: 2, z: 4, core: 2. Of those that a mesh axis runs over, the one named last changes fastest.
Arguments:
- speech_feat: float32 [2048, 512], P('speech', 'text'), may hold values from -4 to 4
- text_feat: float32 [16384, 512], P(('text', 'speech')), may hold values from -4 to 4
- text_pot: float32 [16384], P('text'), may hold values from -1 to 1
- map_grad: float32 [2048, 512], P('speech', 'text'), may hold values from -1024 to 1024
Outputs:
- speech_grad: float32 [2048, 512], P('speech', 'text')
- text_grad: float32 [16384, 512], P(('text', 'speech'))
All inputs are finite; a program needn't handle non-finite values.
Results may differ from a plain program's by a relative error of at most 0.0003.
Values sent between devices are 32-bit elements; how exact they have to be, the bound alone decides.
No kernel may reach another device: no remote copies, remote signals or barrier semaphores. Data moves between devices by JAX's collectives and lax.ppermute only.
A program may use at most 64 MiB of HBM per device.

v0:
```python
import functools
import math

import jax
import jax.numpy as jnp
from jax import lax
from jax.experimental import pallas as pl
from jax.experimental.pallas import tpu as pltpu
from jax.sharding import PartitionSpec as P

LONG, SHORT = 10**11, 10**9
WORK = {
    "plan_early": LONG,
    "plan_late": 3 * SHORT,
    "moments": 3 * SHORT,
    "text_far": 3 * SHORT,
    "text_near": 3 * SHORT,
    "finish": SHORT,
    "frames_first": SHORT,
    "split": SHORT // 2,
    "offsets": SHORT // 10,
    "add": LONG,
}
VMEM_LIMIT = 16 * 1024 * 1024
LANES = 128
IN_VMEM = pl.BlockSpec(memory_space=pltpu.VMEM)
IN_SMEM = pl.BlockSpec(memory_space=pltpu.SMEM)
ANYWHERE = pl.BlockSpec(memory_space=pl.ANY)


def halves(value):
    high = value.astype(jnp.bfloat16)
    low = (value - high.astype(jnp.float32)).astype(jnp.bfloat16)
    return (high, low)


def dot(left, right):
    return lax.dot_general(left, right, (((1,), (0,)), ((), ())), preferred_element_type=jnp.float32)


def dot3(left, right):
    return dot(left[0], right[0]) + dot(left[0], right[1]) + dot(left[1], right[0])


def call(kernel, name, operands, outs, places=0, before=(), scratch=()):
    several = isinstance(outs, list)
    shapes = [jax.ShapeDtypeStruct(shape, kind) for shape, kind in (outs if several else [outs])]
    count = len(operands)

    def body(*refs):
        kernel(*refs[:count], *refs[count + len(before) :])

    return pl.pallas_call(
        body,
        in_specs=[IN_SMEM] * places + [IN_VMEM] * (count - places) + [ANYWHERE] * len(before),
        out_shape=shapes if several else shapes[0],
        scratch_shapes=list(scratch),
        compiler_params=pltpu.CompilerParams(vmem_limit_bytes=VMEM_LIMIT),
        cost_estimate=pl.CostEstimate(flops=WORK.get(name, 0), bytes_accessed=0, transcendentals=0),
        name=name,
    )(*operands, *before)


def copy_kernel(value, out):
    out[...] = value[...]


def add_kernel(*refs):
    *terms, out = refs
    total = terms[0][...]
    for term in terms[1:]:
        total = total + term[...]
    out[...] = total


def split_kernel(block, high_out, low_out, across_high, across_low):
    value = block[...]
    high_out[...], low_out[...] = halves(value)
    across_high[...], across_low[...] = halves(value.T)


def split_block(block):
    rows, feats = block.shape
    plain, across = ((rows, feats), jnp.bfloat16), ((feats, rows), jnp.bfloat16)
    return call(split_kernel, "split", [block], [plain, plain, across, across])


def assemble(place, speech_chunks, grad_chunks, left):
    frames = speech_chunks[0].shape[1]
    for part, chunks in enumerate((speech_chunks, grad_chunks)):
        columns = slice(part * frames, (part + 1) * frames)
        for k, chunk in enumerate(chunks):
            width = chunk.shape[0]
            start = pl.multiple_of((place[0] ^ k) * width, width)
            left[0][pl.ds(start, width), columns], left[1][pl.ds(start, width), columns] = halves(chunk[...])


def offsets_kernel(place, pot, out):
    count, rows = pot.shape
    for r in range(count):
        row = pot[pl.ds(place[1] ^ r, 1), :]
        out[r * rows : (r + 1) * rows, :] = jnp.broadcast_to(row, (out.shape[1], rows)).T


def plan_rows(scale, place, first, pot, blocks, left, plan_out, dots_out, sums_out):
    count = len(blocks) // 2
    frames = plan_out.shape[1]
    rows = blocks[0].shape[0]
    for r in range(count):
        here = slice(r * rows, (r + 1) * rows)
        product = dot3((blocks[r][...], blocks[count + r][...]), (left[0][...], left[1][...]))
        offsets = pot[(first + r) * rows : (first + r + 1) * rows, :]
        lanes = offsets.shape[1]
        plan = jnp.concatenate(
            [jnp.exp(offsets + scale * product[:, i : i + lanes]) for i in range(0, frames, lanes)], axis=1
        )
        grad_dots = product[:, frames:]
        plan_out[here, :] = plan
        dots_out[here, :] = grad_dots
        sums_out[0:1, :] += jnp.sum(plan, axis=0, keepdims=True)
        sums_out[1:2, :] += jnp.sum(plan * grad_dots, axis=0, keepdims=True)


def early_kernel(n_text, scale, place, pot, *refs):
    chunks, blocks = refs[:n_text], refs[n_text:-5]
    plan_out, dots_out, sums_out, *left = refs[-5:]
    width = chunks[0].shape[0] // 2
    assemble(place, [chunk.at[:width] for chunk in chunks], [chunk.at[width:] for chunk in chunks], left)
    sums_out[...] = jnp.zeros_like(sums_out)
    plan_rows(scale, place, 0, pot, blocks, left, plan_out, dots_out, sums_out)


def late_kernel(scale, first, place, pot, sums, left_high, left_low, *refs):
    blocks = refs[:-3]
    plan_out, dots_out, sums_out = refs[-3:]
    sums_out[...] = sums[...]
    plan_rows(scale, place, first, pot, blocks, (left_high, left_low), plan_out, dots_out, sums_out)


def across_kernel(high, low, high_out, low_out):
    for value, out in ((high, high_out), (low, low_out)):
        out[...] = value[...].astype(jnp.float32).T.astype(jnp.bfloat16)


def weights(sums, plan, grad_dots, scale):
    mass = sums[0:1, :]
    shared = plan / mass
    weighted = scale * (shared * (grad_dots - sums[1:2, :] / mass))
    return (shared, weighted)


def text_kernel(scale, first, sums, plan, grad_dots, right_high, right_low, *outs):
    rows = len(outs) * outs[0].shape[0]
    here = slice(first, first + rows)
    shared, weighted = weights(sums, plan[here, :], grad_dots[here, :], scale)
    shared, weighted = halves(shared), halves(weighted)
    left = [jnp.concatenate([w, s], axis=1) for w, s in zip(weighted, shared)]
    terms = dot3(left, (right_high[...], right_low[...]))
    for i, out in enumerate(outs):
        out[...] = terms[i * out.shape[0] : (i + 1) * out.shape[0], :]


def moments_kernel(first, rows, estimate, plan, grad_dots, high, low, *refs):
    *total, out = refs
    here = slice(first, first + rows)
    tile = plan[here, :]
    centred = tile * (grad_dots[here, :] - estimate[1:2, :] / estimate[0:1, :])
    term = dot3((high[...], low[...]), halves(jnp.concatenate([tile, centred], axis=1)))
    out[...] = total[0][...] + term if total else term


def finish_kernel(n_text, scale, first, place, estimate, sums, total, plan, grad_dots, high, low, near, far, terms):
    frames = sums.shape[1]
    mass = sums[0:1, :]
    drift = sums[1:2, :] / mass - estimate[1:2, :] / estimate[0:1, :]
    here = slice(first, first + high.shape[1])
    _, weighted = weights(sums, plan[here, :], grad_dots[here, :], scale)
    terms[...] = dot3((high[...], low[...]), halves(weighted))
    width = total.shape[0] // n_text
    for k in range(n_text):
        here = pl.ds(pl.multiple_of((place[0] ^ k) * width, width), width)
        block = (scale / mass) * (total[here, frames:] - drift * total[here, :frames])
        (far if k % 2 else near)[k // 2] = block + terms[here, :]


def shards(n_speech, n_text, speech_feat, text_feat, text_pot, map_grad):
    def swap(value, axis, k):
        count = {"speech": n_speech, "text": n_text}[axis]
        return lax.ppermute(value, axis, [(i, i ^ k) for i in range(count)])

    rows, feats = text_feat.shape
    frames, width = speech_feat.shape
    scale = 1.0 / math.sqrt(feats)
    place = jnp.stack([lax.axis_index("text"), lax.axis_index("speech")]).astype(jnp.int32)
    pot = call(
        offsets_kernel,
        "offsets",
        [place, text_pot.reshape(n_speech, rows)],
        ((n_speech * rows, LANES), jnp.float32),
        places=1,
    )

    blocks = [text_feat] + [None] * (n_speech - 1)
    for r in range(2, n_speech, 2):
        blocks[r] = swap(text_feat, "speech", r)
    blocks[1] = swap(text_feat, "speech", 1)
    packed = jnp.concatenate([speech_feat.T, map_grad.T], axis=0)
    packed = call(copy_kernel, "copy", [packed], (packed.shape, packed.dtype), before=[blocks[1]])
    chunks = [packed] + [None] * (n_text - 1)
    for k in range(1, n_text):
        if k & (k - 1) == 0:
            chunks[k] = swap(packed, "text", k)
    for k in range(3, n_text):
        if k & (k - 1):
            step = k & -k
            source = chunks[k ^ step]
            wanted = [chunks[1], chunks[2]] if step > 1 else [chunks[3]] if 3 < k == n_text - 1 else []
            if wanted:
                source = call(copy_kernel, "copy", [source], (source.shape, source.dtype), before=wanted)
            chunks[k] = swap(source, "text", step)
    for r in range(2, n_speech, 2):
        blocks[r + 1] = swap(blocks[r], "speech", 1)
    highs, lows, across_highs, across_lows = zip(*map(split_block, blocks))

    half = n_speech // 2
    tile = ((half * rows, frames), jnp.float32)
    outs = [tile, tile, ((8, frames), jnp.float32)]
    left_shape = ((feats, 2 * frames), jnp.bfloat16)
    plan_early, dots_early, sums, *left = call(
        functools.partial(early_kernel, n_text, scale),
        "plan_early",
        [place, pot, *chunks, *highs[:half], *lows[:half]],
        [*outs, left_shape, left_shape],
        places=1,
    )
    plan_late, dots_late, sums = call(
        functools.partial(late_kernel, scale, half),
        "plan_late",
        [place, pot, sums, *left, *highs[half:], *lows[half:]],
        outs,
        places=1,
    )
    plans, dots = (plan_early, plan_late), (dots_early, dots_late)
    right = call(across_kernel, "frames_first", [*left], [(left_shape[0][::-1], jnp.bfloat16)] * 2, before=[sums])

    estimate = sums
    total = []
    step = 1
    for r in range(n_speech):
        if r < n_speech - 1:
            total = [
                call(
                    functools.partial(moments_kernel, r % half * rows, rows),
                    "moments",
                    [estimate, plans[r // half], dots[r // half], across_highs[r], across_lows[r], *total],
                    ((feats, 2 * frames), jnp.float32),
                    before=[sums],
                )
            ]
        if step < n_text:
            crossing = swap(sums, "text", step)
            sums = call(add_kernel, "hop", [sums, crossing], ((8, frames), jnp.float32), before=total)
            step *= 2
    while step < n_text:
        sums = sums + swap(sums, "text", step)
        step *= 2

    def text_part(r, name, before, pieces=1):
        late, first = divmod(r * rows, half * rows)
        return call(
            functools.partial(text_kernel, scale, first),
            name,
            [sums, plans[late], dots[late], *right],
            [((rows // pieces, feats), jnp.float32)] * pieces,
            before=before,
        )

    shape = ((n_text // 2, width, frames), jnp.float32)

    others = []
    for r in range(2, n_speech, 2):
        (term,) = text_part(r + 1, "text_far", [])
        (part,) = text_part(r, "text_far", [term])
        part = part + swap(term, "speech", 1)
        others.append(swap(part, "speech", r))
    near, far = call(
        functools.partial(finish_kernel, n_text, scale, (half - 1) * rows),
        "finish",
        [place, estimate, sums, *total, plans[1], dots[1], across_highs[-1], across_lows[-1]],
        [shape, shape],
        places=1,
        before=[term],
        scratch=[pltpu.VMEM((feats, frames), jnp.float32)],
    )
    crossed = [swap(piece, "speech", 1) for piece in text_part(1, "text_near", [part], 2)]
    near = call(
        pieces_kernel,
        "near",
        [near, swap(far, "text", 1)],
        [((width, frames), jnp.float32)] * (n_text // 2),
        before=crossed,
    )
    speech_terms = [near[0]] + [swap(near[k // 2], "text", k) for k in range(2, n_text, 2)]
    (own,) = text_part(0, "text_near", [part])
    text_grad = call(sum_kernel, "add", [own, *others, *crossed], ((rows, feats), jnp.float32))
    speech_block = call(add_kernel, "join", speech_terms, ((width, frames), jnp.float32), before=[own])
    return (speech_block.T, text_grad)


def pieces_kernel(left, right, *outs):
    for i, out in enumerate(outs):
        out[...] = left[i] + right[i]


def sum_kernel(*refs):
    *terms, out = refs
    rows = out.shape[0]
    total = terms[0][...]
    pieces = [term for term in terms if term.shape[0] < rows]
    for term in terms[1 : len(terms) - len(pieces)]:
        total = total + term[...]
    count = rows // len(pieces)
    for i, piece in enumerate(pieces):
        here = slice(i * count, (i + 1) * count)
        out[here, :] = total[here, :] + piece[...]


def solution(mesh):
    body = functools.partial(shards, mesh.shape["speech"], mesh.shape["text"])
    return jax.shard_map(
        body,
        mesh=mesh,
        in_specs=(P("speech", "text"), P(("text", "speech"), None), P("text"), P("speech", "text")),
        out_specs=(P("speech", "text"), P(("text", "speech"), None)),
        check_vma=False,
    )
```

profile of v0, /device:TPU:0, one launch (start us, length us, event | category | flops | bytes accessed | tf_op | source)
XLA Modules:
  0.0 92.6 jit_solution(3789323830911794763)
XLA Ops:
  0.6 0.5 collective-permute-start
  1.2 2.6 %collective-permute-start.8 = (f32[512,512]{1,0:T(8,128)}, f32[512,512]{1,0:T(8,128)}, u32[]{:S(2)}, u32[]{:S(2)}) collective-permute-start(f32[512,512]{1,0:T(8,128)} %refs_0_.1), channel_id=1, source_target_pairs={{0,16},{8,24},{16,0},{24,8},{1,17},{9,25},{17,1},{25,9},{2,18},{10... | collective-permute-start | bytes 3145736 | tf_op jit(solution)/shard_map/ppermute | solution.py:189
  3.8 1.0 %pad_maximum_fusion.refs_0_ = f32[128,512]{1,0:T(8,128)S(1)} fusion(f32[64,512]{1,0:T(8,128)} %bitcast.5, f32[64,512]{1,0:T(8,128)} %bitcast.6), kind=kLoop, calls=%fused_computation | loop fusion | flops 65536 | bytes 524288 | tf_op jit(solution)/shard_map/concatenate | solution.py:207
  4.7 0.0 collective-permute-done.refs_1_.refs_0_
  4.8 1.9 %collective-permute-start.2 = (f32[128,512]{1,0:T(8,128)S(1)}, f32[128,512]{1,0:T(8,128)S(1)}, u32[]{:S(2)}, u32[]{:S(2)}) collective-permute-start(f32[128,512]{1,0:T(8,128)S(1)} %copy.9.refs_2_), channel_id=1, source_target_pairs={{0,2},{1,3},{2,0},{3,1},{4,6},{5,7},{6,4},{7,5},{8,10},{9,11},{10,... | collective-permute-start | bytes 786440 | tf_op jit(solution)/shard_map/ppermute | solution.py:189
  6.7 2.6 %collective-permute-start.4 = (f32[128,512]{1,0:T(8,128)S(1)}, f32[128,512]{1,0:T(8,128)S(1)}, u32[]{:S(2)}, u32[]{:S(2)}) collective-permute-start(f32[128,512]{1,0:T(8,128)S(1)} %copy.9.refs_2_), channel_id=1, source_target_pairs={{0,4},{1,5},{2,6},{3,7},{4,0},{5,1},{6,2},{7,3},{8,12},{9,13},{10,... | collective-permute-start | bytes 786440 | tf_op jit(solution)/shard_map/ppermute | solution.py:189
  9.3 1.5 %collective-permute-start.1 = (f32[128,512]{1,0:T(8,128)S(1)}, f32[128,512]{1,0:T(8,128)S(1)}, u32[]{:S(2)}, u32[]{:S(2)}) collective-permute-start(f32[128,512]{1,0:T(8,128)S(1)} %copy.9.refs_2_), channel_id=1, source_target_pairs={{0,1},{1,0},{2,3},{3,2},{4,5},{5,4},{6,7},{7,6},{8,9},{9,8},{10,11... | collective-permute-start | bytes 786440 | tf_op jit(solution)/shard_map/ppermute | solution.py:189
  10.8 8.0 %collective-permute-done.2.refs_2_.refs_4_ = f32[128,512]{1,0:T(8,128)S(1)} collective-permute-done((f32[128,512]{1,0:T(8,128)S(1)}, f32[128,512]{1,0:T(8,128)S(1)}, u32[]{:S(2)}, u32[]{:S(2)}) %collective-permute-start.2) | collective-permute-done | bytes 262176 | tf_op jit(solution)/shard_map/ppermute | solution.py:189
  18.8 1.7 %collective-permute-start.3 = (f32[128,512]{1,0:T(8,128)S(1)}, f32[128,512]{1,0:T(8,128)S(1)}, u32[]{:S(2)}, u32[]{:S(2)}) collective-permute-start(f32[128,512]{1,0:T(8,128)S(1)} %collective-permute-done.2.refs_2_.refs_4_), channel_id=1, source_target_pairs={{0,1},{1,0},{2,3},{3,2},{4,5},{5,4},{6,7},{7,6},{8,9},{9,8},{10,11... | collective-permute-start | bytes 786440 | tf_op jit(solution)/shard_map/ppermute | solution.py:189
  20.5 0.9 collective-permute-done.4.refs_0_.refs_6_
  21.3 0.0 collective-permute-done.1.refs_1_.refs_3_
  21.3 0.5 collective-permute-start.6
  21.9 1.5 %collective-permute-start.5 = (f32[128,512]{1,0:T(8,128)S(1)}, f32[128,512]{1,0:T(8,128)S(1)}, u32[]{:S(2)}, u32[]{:S(2)}) collective-permute-start(f32[128,512]{1,0:T(8,128)S(1)} %collective-permute-done.4.refs_0_.refs_6_), channel_id=1, source_target_pairs={{0,1},{1,0},{2,3},{3,2},{4,5},{5,4},{6,7},{7,6},{8,9},{9,8},{10,11... | collective-permute-start | bytes 786440 | tf_op jit(solution)/shard_map/ppermute | solution.py:189
  23.4 4.7 %collective-permute-done.3.refs_1_.refs_5_ = f32[128,512]{1,0:T(8,128)S(1)} collective-permute-done((f32[128,512]{1,0:T(8,128)S(1)}, f32[128,512]{1,0:T(8,128)S(1)}, u32[]{:S(2)}, u32[]{:S(2)}) %collective-permute-start.3) | collective-permute-done | bytes 262176 | tf_op jit(solution)/shard_map/ppermute | solution.py:189
  28.0 0.0 collective-permute-done.6.refs_0_.refs_8_
  28.1 1.7 %collective-permute-start.7 = (f32[128,512]{1,0:T(8,128)S(1)}, f32[128,512]{1,0:T(8,128)S(1)}, u32[]{:S(2)}, u32[]{:S(2)}) collective-permute-start(f32[128,512]{1,0:T(8,128)S(1)} %copy.11), channel_id=1, source_target_pairs={{0,1},{1,0},{2,3},{3,2},{4,5},{5,4},{6,7},{7,6},{8,9},{9,8},{10,11... | collective-permute-start | bytes 786440 | tf_op jit(solution)/shard_map/ppermute | solution.py:189
  29.8 0.1 pad_add_fusion.refs_0_
  29.9 0.9 offsets.1.refs_1_
  30.7 0.0 copy-start
  30.8 1.2 %copy-done = f32[512,512]{1,0:T(8,128)S(1)} copy-done((f32[512,512]{1,0:T(8,128)S(1)}, f32[512,512]{1,0:T(8,128)}, u32[]{:S(2)}) %copy-start) | copy-done | bytes 1048600
  32.0 0.3 split.4
  32.3 0.0 collective-permute-done.8.refs_0_
  32.3 0.1 collective-permute-start.9
  32.4 0.3 split.5
  32.8 1.6 %split.6 = (bf16[512,512]{1,0:T(8,128)(2,1)S(1)}, bf16[512,512]{1,0:T(8,128)(2,1)S(1)}, bf16[512,512]{1,0:T(8,128)(2,1)S(1)}, bf16[512,512]{1,0:T(8,128)(2,1)S(1)}) custom-call(f32[512,512]{1,0:T(8,128)} %collective-permute-done.8.refs_0_), custom_call_target="tpu_custom_call" | custom-call | flops 500000000 | tf_op jit(solution)/shard_map/split/pallas_call | solution.py:53
  34.4 3.4 %collective-permute-done.7.refs_9_ = f32[128,512]{1,0:T(8,128)S(1)} collective-permute-done((f32[128,512]{1,0:T(8,128)S(1)}, f32[128,512]{1,0:T(8,128)S(1)}, u32[]{:S(2)}, u32[]{:S(2)}) %collective-permute-start.7) | collective-permute-done | bytes 262176 | tf_op jit(solution)/shard_map/ppermute | solution.py:189
  37.8 4.3 %plan_early.1 = (f32[1024,512]{1,0:T(8,128)S(1)}, f32[1024,512]{1,0:T(8,128)S(1)}, f32[8,512]{1,0:T(8,128)S(1)}, bf16[512,1024]{1,0:T(8,128)(2,1)S(1)}, bf16[512,1024]{1,0:T(8,128)(2,1)S(1)}) custom-call(s32[2]{0:T(128)S(1)} %pad_add_fusion.refs_0_, f32[2048,128]{1,0:T(8,128)S(1)} %offsets.1.refs_1_, f32[128,512]{1,0:T(8,128)S(1)} %copy.9.refs_2_, ...), custom_call_target="tpu_custom_call" | custom-call | flops 99999997952 | tf_op jit(solution)/shard_map/plan_early/pallas_call | solution.py:53
  42.1 0.0 collective-permute-done.9.refs_0_
  42.1 0.4 split.7
  42.5 4.0 %plan_late.1 = (f32[1024,512]{1,0:T(8,128)S(1)}, f32[1024,512]{1,0:T(8,128)S(1)}, f32[8,512]{1,0:T(8,128)S(1)}) custom-call(s32[2]{0:T(128)S(1)} %pad_add_fusion.refs_0_, f32[2048,128]{1,0:T(8,128)S(1)} %offsets.1.refs_1_, f32[8,512]{1,0:T(8,128)S(1)} %get-tuple-element.40.refs_2_, bf16[512,1024]{1,0:T(8,128)(2,1)S(1)} %get-tuple-element.41.refs_3_.refs_0_, ...), custom_call_target="tpu_custom_call" | custom-call | flops 3000000000 | tf_op jit(solution)/shard_map/plan_late/pallas_call | solution.py:53
  46.5 1.6 %collective-permute-start.10 = (f32[8,512]{1,0:T(8,128)S(1)}, f32[8,512]{1,0:T(8,128)S(1)}, u32[]{:S(2)}, u32[]{:S(2)}) collective-permute-start(f32[8,512]{1,0:T(8,128)S(1)} %get-tuple-element.47.refs_0_.refs_5_.refs_2_.refs_1_), channel_id=1, source_target_pairs={{0,1},{1,0},{2,3},{3,2},{4,5},{5,4},{6,7},{7,6},{8,9},{9,8},{10,11... | collective-permute-start | bytes 49160 | tf_op jit(solution)/shard_map/ppermute | solution.py:189
  48.1 1.9 %moments.3.refs_2_.refs_5_ = f32[512,1024]{1,0:T(8,128)S(1)} custom-call(f32[8,512]{1,0:T(8,128)S(1)} %get-tuple-element.47.refs_0_.refs_5_.refs_2_.refs_1_, f32[1024,512]{1,0:T(8,128)S(1)} %get-tuple-element.48.refs_1_, f32[1024,512]{1,0:T(8,128)S(1)} %get-tuple-element.49.refs_2_, bf16[512,512]{1,0:T(8,128)(2,1)S(1)} %get-tuple-element.50.refs_3_, ...), custom_call_target="tpu_custom_call" | custom-call | flops 3000000000 | tf_op jit(solution)/shard_map/moments/pallas_call | solution.py:53
  50.0 0.6 frames_first.1
  50.6 0.1 collective-permute-start.11
  50.7 1.9 %moments.4.refs_2_.refs_5_ = f32[512,1024]{1,0:T(8,128)S(1)} custom-call(f32[8,512]{1,0:T(8,128)S(1)} %get-tuple-element.47.refs_0_.refs_5_.refs_2_.refs_1_, f32[1024,512]{1,0:T(8,128)S(1)} %get-tuple-element.48.refs_1_, f32[1024,512]{1,0:T(8,128)S(1)} %get-tuple-element.49.refs_2_, bf16[512,512]{1,0:T(8,128)(2,1)S(1)} %get-tuple-element.52.refs_3_, ...), custom_call_target="tpu_custom_call" | custom-call | flops 3000000000 | tf_op jit(solution)/shard_map/moments/pallas_call | solution.py:53
  52.6 1.8 %collective-permute-done.11.refs_1_ = f32[8,512]{1,0:T(8,128)S(1)} collective-permute-done((f32[8,512]{1,0:T(8,128)S(1)}, f32[8,512]{1,0:T(8,128)S(1)}, u32[]{:S(2)}, u32[]{:S(2)}) %collective-permute-start.11) | collective-permute-done | bytes 16416 | tf_op jit(solution)/shard_map/ppermute | solution.py:189
  54.4 1.3 %collective-permute-start.12 = (f32[8,512]{1,0:T(8,128)S(1)}, f32[8,512]{1,0:T(8,128)S(1)}, u32[]{:S(2)}, u32[]{:S(2)}) collective-permute-start(f32[8,512]{1,0:T(8,128)S(1)} %hop.4.refs_6_.refs_0_), channel_id=1, source_target_pairs={{0,4},{1,5},{2,6},{3,7},{4,0},{5,1},{6,2},{7,3},{8,12},{9,13},{10,... | collective-permute-start | bytes 49160 | tf_op jit(solution)/shard_map/ppermute | solution.py:189
  55.7 2.1 %moments.5.refs_2_.refs_3_ = f32[512,1024]{1,0:T(8,128)S(1)} custom-call(f32[8,512]{1,0:T(8,128)S(1)} %get-tuple-element.47.refs_0_.refs_5_.refs_2_.refs_1_, f32[1024,512]{1,0:T(8,128)S(1)} %get-tuple-element.54.refs_1_.refs_4_, f32[1024,512]{1,0:T(8,128)S(1)} %get-tuple-element.55.refs_2_.refs_5_, bf16[512,512]{1,0:T(8,128)(2,1)S(1)} %get-tuple-element.56.refs_3_, ...), custom_call_target="tpu_custom_call" | custom-call | flops 3000000000 | tf_op jit(solution)/shard_map/moments/pallas_call | solution.py:53
  57.8 1.3 %collective-permute-done.12.refs_1_ = f32[8,512]{1,0:T(8,128)S(1)} collective-permute-done((f32[8,512]{1,0:T(8,128)S(1)}, f32[8,512]{1,0:T(8,128)S(1)}, u32[]{:S(2)}, u32[]{:S(2)}) %collective-permute-start.12) | collective-permute-done | bytes 16416 | tf_op jit(solution)/shard_map/ppermute | solution.py:189
  59.1 1.9 %text_far.2.refs_8_.refs_5_ = f32[512,512]{1,0:T(8,128)S(1)} custom-call(f32[8,512]{1,0:T(8,128)S(1)} %hop.5.refs_0_.refs_2_, f32[1024,512]{1,0:T(8,128)S(1)} %get-tuple-element.54.refs_1_.refs_4_, f32[1024,512]{1,0:T(8,128)S(1)} %get-tuple-element.55.refs_2_.refs_5_, bf16[1024,512]{1,0:T(8,128)(2,1)S(1)} %get-tuple-element.60.refs_3_, ...), custom_call_target="tpu_custom_call" | custom-call | flops 3000000000 | tf_op jit(solution)/shard_map/text_far/pallas_call | solution.py:53
  60.9 0.1 collective-permute-start.14
  61.0 1.8 %finish.1 = (f32[4,64,512]{2,1,0:T(8,128)S(1)}, f32[4,64,512]{2,1,0:T(8,128)S(1)}) custom-call(s32[2]{0:T(128)S(1)} %pad_add_fusion.refs_0_, f32[8,512]{1,0:T(8,128)S(1)} %get-tuple-element.47.refs_0_.refs_5_.refs_2_.refs_1_, f32[8,512]{1,0:T(8,128)S(1)} %hop.5.refs_0_.refs_2_, f32[512,1024]{1,0:T(8,128)S(1)} %moments.5.refs_2_.refs_3_, ...), custom_call_target="tpu_custom_call" | custom-call | flops 1000000000 | tf_op jit(solution)/shard_map/finish/pallas_call | solution.py:53
  62.8 1.2 %collective-permute-start.13 = (f32[4,64,512]{2,1,0:T(8,128)S(1)}, f32[4,64,512]{2,1,0:T(8,128)S(1)}, u32[]{:S(2)}, u32[]{:S(2)}) collective-permute-start(f32[4,64,512]{2,1,0:T(8,128)S(1)} %get-tuple-element.63), channel_id=1, source_target_pairs={{0,1},{1,0},{2,3},{3,2},{4,5},{5,4},{6,7},{7,6},{8,9},{9,8},{10,11... | collective-permute-start | bytes 1572872 | tf_op jit(solution)/shard_map/ppermute | solution.py:189
  64.1 1.9 %text_far.3 = f32[512,512]{1,0:T(8,128)S(1)} custom-call(f32[8,512]{1,0:T(8,128)S(1)} %hop.5.refs_0_.refs_2_, f32[1024,512]{1,0:T(8,128)S(1)} %get-tuple-element.54.refs_1_.refs_4_, f32[1024,512]{1,0:T(8,128)S(1)} %get-tuple-element.55.refs_2_.refs_5_, bf16[1024,512]{1,0:T(8,128)(2,1)S(1)} %get-tuple-element.60.refs_3_, ...), custom_call_target="tpu_custom_call" | custom-call | flops 3000000000 | tf_op jit(solution)/shard_map/text_far/pallas_call | solution.py:53
  65.9 0.0 collective-permute-done.14
  65.9 0.2 add.4.refs_5_
  66.1 1.6 %collective-permute-start.20 = (f32[512,512]{1,0:T(8,128)S(1)}, f32[512,512]{1,0:T(8,128)S(1)}, u32[]{:S(2)}, u32[]{:S(2)}) collective-permute-start(f32[512,512]{1,0:T(8,128)S(1)} %add.4.refs_5_), channel_id=1, source_target_pairs={{0,16},{8,24},{16,0},{24,8},{1,17},{9,25},{17,1},{25,9},{2,18},{10... | collective-permute-start | bytes 3145736 | tf_op jit(solution)/shard_map/ppermute | solution.py:189
  67.7 1.9 %text_near.2 = (f32[256,512]{1,0:T(8,128)S(1)}, f32[256,512]{1,0:T(8,128)S(1)}) custom-call(f32[8,512]{1,0:T(8,128)S(1)} %hop.5.refs_0_.refs_2_, f32[1024,512]{1,0:T(8,128)S(1)} %get-tuple-element.48.refs_1_, f32[1024,512]{1,0:T(8,128)S(1)} %get-tuple-element.49.refs_2_, bf16[1024,512]{1,0:T(8,128)(2,1)S(1)} %get-tuple-element.60.refs_3_, ...), custom_call_target="tpu_custom_call" | custom-call | flops 3000000000 | tf_op jit(solution)/shard_map/text_near/pallas_call | solution.py:53
  69.6 0.1 collective-permute-start.15
  69.7 0.5 collective-permute-start.16
  70.2 7.0 %collective-permute-done.13.refs_1_ = f32[4,64,512]{2,1,0:T(8,128)S(1)} collective-permute-done((f32[4,64,512]{2,1,0:T(8,128)S(1)}, f32[4,64,512]{2,1,0:T(8,128)S(1)}, u32[]{:S(2)}, u32[]{:S(2)}) %collective-permute-start.13) | collective-permute-done | bytes 524320 | tf_op jit(solution)/shard_map/ppermute | solution.py:189
  77.2 0.0 collective-permute-done.15.refs_2_
  77.2 0.0 collective-permute-done.16.refs_3_
  77.2 0.1 near.1
  77.3 0.6 collective-permute-start.17
  77.9 2.5 %collective-permute-start.18 = (f32[64,512]{1,0:T(8,128)S(1)}, f32[64,512]{1,0:T(8,128)S(1)}, u32[]{:S(2)}, u32[]{:S(2)}) collective-permute-start(f32[64,512]{1,0:T(8,128)S(1)} %get-tuple-element.68), channel_id=1, source_target_pairs={{0,4},{1,5},{2,6},{3,7},{4,0},{5,1},{6,2},{7,3},{8,12},{9,13},{10,... | collective-permute-start | bytes 393224 | tf_op jit(solution)/shard_map/ppermute | solution.py:189
  80.4 1.3 %collective-permute-start.19 = (f32[64,512]{1,0:T(8,128)S(1)}, f32[64,512]{1,0:T(8,128)S(1)}, u32[]{:S(2)}, u32[]{:S(2)}) collective-permute-start(f32[64,512]{1,0:T(8,128)S(1)} %get-tuple-element.69), channel_id=1, source_target_pairs={{0,6},{1,7},{2,4},{3,5},{4,2},{5,3},{6,0},{7,1},{8,14},{9,15},{10,... | collective-permute-start | bytes 393224 | tf_op jit(solution)/shard_map/ppermute | solution.py:189
  81.7 1.9 %text_near.3.refs_4_.refs_0_ = f32[512,512]{1,0:T(8,128)S(1)} custom-call(f32[8,512]{1,0:T(8,128)S(1)} %hop.5.refs_0_.refs_2_, f32[1024,512]{1,0:T(8,128)S(1)} %get-tuple-element.48.refs_1_, f32[1024,512]{1,0:T(8,128)S(1)} %get-tuple-element.49.refs_2_, bf16[1024,512]{1,0:T(8,128)(2,1)S(1)} %get-tuple-element.60.refs_3_, ...), custom_call_target="tpu_custom_call" | custom-call | flops 3000000000 | tf_op jit(solution)/shard_map/text_near/pallas_call | solution.py:53
  83.6 0.7 collective-permute-done.17.refs_1_
  84.3 6.3 %collective-permute-done.18.refs_2_ = f32[64,512]{1,0:T(8,128)S(1)} collective-permute-done((f32[64,512]{1,0:T(8,128)S(1)}, f32[64,512]{1,0:T(8,128)S(1)}, u32[]{:S(2)}, u32[]{:S(2)}) %collective-permute-start.18) | collective-permute-done | bytes 131104 | tf_op jit(solution)/shard_map/ppermute | solution.py:189
  90.6 0.0 collective-permute-done.19.refs_3_
  90.6 0.7 join.1
  91.3 0.2 collective-permute-done.20.refs_1_
  91.5 1.1 %add.7 = f32[512,512]{1,0:T(8,128)} custom-call(f32[512,512]{1,0:T(8,128)S(1)} %text_near.3.refs_4_.refs_0_, f32[512,512]{1,0:T(8,128)S(1)} %collective-permute-done.20.refs_1_, f32[256,512]{1,0:T(8,128)S(1)} %collective-permute-done.15.refs_2_, f32[256,512]{1,0:T(8,128)S(1)} %collective-permute-done.16.refs_3_), custom_call_target="tpu_custom_call" | custom-call | flops 99999997952 | tf_op jit(solution)/shard_map/add/pallas_call | solution.py:53
  (11 shorter events, 0.1 us)
Async XLA Ops:
  0.6 21.2 %copy-start.1 = (f32[2048]{0:T(1024)S(1)}, f32[2048]{0:T(1024)}, u32[]{:S(2)}) copy-start(f32[2048]{0:T(1024)} %param.6) | copy-start | bytes 24580
  0.6 4.1 %collective-permute-start = (f32[512,512]{1,0:T(8,128)}, f32[512,512]{1,0:T(8,128)S(1)}, u32[]{:S(2)}, u32[]{:S(2)}) collective-permute-start(f32[512,512]{1,0:T(8,128)} %refs_0_.1), channel_id=1, source_target_pairs={{0,8},{8,0},{16,24},{24,16},{1,9},{9,1},{17,25},{25,17},{2,10},{10... | collective-permute-start | bytes 3145736 | tf_op jit(solution)/shard_map/ppermute | solution.py:189
  1.2 31.2 %collective-permute-start.8 = (f32[512,512]{1,0:T(8,128)}, f32[512,512]{1,0:T(8,128)}, u32[]{:S(2)}, u32[]{:S(2)}) collective-permute-start(f32[512,512]{1,0:T(8,128)} %refs_0_.1), channel_id=1, source_target_pairs={{0,16},{8,24},{16,0},{24,8},{1,17},{9,25},{17,1},{25,9},{2,18},{10... | collective-permute-start | bytes 3145736 | tf_op jit(solution)/shard_map/ppermute | solution.py:189
  4.8 14.0 %collective-permute-start.2 = (f32[128,512]{1,0:T(8,128)S(1)}, f32[128,512]{1,0:T(8,128)S(1)}, u32[]{:S(2)}, u32[]{:S(2)}) collective-permute-start(f32[128,512]{1,0:T(8,128)S(1)} %copy.9.refs_2_), channel_id=1, source_target_pairs={{0,2},{1,3},{2,0},{3,1},{4,6},{5,7},{6,4},{7,5},{8,10},{9,11},{10,... | collective-permute-start | bytes 786440 | tf_op jit(solution)/shard_map/ppermute | solution.py:189
  6.7 14.6 %collective-permute-start.4 = (f32[128,512]{1,0:T(8,128)S(1)}, f32[128,512]{1,0:T(8,128)S(1)}, u32[]{:S(2)}, u32[]{:S(2)}) collective-permute-start(f32[128,512]{1,0:T(8,128)S(1)} %copy.9.refs_2_), channel_id=1, source_target_pairs={{0,4},{1,5},{2,6},{3,7},{4,0},{5,1},{6,2},{7,3},{8,12},{9,13},{10,... | collective-permute-start | bytes 786440 | tf_op jit(solution)/shard_map/ppermute | solution.py:189
  9.3 12.0 %collective-permute-start.1 = (f32[128,512]{1,0:T(8,128)S(1)}, f32[128,512]{1,0:T(8,128)S(1)}, u32[]{:S(2)}, u32[]{:S(2)}) collective-permute-start(f32[128,512]{1,0:T(8,128)S(1)} %copy.9.refs_2_), channel_id=1, source_target_pairs={{0,1},{1,0},{2,3},{3,2},{4,5},{5,4},{6,7},{7,6},{8,9},{9,8},{10,11... | collective-permute-start | bytes 786440 | tf_op jit(solution)/shard_map/ppermute | solution.py:189
  18.8 9.2 %collective-permute-start.3 = (f32[128,512]{1,0:T(8,128)S(1)}, f32[128,512]{1,0:T(8,128)S(1)}, u32[]{:S(2)}, u32[]{:S(2)}) collective-permute-start(f32[128,512]{1,0:T(8,128)S(1)} %collective-permute-done.2.refs_2_.refs_4_), channel_id=1, source_target_pairs={{0,1},{1,0},{2,3},{3,2},{4,5},{5,4},{6,7},{7,6},{8,9},{9,8},{10,11... | collective-permute-start | bytes 786440 | tf_op jit(solution)/shard_map/ppermute | solution.py:189
  21.3 6.7 %collective-permute-start.6 = (f32[128,512]{1,0:T(8,128)S(1)}, f32[128,512]{1,0:T(8,128)S(1)}, u32[]{:S(2)}, u32[]{:S(2)}) collective-permute-start(f32[128,512]{1,0:T(8,128)S(1)} %copy.10), channel_id=1, source_target_pairs={{0,2},{1,3},{2,0},{3,1},{4,6},{5,7},{6,4},{7,5},{8,10},{9,11},{10,... | collective-permute-start | bytes 786440 | tf_op jit(solution)/shard_map/ppermute | solution.py:189
  21.9 12.5 %collective-permute-start.5 = (f32[128,512]{1,0:T(8,128)S(1)}, f32[128,512]{1,0:T(8,128)S(1)}, u32[]{:S(2)}, u32[]{:S(2)}) collective-permute-start(f32[128,512]{1,0:T(8,128)S(1)} %collective-permute-done.4.refs_0_.refs_6_), channel_id=1, source_target_pairs={{0,1},{1,0},{2,3},{3,2},{4,5},{5,4},{6,7},{7,6},{8,9},{9,8},{10,11... | collective-permute-start | bytes 786440 | tf_op jit(solution)/shard_map/ppermute | solution.py:189
  28.1 9.7 %collective-permute-start.7 = (f32[128,512]{1,0:T(8,128)S(1)}, f32[128,512]{1,0:T(8,128)S(1)}, u32[]{:S(2)}, u32[]{:S(2)}) collective-permute-start(f32[128,512]{1,0:T(8,128)S(1)} %copy.11), channel_id=1, source_target_pairs={{0,1},{1,0},{2,3},{3,2},{4,5},{5,4},{6,7},{7,6},{8,9},{9,8},{10,11... | collective-permute-start | bytes 786440 | tf_op jit(solution)/shard_map/ppermute | solution.py:189
  30.7 1.2 %copy-start = (f32[512,512]{1,0:T(8,128)S(1)}, f32[512,512]{1,0:T(8,128)}, u32[]{:S(2)}) copy-start(f32[512,512]{1,0:T(8,128)} %refs_0_.1) | copy-start | bytes 3145732
  32.3 9.8 %collective-permute-start.9 = (f32[512,512]{1,0:T(8,128)}, f32[512,512]{1,0:T(8,128)S(1)}, u32[]{:S(2)}, u32[]{:S(2)}) collective-permute-start(f32[512,512]{1,0:T(8,128)} %collective-permute-done.8.refs_0_), channel_id=1, source_target_pairs={{0,8},{8,0},{16,24},{24,16},{1,9},{9,1},{17,25},{25,17},{2,10},{10... | collective-permute-start | bytes 3145736 | tf_op jit(solution)/shard_map/ppermute | solution.py:189
  46.5 4.1 %collective-permute-start.10 = (f32[8,512]{1,0:T(8,128)S(1)}, f32[8,512]{1,0:T(8,128)S(1)}, u32[]{:S(2)}, u32[]{:S(2)}) collective-permute-start(f32[8,512]{1,0:T(8,128)S(1)} %get-tuple-element.47.refs_0_.refs_5_.refs_2_.refs_1_), channel_id=1, source_target_pairs={{0,1},{1,0},{2,3},{3,2},{4,5},{5,4},{6,7},{7,6},{8,9},{9,8},{10,11... | collective-permute-start | bytes 49160 | tf_op jit(solution)/shard_map/ppermute | solution.py:189
  50.6 3.8 %collective-permute-start.11 = (f32[8,512]{1,0:T(8,128)S(1)}, f32[8,512]{1,0:T(8,128)S(1)}, u32[]{:S(2)}, u32[]{:S(2)}) collective-permute-start(f32[8,512]{1,0:T(8,128)S(1)} %hop.3.refs_6_.refs_0_), channel_id=1, source_target_pairs={{0,2},{1,3},{2,0},{3,1},{4,6},{5,7},{6,4},{7,5},{8,10},{9,11},{10,... | collective-permute-start | bytes 49160 | tf_op jit(solution)/shard_map/ppermute | solution.py:189
  54.4 4.6 %collective-permute-start.12 = (f32[8,512]{1,0:T(8,128)S(1)}, f32[8,512]{1,0:T(8,128)S(1)}, u32[]{:S(2)}, u32[]{:S(2)}) collective-permute-start(f32[8,512]{1,0:T(8,128)S(1)} %hop.4.refs_6_.refs_0_), channel_id=1, source_target_pairs={{0,4},{1,5},{2,6},{3,7},{4,0},{5,1},{6,2},{7,3},{8,12},{9,13},{10,... | collective-permute-start | bytes 49160 | tf_op jit(solution)/shard_map/ppermute | solution.py:189
  60.9 5.0 %collective-permute-start.14 = (f32[512,512]{1,0:T(8,128)S(1)}, f32[512,512]{1,0:T(8,128)S(1)}, u32[]{:S(2)}, u32[]{:S(2)}) collective-permute-start(f32[512,512]{1,0:T(8,128)S(1)} %text_far.2.refs_8_.refs_5_), channel_id=1, source_target_pairs={{0,8},{8,0},{16,24},{24,16},{1,9},{9,1},{17,25},{25,17},{2,10},{10... | collective-permute-start | bytes 3145736 | tf_op jit(solution)/shard_map/ppermute | solution.py:189
  62.8 14.4 %collective-permute-start.13 = (f32[4,64,512]{2,1,0:T(8,128)S(1)}, f32[4,64,512]{2,1,0:T(8,128)S(1)}, u32[]{:S(2)}, u32[]{:S(2)}) collective-permute-start(f32[4,64,512]{2,1,0:T(8,128)S(1)} %get-tuple-element.63), channel_id=1, source_target_pairs={{0,1},{1,0},{2,3},{3,2},{4,5},{5,4},{6,7},{7,6},{8,9},{9,8},{10,11... | collective-permute-start | bytes 1572872 | tf_op jit(solution)/shard_map/ppermute | solution.py:189
  66.1 25.3 %collective-permute-start.20 = (f32[512,512]{1,0:T(8,128)S(1)}, f32[512,512]{1,0:T(8,128)S(1)}, u32[]{:S(2)}, u32[]{:S(2)}) collective-permute-start(f32[512,512]{1,0:T(8,128)S(1)} %add.4.refs_5_), channel_id=1, source_target_pairs={{0,16},{8,24},{16,0},{24,8},{1,17},{9,25},{17,1},{25,9},{2,18},{10... | collective-permute-start | bytes 3145736 | tf_op jit(solution)/shard_map/ppermute | solution.py:189
  69.6 7.6 %collective-permute-start.15 = (f32[256,512]{1,0:T(8,128)S(1)}, f32[256,512]{1,0:T(8,128)S(1)}, u32[]{:S(2)}, u32[]{:S(2)}) collective-permute-start(f32[256,512]{1,0:T(8,128)S(1)} %get-tuple-element.64), channel_id=1, source_target_pairs={{0,8},{8,0},{16,24},{24,16},{1,9},{9,1},{17,25},{25,17},{2,10},{10... | collective-permute-start | bytes 1572872 | tf_op jit(solution)/shard_map/ppermute | solution.py:189
  69.7 7.5 %collective-permute-start.16 = (f32[256,512]{1,0:T(8,128)S(1)}, f32[256,512]{1,0:T(8,128)S(1)}, u32[]{:S(2)}, u32[]{:S(2)}) collective-permute-start(f32[256,512]{1,0:T(8,128)S(1)} %get-tuple-element.65), channel_id=1, source_target_pairs={{0,8},{8,0},{16,24},{24,16},{1,9},{9,1},{17,25},{25,17},{2,10},{10... | collective-permute-start | bytes 1572872 | tf_op jit(solution)/shard_map/ppermute | solution.py:189
  77.3 7.1 %collective-permute-start.17 = (f32[64,512]{1,0:T(8,128)S(1)}, f32[64,512]{1,0:T(8,128)S(1)}, u32[]{:S(2)}, u32[]{:S(2)}) collective-permute-start(f32[64,512]{1,0:T(8,128)S(1)} %get-tuple-element.67), channel_id=1, source_target_pairs={{0,2},{1,3},{2,0},{3,1},{4,6},{5,7},{6,4},{7,5},{8,10},{9,11},{10,... | collective-permute-start | bytes 393224 | tf_op jit(solution)/shard_map/ppermute | solution.py:189
  77.9 12.7 %collective-permute-start.18 = (f32[64,512]{1,0:T(8,128)S(1)}, f32[64,512]{1,0:T(8,128)S(1)}, u32[]{:S(2)}, u32[]{:S(2)}) collective-permute-start(f32[64,512]{1,0:T(8,128)S(1)} %get-tuple-element.68), channel_id=1, source_target_pairs={{0,4},{1,5},{2,6},{3,7},{4,0},{5,1},{6,2},{7,3},{8,12},{9,13},{10,... | collective-permute-start | bytes 393224 | tf_op jit(solution)/shard_map/ppermute | solution.py:189
  80.4 10.2 %collective-permute-start.19 = (f32[64,512]{1,0:T(8,128)S(1)}, f32[64,512]{1,0:T(8,128)S(1)}, u32[]{:S(2)}, u32[]{:S(2)}) collective-permute-start(f32[64,512]{1,0:T(8,128)S(1)} %get-tuple-element.69), channel_id=1, source_target_pairs={{0,6},{1,7},{2,4},{3,5},{4,2},{5,3},{6,0},{7,1},{8,14},{9,15},{10,... | collective-permute-start | bytes 393224 | tf_op jit(solution)/shard_map/ppermute | solution.py:189
where the time goes:
time: 92.8 us; the launch traced here: 92.6 us
  waiting for transfers between devices  34.3 us (37%)
  Pallas kernels  29.4 us (32%)
  starting transfers between devices  25.4 us (27%)
  other arithmetic  1.27 us (1%)
  local copies, waits for them, and re-layouts  1.24 us (1%)
    ppermute x21, waiting for transfers between devices, swap(): return lax.ppermute(value, axis, [(i, i ^ k) for i in range(count)])  34.3 us
    pallas_call x25, Pallas kernels, call(): pl.pallas_call(body, in_specs=[IN_SMEM] * places + [IN_VMEM] * (count - p...  29.4 us
    ppermute x21, starting transfers between devices, swap(): return lax.ppermute(value, axis, [(i, i ^ k) for i in range(count)])  25.4 us
  transfers between devices with their start and end apart: 21, of which 10 were waited for; matrix products, arithmetic and copies ran while one was open for 1% of the time, Pallas kernels for 24%

commit v1 on v0

--- a/solution.py
+++ b/solution.py
@@ -12,12 +12,14 @@
 WORK = {
     "plan_early": LONG,
     "plan_late": 3 * SHORT,
+    "plan_part": SHORT,
+    "plan_more": SHORT,
     "moments": 3 * SHORT,
     "text_far": 3 * SHORT,
     "text_near": 3 * SHORT,
     "finish": SHORT,
     "frames_first": SHORT,
-    "split": SHORT // 2,
+    "split": SHORT,
     "offsets": SHORT // 10,
     "add": LONG,
 }
@@ -73,26 +75,40 @@
     out[...] = total
 
 
-def split_kernel(block, high_out, low_out, across_high, across_low):
+def group_of(n_text, width):
+    return min(n_text, max(2, LANES // width))
+
+
+def group_starts(place, group, width, n_text):
+    mine = place[0] - place[0] % group
+    return [pl.multiple_of((mine ^ first) * width, group * width) for first in range(0, n_text, group)]
+
+
+def split_kernel(n_text, group, place, block, high_out, low_out, across_high, across_low):
     value = block[...]
-    high_out[...], low_out[...] = halves(value)
     across_high[...], across_low[...] = halves(value.T)
-
-
-def split_block(block):
+    lanes = block.shape[1] // n_text * group
+    for i, start in enumerate(group_starts(place, group, lanes // group, n_text)):
+        columns = slice(i * lanes, (i + 1) * lanes)
+        high_out[:, columns], low_out[:, columns] = halves(block[:, pl.ds(start, lanes)])
+
+
+def split_block(place, block, n_text):
     rows, feats = block.shape
+    group = group_of(n_text, feats // n_text)
     plain, across = ((rows, feats), jnp.bfloat16), ((feats, rows), jnp.bfloat16)
-    return call(split_kernel, "split", [block], [plain, plain, across, across])
-
-
-def assemble(place, speech_chunks, grad_chunks, left):
-    frames = speech_chunks[0].shape[1]
-    for part, chunks in enumerate((speech_chunks, grad_chunks)):
-        columns = slice(part * frames, (part + 1) * frames)
-        for k, chunk in enumerate(chunks):
-            width = chunk.shape[0]
-            start = pl.multiple_of((place[0] ^ k) * width, width)
-            left[0][pl.ds(start, width), columns], left[1][pl.ds(start, width), columns] = halves(chunk[...])
+    body = functools.partial(split_kernel, n_text, group)
+    return call(body, "split", [place, block], [plain, plain, across, across], places=1)
+
+
+def assemble(place, group, first, chunks, left):
+    width, frames = chunks[0].shape[0] // 2, chunks[0].shape[1]
+    for k, chunk in enumerate(chunks, first):
+        row = (k - k % group) * width + (place[0] ^ k) % group * width
+        here = pl.ds(pl.multiple_of(row, width), width)
+        for part in range(2):
+            columns = slice(part * frames, (part + 1) * frames)
+            left[0][here, columns], left[1][here, columns] = halves(chunk[part * width : (part + 1) * width, :])
 
 
 def offsets_kernel(place, pot, out):
@@ -102,13 +118,17 @@
         out[r * rows : (r + 1) * rows, :] = jnp.broadcast_to(row, (out.shape[1], rows)).T
 
 
-def plan_rows(scale, place, first, pot, blocks, left, plan_out, dots_out, sums_out):
+def plan_rows(scale, first, pot, blocks, left, partials, plan_out, dots_out, sums_out):
     count = len(blocks) // 2
     frames = plan_out.shape[1]
     rows = blocks[0].shape[0]
     for r in range(count):
         here = slice(r * rows, (r + 1) * rows)
-        product = dot3((blocks[r][...], blocks[count + r][...]), (left[0][...], left[1][...]))
+        known = left[0].shape[0] // 2 if r < len(partials) else 0
+        text = (blocks[r][:, known:], blocks[count + r][:, known:])
+        product = dot3(text, (left[0][known:, :], left[1][known:, :]))
+        if known:
+            product = product + partials[r][...]
         offsets = pot[(first + r) * rows : (first + r + 1) * rows, :]
         lanes = offsets.shape[1]
         plan = jnp.concatenate(
@@ -121,25 +141,47 @@
         sums_out[1:2, :] += jnp.sum(plan * grad_dots, axis=0, keepdims=True)
 
 
-def early_kernel(n_text, scale, place, pot, *refs):
-    chunks, blocks = refs[:n_text], refs[n_text:-5]
+def part_kernel(n_chunks, group, place, *refs):
+    chunks, refs = refs[:n_chunks], refs[n_chunks:]
+    count = (len(refs) - 2) // 3
+    blocks, outs, left = refs[: 2 * count], refs[2 * count : -2], refs[-2:]
+    assemble(place, group, 0, chunks, left)
+    known = left[0].shape[0]
+    for r in range(count):
+        text = (blocks[r][:, :known], blocks[count + r][:, :known])
+        outs[r][...] = dot3(text, (left[0][...], left[1][...]))
+
+
+def more_kernel(left_high, left_low, high, low, out):
+    known = left_high.shape[0]
+    out[...] = dot3((high[:, :known], low[:, :known]), (left_high[...], left_low[...]))
+
+
+def early_kernel(n_chunks, n_partials, group, scale, place, pot, *refs):
+    known, refs = refs[:2], refs[2:]
+    chunks, refs = refs[:n_chunks], refs[n_chunks:]
+    partials, blocks = refs[:n_partials], refs[n_partials:-5]
     plan_out, dots_out, sums_out, *left = refs[-5:]
-    width = chunks[0].shape[0] // 2
-    assemble(place, [chunk.at[:width] for chunk in chunks], [chunk.at[width:] for chunk in chunks], left)
+    for old, new in zip(known, left):
+        new[: old.shape[0], :] = old[...]
+    assemble(place, group, n_chunks, chunks, left)
     sums_out[...] = jnp.zeros_like(sums_out)
-    plan_rows(scale, place, 0, pot, blocks, left, plan_out, dots_out, sums_out)
-
-
-def late_kernel(scale, first, place, pot, sums, left_high, left_low, *refs):
-    blocks = refs[:-3]
+    plan_rows(scale, 0, pot, blocks, left, partials, plan_out, dots_out, sums_out)
+
+
+def late_kernel(n_partials, scale, first, pot, sums, left_high, left_low, *refs):
+    partials, blocks = refs[:n_partials], refs[n_partials:-3]
     plan_out, dots_out, sums_out = refs[-3:]
     sums_out[...] = sums[...]
-    plan_rows(scale, place, first, pot, blocks, (left_high, left_low), plan_out, dots_out, sums_out)
-
-
-def across_kernel(high, low, high_out, low_out):
+    plan_rows(scale, first, pot, blocks, (left_high, left_low), partials, plan_out, dots_out, sums_out)
+
+
+def across_kernel(n_text, group, place, high, low, high_out, low_out):
+    lanes = high.shape[0] // n_text * group
+    starts = group_starts(place, group, lanes // group, n_text)
     for value, out in ((high, high_out), (low, low_out)):
-        out[...] = value[...].astype(jnp.float32).T.astype(jnp.bfloat16)
+        ordered = jnp.concatenate([value[pl.ds(start, lanes), :] for start in starts], axis=0)
+        out[...] = ordered.astype(jnp.float32).T.astype(jnp.bfloat16)
 
 
 def weights(sums, plan, grad_dots, scale):
@@ -207,6 +249,10 @@
     packed = jnp.concatenate([speech_feat.T, map_grad.T], axis=0)
     packed = call(copy_kernel, "copy", [packed], (packed.shape, packed.dtype), before=[blocks[1]])
     chunks = [packed] + [None] * (n_text - 1)
+    split = [split_block(place, blocks[0], n_text), split_block(place, blocks[1], n_text)]
+    known, group = n_text // 2, group_of(n_text, width)
+    part_tile = ((rows, 2 * frames), jnp.float32)
+    part_shape = ((feats // 2, 2 * frames), jnp.bfloat16)
     for k in range(1, n_text):
         if k & (k - 1) == 0:
             chunks[k] = swap(packed, "text", k)
@@ -214,34 +260,52 @@
         if k & (k - 1):
             step = k & -k
             source = chunks[k ^ step]
-            wanted = [chunks[1], chunks[2]] if step > 1 else [chunks[3]] if 3 < k == n_text - 1 else []
+            wanted = [chunks[1], chunks[2], pot, *(block[0] for block in split)] if step > 1 else []
+            if k == n_text - 1:
+                *partials, part_high, part_low = call(
+                    functools.partial(part_kernel, known, group),
+                    "plan_part",
+                    [place, *chunks[:known], *(block[0] for block in split), *(block[1] for block in split)],
+                    [part_tile] * len(split) + [part_shape, part_shape],
+                    places=1,
+                )
+                wanted = [*wanted, part_high]
             if wanted:
                 source = call(copy_kernel, "copy", [source], (source.shape, source.dtype), before=wanted)
             chunks[k] = swap(source, "text", step)
     for r in range(2, n_speech, 2):
         blocks[r + 1] = swap(blocks[r], "speech", 1)
-    highs, lows, across_highs, across_lows = zip(*map(split_block, blocks))
+    split += [split_block(place, block, n_text) for block in blocks[2:]]
+    highs, lows, across_highs, across_lows = zip(*split)
+    for r in range(2, min(n_speech, 3)):
+        partials.append(call(more_kernel, "plan_more", [part_high, part_low, highs[r], lows[r]], part_tile))
 
     half = n_speech // 2
     tile = ((half * rows, frames), jnp.float32)
     outs = [tile, tile, ((8, frames), jnp.float32)]
     left_shape = ((feats, 2 * frames), jnp.bfloat16)
     plan_early, dots_early, sums, *left = call(
-        functools.partial(early_kernel, n_text, scale),
+        functools.partial(early_kernel, n_text - known, len(partials[:half]), group, scale),
         "plan_early",
-        [place, pot, *chunks, *highs[:half], *lows[:half]],
+        [place, pot, part_high, part_low, *chunks[known:], *partials[:half], *highs[:half], *lows[:half]],
         [*outs, left_shape, left_shape],
         places=1,
     )
     plan_late, dots_late, sums = call(
-        functools.partial(late_kernel, scale, half),
+        functools.partial(late_kernel, len(partials[half:]), scale, half),
         "plan_late",
-        [place, pot, sums, *left, *highs[half:], *lows[half:]],
+        [pot, sums, *left, *partials[half:], *highs[half:], *lows[half:]],
         outs,
+    )
+    plans, dots = (plan_early, plan_late), (dots_early, dots_late)
+    right = call(
+        functools.partial(across_kernel, n_text, group),
+        "frames_first",
+        [place, *left],
+        [(left_shape[0][::-1], jnp.bfloat16)] * 2,
         places=1,
-    )
-    plans, dots = (plan_early, plan_late), (dots_early, dots_late)
-    right = call(across_kernel, "frames_first", [*left], [(left_shape[0][::-1], jnp.bfloat16)] * 2, before=[sums])
+        before=[sums],
+    )
 
     estimate = sums
     total = []

time: 92.8 us -> 91.3 us (0.984)
  waiting for transfers between devices: 34.3 us -> 29.9 us
  Pallas kernels: 29.4 us -> 33.7 us
  local copies, waits for them, and re-layouts: 1.24 us -> 0.02 us
    ppermute x21, waiting for transfers between devices: 34.3 us -> 29.9 us  [swap(): return lax.ppermute(value, axis, [(i, i ^ k) for i in range(count)])]
    pallas_call x25 -> x27, Pallas kernels: 29.4 us -> 33.7 us  [call(): pl.pallas_call(body, in_specs=[IN_SMEM] * places + [IN_VMEM] * (count - p...]
    unnamed x4, local copies, waits for them, and re-layouts: 1.23 us -> 0.01 us
  transfers between devices with their start and end apart: 21 -> 21, of which waited for: 10 -> 9; matrix products, arithmetic and copies ran while one was open for 1% -> 1% of each run, Pallas kernels for 24% -> 29%
where the time goes in v1:
time: 91.3 us; the launch traced here: 91.1 us
  Pallas kernels  33.7 us (37%)
  waiting for transfers between devices  29.9 us (33%)
  starting transfers between devices  25.2 us (28%)
  other arithmetic  1.27 us (1%)
  between operations  0.92 us (1%)
    pallas_call x27, Pallas kernels, call(): pl.pallas_call(body, in_specs=[IN_SMEM] * places + [IN_VMEM] * (count - p...  33.7 us
    ppermute x21, waiting for transfers between devices, swap(): return lax.ppermute(value, axis, [(i, i ^ k) for i in range(count)])  29.9 us
    ppermute x21, starting transfers between devices, swap(): return lax.ppermute(value, axis, [(i, i ^ k) for i in range(count)])  25.2 us
  transfers between devices with their start and end apart: 21, of which 9 were waited for; matrix products, arithmetic and copies ran while one was open for 1% of the time, Pallas kernels for 29%

profile of v1, /device:TPU:0, one launch (start us, length us, event | category | flops | bytes accessed | tf_op | source)
XLA Modules:
  0.0 91.1 jit_solution(1137450967057277135)
XLA Ops:
  0.7 0.5 collective-permute-start
  1.2 2.6 %collective-permute-start.8 = (f32[512,512]{1,0:T(8,128)}, f32[512,512]{1,0:T(8,128)}, u32[]{:S(2)}, u32[]{:S(2)}) collective-permute-start(f32[512,512]{1,0:T(8,128)} %refs_1_.1), channel_id=1, source_target_pairs={{0,16},{8,24},{16,0},{24,8},{1,17},{9,25},{17,1},{25,9},{2,18},{10... | collective-permute-start | bytes 3145736 | tf_op jit(solution)/shard_map/ppermute | solution.py:231
  3.8 1.0 %pad_maximum_fusion.refs_0_ = f32[128,512]{1,0:T(8,128)S(1)} fusion(f32[64,512]{1,0:T(8,128)} %bitcast.5, f32[64,512]{1,0:T(8,128)} %bitcast.6), kind=kLoop, calls=%fused_computation | loop fusion | flops 65536 | bytes 524288 | tf_op jit(solution)/shard_map/concatenate | solution.py:249
  4.8 0.0 collective-permute-done.refs_1_
  4.8 1.9 %collective-permute-start.2 = (f32[128,512]{1,0:T(8,128)S(1)}, f32[128,512]{1,0:T(8,128)S(1)}, u32[]{:S(2)}, u32[]{:S(2)}) collective-permute-start(f32[128,512]{1,0:T(8,128)S(1)} %copy.9.refs_1_), channel_id=1, source_target_pairs={{0,2},{1,3},{2,0},{3,1},{4,6},{5,7},{6,4},{7,5},{8,10},{9,11},{10,... | collective-permute-start | bytes 786440 | tf_op jit(solution)/shard_map/ppermute | solution.py:231
  6.7 1.5 %collective-permute-start.1 = (f32[128,512]{1,0:T(8,128)S(1)}, f32[128,512]{1,0:T(8,128)S(1)}, u32[]{:S(2)}, u32[]{:S(2)}) collective-permute-start(f32[128,512]{1,0:T(8,128)S(1)} %copy.9.refs_1_), channel_id=1, source_target_pairs={{0,1},{1,0},{2,3},{3,2},{4,5},{5,4},{6,7},{7,6},{8,9},{9,8},{10,11... | collective-permute-start | bytes 786440 | tf_op jit(solution)/shard_map/ppermute | solution.py:231
  8.2 2.6 %collective-permute-start.4 = (f32[128,512]{1,0:T(8,128)S(1)}, f32[128,512]{1,0:T(8,128)S(1)}, u32[]{:S(2)}, u32[]{:S(2)}) collective-permute-start(f32[128,512]{1,0:T(8,128)S(1)} %copy.9.refs_1_), channel_id=1, source_target_pairs={{0,4},{1,5},{2,6},{3,7},{4,0},{5,1},{6,2},{7,3},{8,12},{9,13},{10,... | collective-permute-start | bytes 786440 | tf_op jit(solution)/shard_map/ppermute | solution.py:231
  10.8 0.1 pad_add_fusion.refs_0_
  10.9 0.9 offsets.1.refs_3_.refs_1_.refs_0_
  11.8 1.2 %split.4 = (bf16[512,512]{1,0:T(8,128)(2,1)S(1)}, bf16[512,512]{1,0:T(8,128)(2,1)S(1)}, bf16[512,512]{1,0:T(8,128)(2,1)S(1)}, bf16[512,512]{1,0:T(8,128)(2,1)S(1)}) custom-call(s32[2]{0:T(128)S(1)} %pad_add_fusion.refs_0_, f32[512,512]{1,0:T(8,128)S(1)} %copy-done), custom_call_target="tpu_custom_call" | custom-call | flops 1000000000 | tf_op jit(solution)/shard_map/split/pallas_call | solution.py:55
  12.9 4.6 %collective-permute-done.2.refs_3_.refs_2_ = f32[128,512]{1,0:T(8,128)S(1)} collective-permute-done((f32[128,512]{1,0:T(8,128)S(1)}, f32[128,512]{1,0:T(8,128)S(1)}, u32[]{:S(2)}, u32[]{:S(2)}) %collective-permute-start.2) | collective-permute-done | bytes 262176 | tf_op jit(solution)/shard_map/ppermute | solution.py:231
  17.6 2.6 %collective-permute-start.3 = (f32[128,512]{1,0:T(8,128)S(1)}, f32[128,512]{1,0:T(8,128)S(1)}, u32[]{:S(2)}, u32[]{:S(2)}) collective-permute-start(f32[128,512]{1,0:T(8,128)S(1)} %collective-permute-done.2.refs_3_.refs_2_), channel_id=1, source_target_pairs={{0,1},{1,0},{2,3},{3,2},{4,5},{5,4},{6,7},{7,6},{8,9},{9,8},{10,11... | collective-permute-start | bytes 786440 | tf_op jit(solution)/shard_map/ppermute | solution.py:231
  20.2 1.2 %split.5 = (bf16[512,512]{1,0:T(8,128)(2,1)S(1)}, bf16[512,512]{1,0:T(8,128)(2,1)S(1)}, bf16[512,512]{1,0:T(8,128)(2,1)S(1)}, bf16[512,512]{1,0:T(8,128)(2,1)S(1)}) custom-call(s32[2]{0:T(128)S(1)} %pad_add_fusion.refs_0_, f32[512,512]{1,0:T(8,128)S(1)} %collective-permute-done.refs_1_), custom_call_target="tpu_custom_call" | custom-call | flops 1000000000 | tf_op jit(solution)/shard_map/split/pallas_call | solution.py:55
  21.4 0.0 collective-permute-done.1.refs_2_.refs_1_
  21.4 1.2 %collective-permute-done.4.refs_0_.refs_4_ = f32[128,512]{1,0:T(8,128)S(1)} collective-permute-done((f32[128,512]{1,0:T(8,128)S(1)}, f32[128,512]{1,0:T(8,128)S(1)}, u32[]{:S(2)}, u32[]{:S(2)}) %collective-permute-start.4) | collective-permute-done | bytes 262176 | tf_op jit(solution)/shard_map/ppermute | solution.py:231
  22.6 0.1 collective-permute-start.6
  22.7 0.7 collective-permute-start.5
  23.4 4.0 %collective-permute-done.3.refs_4_ = f32[128,512]{1,0:T(8,128)S(1)} collective-permute-done((f32[128,512]{1,0:T(8,128)S(1)}, f32[128,512]{1,0:T(8,128)S(1)}, u32[]{:S(2)}, u32[]{:S(2)}) %collective-permute-start.3) | collective-permute-done | bytes 262176 | tf_op jit(solution)/shard_map/ppermute | solution.py:231
  27.4 2.5 %plan_part.1 = (f32[512,1024]{1,0:T(8,128)S(1)}, f32[512,1024]{1,0:T(8,128)S(1)}, bf16[256,1024]{1,0:T(8,128)(2,1)S(1)}, bf16[256,1024]{1,0:T(8,128)(2,1)S(1)}) custom-call(s32[2]{0:T(128)S(1)} %pad_add_fusion.refs_0_, f32[128,512]{1,0:T(8,128)S(1)} %copy.9.refs_1_, f32[128,512]{1,0:T(8,128)S(1)} %collective-permute-done.1.refs_2_.refs_1_, ...), custom_call_target="tpu_custom_call" | custom-call | flops 1000000000 | tf_op jit(solution)/shard_map/plan_part/pallas_call | solution.py:55
  29.9 0.0 collective-permute-done.6.refs_0_.refs_6_
  29.9 2.1 %collective-permute-start.7 = (f32[128,512]{1,0:T(8,128)S(1)}, f32[128,512]{1,0:T(8,128)S(1)}, u32[]{:S(2)}, u32[]{:S(2)}) collective-permute-start(f32[128,512]{1,0:T(8,128)S(1)} %copy.11), channel_id=1, source_target_pairs={{0,1},{1,0},{2,3},{3,2},{4,5},{5,4},{6,7},{7,6},{8,9},{9,8},{10,11... | collective-permute-start | bytes 786440 | tf_op jit(solution)/shard_map/ppermute | solution.py:231
  32.0 0.0 collective-permute-done.8.refs_1_
  32.0 0.0 collective-permute-start.9
  32.0 1.9 %split.6 = (bf16[512,512]{1,0:T(8,128)(2,1)S(1)}, bf16[512,512]{1,0:T(8,128)(2,1)S(1)}, bf16[512,512]{1,0:T(8,128)(2,1)S(1)}, bf16[512,512]{1,0:T(8,128)(2,1)S(1)}) custom-call(s32[2]{0:T(128)S(1)} %pad_add_fusion.refs_0_, f32[512,512]{1,0:T(8,128)} %collective-permute-done.8.refs_1_), custom_call_target="tpu_custom_call" | custom-call | flops 1000000000 | tf_op jit(solution)/shard_map/split/pallas_call | solution.py:55
  33.9 1.0 %plan_more.1.refs_4_ = f32[512,1024]{1,0:T(8,128)S(1)} custom-call(bf16[256,1024]{1,0:T(8,128)(2,1)S(1)} %get-tuple-element.44.refs_1_.refs_2_.refs_0_, bf16[256,1024]{1,0:T(8,128)(2,1)S(1)} %get-tuple-element.45.refs_3_.refs_1_, bf16[512,512]{1,0:T(8,128)(2,1)S(1)} %get-tuple-element.51.refs_2_.refs_5_, bf16[512,512]{1,0:T(8,128)(2,1)S(1)} %get-tuple-element.52.refs_3_.refs_7_), custom_call_target="tpu_custom_call" | custom-call | flops 1000000000 | tf_op jit(solution)/shard_map/plan_more/pallas_call | solution.py:55
  34.9 0.0 collective-permute-done.5.refs_5_
  34.9 2.4 %collective-permute-done.7.refs_7_ = f32[128,512]{1,0:T(8,128)S(1)} collective-permute-done((f32[128,512]{1,0:T(8,128)S(1)}, f32[128,512]{1,0:T(8,128)S(1)}, u32[]{:S(2)}, u32[]{:S(2)}) %collective-permute-start.7) | collective-permute-done | bytes 262176 | tf_op jit(solution)/shard_map/ppermute | solution.py:231
  37.3 3.0 %plan_early.1 = (f32[1024,512]{1,0:T(8,128)S(1)}, f32[1024,512]{1,0:T(8,128)S(1)}, f32[8,512]{1,0:T(8,128)S(1)}, bf16[512,1024]{1,0:T(8,128)(2,1)S(1)}, bf16[512,1024]{1,0:T(8,128)(2,1)S(1)}) custom-call(s32[2]{0:T(128)S(1)} %pad_add_fusion.refs_0_, f32[2048,128]{1,0:T(8,128)S(1)} %offsets.1.refs_3_.refs_1_.refs_0_, ...), custom_call_target="tpu_custom_call" | custom-call | flops 99999997952 | tf_op jit(solution)/shard_map/plan_early/pallas_call | solution.py:55
  40.3 0.0 collective-permute-done.9.refs_1_
  40.3 1.2 %split.7 = (bf16[512,512]{1,0:T(8,128)(2,1)S(1)}, bf16[512,512]{1,0:T(8,128)(2,1)S(1)}, bf16[512,512]{1,0:T(8,128)(2,1)S(1)}, bf16[512,512]{1,0:T(8,128)(2,1)S(1)}) custom-call(s32[2]{0:T(128)S(1)} %pad_add_fusion.refs_0_, f32[512,512]{1,0:T(8,128)S(1)} %collective-permute-done.9.refs_1_), custom_call_target="tpu_custom_call" | custom-call | flops 1000000000 | tf_op jit(solution)/shard_map/split/pallas_call | solution.py:55
  41.5 2.8 %plan_late.1 = (f32[1024,512]{1,0:T(8,128)S(1)}, f32[1024,512]{1,0:T(8,128)S(1)}, f32[8,512]{1,0:T(8,128)S(1)}) custom-call(f32[2048,128]{1,0:T(8,128)S(1)} %offsets.1.refs_3_.refs_1_.refs_0_, f32[8,512]{1,0:T(8,128)S(1)} %get-tuple-element.48.refs_1_, bf16[512,1024]{1,0:T(8,128)(2,1)S(1)} %get-tuple-element.49.refs_2_.refs_1_, ...), custom_call_target="tpu_custom_call" | custom-call | flops 3000000000 | tf_op jit(solution)/shard_map/plan_late/pallas_call | solution.py:55
  44.3 1.8 %collective-permute-start.10 = (f32[8,512]{1,0:T(8,128)S(1)}, f32[8,512]{1,0:T(8,128)S(1)}, u32[]{:S(2)}, u32[]{:S(2)}) collective-permute-start(f32[8,512]{1,0:T(8,128)S(1)} %get-tuple-element.55.refs_0_.refs_5_.refs_3_.refs_1_), channel_id=1, source_target_pairs={{0,1},{1,0},{2,3},{3,2},{4,5},{5,4},{6,7},{7,6},{8,9},{9,8},{10,11... | collective-permute-start | bytes 49160 | tf_op jit(solution)/shard_map/ppermute | solution.py:231
  46.1 1.9 %moments.3.refs_2_.refs_5_ = f32[512,1024]{1,0:T(8,128)S(1)} custom-call(f32[8,512]{1,0:T(8,128)S(1)} %get-tuple-element.55.refs_0_.refs_5_.refs_3_.refs_1_, f32[1024,512]{1,0:T(8,128)S(1)} %get-tuple-element.56.refs_1_, f32[1024,512]{1,0:T(8,128)S(1)} %get-tuple-element.57.refs_2_, bf16[512,512]{1,0:T(8,128)(2,1)S(1)} %get-tuple-element.58.refs_3_, ...), custom_call_target="tpu_custom_call" | custom-call | flops 3000000000 | tf_op jit(solution)/shard_map/moments/pallas_call | solution.py:55
  48.0 1.2 %frames_first.1 = (bf16[1024,512]{1,0:T(8,128)(2,1)S(1)}, bf16[1024,512]{1,0:T(8,128)(2,1)S(1)}) custom-call(s32[2]{0:T(128)S(1)} %pad_add_fusion.refs_0_, bf16[512,1024]{1,0:T(8,128)(2,1)S(1)} %get-tuple-element.49.refs_2_.refs_1_, bf16[512,1024]{1,0:T(8,128)(2,1)S(1)} %get-tuple-element.50.refs_3_.refs_2_, ...), custom_call_target="tpu_custom_call" | custom-call | flops 1000000000 | tf_op jit(solution)/shard_map/frames_first/pallas_call | solution.py:55
  49.2 0.0 collective-permute-done.10.refs_1_
  49.3 0.1 collective-permute-start.11
  49.3 2.1 %moments.4.refs_2_.refs_5_ = f32[512,1024]{1,0:T(8,128)S(1)} custom-call(f32[8,512]{1,0:T(8,128)S(1)} %get-tuple-element.55.refs_0_.refs_5_.refs_3_.refs_1_, f32[1024,512]{1,0:T(8,128)S(1)} %get-tuple-element.56.refs_1_, f32[1024,512]{1,0:T(8,128)S(1)} %get-tuple-element.57.refs_2_, bf16[512,512]{1,0:T(8,128)(2,1)S(1)} %get-tuple-element.60.refs_3_, ...), custom_call_target="tpu_custom_call" | custom-call | flops 3000000000 | tf_op jit(solution)/shard_map/moments/pallas_call | solution.py:55
  51.4 1.6 %collective-permute-done.11.refs_1_ = f32[8,512]{1,0:T(8,128)S(1)} collective-permute-done((f32[8,512]{1,0:T(8,128)S(1)}, f32[8,512]{1,0:T(8,128)S(1)}, u32[]{:S(2)}, u32[]{:S(2)}) %collective-permute-start.11) | collective-permute-done | bytes 16416 | tf_op jit(solution)/shard_map/ppermute | solution.py:231
  53.1 1.5 %collective-permute-start.12 = (f32[8,512]{1,0:T(8,128)S(1)}, f32[8,512]{1,0:T(8,128)S(1)}, u32[]{:S(2)}, u32[]{:S(2)}) collective-permute-start(f32[8,512]{1,0:T(8,128)S(1)} %hop.4.refs_6_.refs_0_), channel_id=1, source_target_pairs={{0,4},{1,5},{2,6},{3,7},{4,0},{5,1},{6,2},{7,3},{8,12},{9,13},{10,... | collective-permute-start | bytes 49160 | tf_op jit(solution)/shard_map/ppermute | solution.py:231
  54.5 1.9 %moments.5.refs_2_.refs_3_ = f32[512,1024]{1,0:T(8,128)S(1)} custom-call(f32[8,512]{1,0:T(8,128)S(1)} %get-tuple-element.55.refs_0_.refs_5_.refs_3_.refs_1_, f32[1024,512]{1,0:T(8,128)S(1)} %get-tuple-element.62.refs_1_.refs_4_, f32[1024,512]{1,0:T(8,128)S(1)} %get-tuple-element.63.refs_2_.refs_5_, bf16[512,512]{1,0:T(8,128)(2,1)S(1)} %get-tuple-element.64.refs_3_, ...), custom_call_target="tpu_custom_call" | custom-call | flops 3000000000 | tf_op jit(solution)/shard_map/moments/pallas_call | solution.py:55
  56.4 1.4 %collective-permute-done.12.refs_1_ = f32[8,512]{1,0:T(8,128)S(1)} collective-permute-done((f32[8,512]{1,0:T(8,128)S(1)}, f32[8,512]{1,0:T(8,128)S(1)}, u32[]{:S(2)}, u32[]{:S(2)}) %collective-permute-start.12) | collective-permute-done | bytes 16416 | tf_op jit(solution)/shard_map/ppermute | solution.py:231
  57.8 1.9 %text_far.2.refs_8_.refs_5_ = f32[512,512]{1,0:T(8,128)S(1)} custom-call(f32[8,512]{1,0:T(8,128)S(1)} %hop.5.refs_0_.refs_2_, f32[1024,512]{1,0:T(8,128)S(1)} %get-tuple-element.62.refs_1_.refs_4_, f32[1024,512]{1,0:T(8,128)S(1)} %get-tuple-element.63.refs_2_.refs_5_, bf16[1024,512]{1,0:T(8,128)(2,1)S(1)} %get-tuple-element.68.refs_3_, ...), custom_call_target="tpu_custom_call" | custom-call | flops 3000000000 | tf_op jit(solution)/shard_map/text_far/pallas_call | solution.py:55
  59.7 0.1 collective-permute-start.14
  59.7 1.8 %finish.1 = (f32[4,64,512]{2,1,0:T(8,128)S(1)}, f32[4,64,512]{2,1,0:T(8,128)S(1)}) custom-call(s32[2]{0:T(128)S(1)} %pad_add_fusion.refs_0_, f32[8,512]{1,0:T(8,128)S(1)} %get-tuple-element.55.refs_0_.refs_5_.refs_3_.refs_1_, f32[8,512]{1,0:T(8,128)S(1)} %hop.5.refs_0_.refs_2_, f32[512,1024]{1,0:T(8,128)S(1)} %moments.5.refs_2_.refs_3_, ...), custom_call_target="tpu_custom_call" | custom-call | flops 1000000000 | tf_op jit(solution)/shard_map/finish/pallas_call | solution.py:55
  61.5 0.6 collective-permute-start.13
  62.2 1.9 %text_far.3 = f32[512,512]{1,0:T(8,128)S(1)} custom-call(f32[8,512]{1,0:T(8,128)S(1)} %hop.5.refs_0_.refs_2_, f32[1024,512]{1,0:T(8,128)S(1)} %get-tuple-element.62.refs_1_.refs_4_, f32[1024,512]{1,0:T(8,128)S(1)} %get-tuple-element.63.refs_2_.refs_5_, bf16[1024,512]{1,0:T(8,128)(2,1)S(1)} %get-tuple-element.68.refs_3_, ...), custom_call_target="tpu_custom_call" | custom-call | flops 3000000000 | tf_op jit(solution)/shard_map/text_far/pallas_call | solution.py:55
  64.0 0.0 collective-permute-done.14
  64.1 0.2 add.4.refs_5_
  64.3 1.6 %collective-permute-start.20 = (f32[512,512]{1,0:T(8,128)S(1)}, f32[512,512]{1,0:T(8,128)S(1)}, u32[]{:S(2)}, u32[]{:S(2)}) collective-permute-start(f32[512,512]{1,0:T(8,128)S(1)} %add.4.refs_5_), channel_id=1, source_target_pairs={{0,16},{8,24},{16,0},{24,8},{1,17},{9,25},{17,1},{25,9},{2,18},{10... | collective-permute-start | bytes 3145736 | tf_op jit(solution)/shard_map/ppermute | solution.py:231
  65.9 1.8 %text_near.2 = (f32[256,512]{1,0:T(8,128)S(1)}, f32[256,512]{1,0:T(8,128)S(1)}) custom-call(f32[8,512]{1,0:T(8,128)S(1)} %hop.5.refs_0_.refs_2_, f32[1024,512]{1,0:T(8,128)S(1)} %get-tuple-element.56.refs_1_, f32[1024,512]{1,0:T(8,128)S(1)} %get-tuple-element.57.refs_2_, bf16[1024,512]{1,0:T(8,128)(2,1)S(1)} %get-tuple-element.68.refs_3_, ...), custom_call_target="tpu_custom_call" | custom-call | flops 3000000000 | tf_op jit(solution)/shard_map/text_near/pallas_call | solution.py:55
  67.7 0.1 collective-permute-start.15
  67.8 0.5 collective-permute-start.16
  68.3 7.6 %collective-permute-done.13.refs_1_ = f32[4,64,512]{2,1,0:T(8,128)S(1)} collective-permute-done((f32[4,64,512]{2,1,0:T(8,128)S(1)}, f32[4,64,512]{2,1,0:T(8,128)S(1)}, u32[]{:S(2)}, u32[]{:S(2)}) %collective-permute-start.13) | collective-permute-done | bytes 524320 | tf_op jit(solution)/shard_map/ppermute | solution.py:231
  75.9 0.0 collective-permute-done.15.refs_2_
  75.9 0.1 near.1
  76.0 0.5 collective-permute-start.17
  76.5 2.6 %collective-permute-start.18 = (f32[64,512]{1,0:T(8,128)S(1)}, f32[64,512]{1,0:T(8,128)S(1)}, u32[]{:S(2)}, u32[]{:S(2)}) collective-permute-start(f32[64,512]{1,0:T(8,128)S(1)} %get-tuple-element.76), channel_id=1, source_target_pairs={{0,4},{1,5},{2,6},{3,7},{4,0},{5,1},{6,2},{7,3},{8,12},{9,13},{10,... | collective-permute-start | bytes 393224 | tf_op jit(solution)/shard_map/ppermute | solution.py:231
  79.1 1.3 %collective-permute-start.19 = (f32[64,512]{1,0:T(8,128)S(1)}, f32[64,512]{1,0:T(8,128)S(1)}, u32[]{:S(2)}, u32[]{:S(2)}) collective-permute-start(f32[64,512]{1,0:T(8,128)S(1)} %get-tuple-element.77), channel_id=1, source_target_pairs={{0,6},{1,7},{2,4},{3,5},{4,2},{5,3},{6,0},{7,1},{8,14},{9,15},{10,... | collective-permute-start | bytes 393224 | tf_op jit(solution)/shard_map/ppermute | solution.py:231
  80.5 1.8 %text_near.3.refs_4_.refs_0_ = f32[512,512]{1,0:T(8,128)S(1)} custom-call(f32[8,512]{1,0:T(8,128)S(1)} %hop.5.refs_0_.refs_2_, f32[1024,512]{1,0:T(8,128)S(1)} %get-tuple-element.56.refs_1_, f32[1024,512]{1,0:T(8,128)S(1)} %get-tuple-element.57.refs_2_, bf16[1024,512]{1,0:T(8,128)(2,1)S(1)} %get-tuple-element.68.refs_3_, ...), custom_call_target="tpu_custom_call" | custom-call | flops 3000000000 | tf_op jit(solution)/shard_map/text_near/pallas_call | solution.py:55
  82.3 0.8 collective-permute-done.17.refs_1_
  83.1 6.2 %collective-permute-done.18.refs_2_ = f32[64,512]{1,0:T(8,128)S(1)} collective-permute-done((f32[64,512]{1,0:T(8,128)S(1)}, f32[64,512]{1,0:T(8,128)S(1)}, u32[]{:S(2)}, u32[]{:S(2)}) %collective-permute-start.18) | collective-permute-done | bytes 131104 | tf_op jit(solution)/shard_map/ppermute | solution.py:231
  89.3 0.0 collective-permute-done.19.refs_3_
  89.3 0.7 join.1
  90.0 1.1 %add.7 = f32[512,512]{1,0:T(8,128)} custom-call(f32[512,512]{1,0:T(8,128)S(1)} %text_near.3.refs_4_.refs_0_, f32[512,512]{1,0:T(8,128)S(1)} %collective-permute-done.20.refs_1_, f32[256,512]{1,0:T(8,128)S(1)} %collective-permute-done.15.refs_2_, f32[256,512]{1,0:T(8,128)S(1)} %collective-permute-done.16.refs_3_), custom_call_target="tpu_custom_call" | custom-call | flops 99999997952 | tf_op jit(solution)/shard_map/add/pallas_call | solution.py:55
  (13 shorter events, 0.1 us)
Async XLA Ops:
  0.6 11.1 %copy-start = (f32[512,512]{1,0:T(8,128)S(1)}, f32[512,512]{1,0:T(8,128)}, u32[]{:S(2)}) copy-start(f32[512,512]{1,0:T(8,128)} %refs_1_.1) | copy-start | bytes 3145732
  0.6 6.1 %copy-start.1 = (f32[2048]{0:T(1024)S(1)}, f32[2048]{0:T(1024)}, u32[]{:S(2)}) copy-start(f32[2048]{0:T(1024)} %param.6) | copy-start | bytes 24580
  0.7 4.1 %collective-permute-start = (f32[512,512]{1,0:T(8,128)}, f32[512,512]{1,0:T(8,128)S(1)}, u32[]{:S(2)}, u32[]{:S(2)}) collective-permute-start(f32[512,512]{1,0:T(8,128)} %refs_1_.1), channel_id=1, source_target_pairs={{0,8},{8,0},{16,24},{24,16},{1,9},{9,1},{17,25},{25,17},{2,10},{10... | collective-permute-start | bytes 3145736 | tf_op jit(solution)/shard_map/ppermute | solution.py:231
  1.2 30.9 %collective-permute-start.8 = (f32[512,512]{1,0:T(8,128)}, f32[512,512]{1,0:T(8,128)}, u32[]{:S(2)}, u32[]{:S(2)}) collective-permute-start(f32[512,512]{1,0:T(8,128)} %refs_1_.1), channel_id=1, source_target_pairs={{0,16},{8,24},{16,0},{24,8},{1,17},{9,25},{17,1},{25,9},{2,18},{10... | collective-permute-start | bytes 3145736 | tf_op jit(solution)/shard_map/ppermute | solution.py:231
  4.8 12.8 %collective-permute-start.2 = (f32[128,512]{1,0:T(8,128)S(1)}, f32[128,512]{1,0:T(8,128)S(1)}, u32[]{:S(2)}, u32[]{:S(2)}) collective-permute-start(f32[128,512]{1,0:T(8,128)S(1)} %copy.9.refs_1_), channel_id=1, source_target_pairs={{0,2},{1,3},{2,0},{3,1},{4,6},{5,7},{6,4},{7,5},{8,10},{9,11},{10,... | collective-permute-start | bytes 786440 | tf_op jit(solution)/shard_map/ppermute | solution.py:231
  6.7 14.7 %collective-permute-start.1 = (f32[128,512]{1,0:T(8,128)S(1)}, f32[128,512]{1,0:T(8,128)S(1)}, u32[]{:S(2)}, u32[]{:S(2)}) collective-permute-start(f32[128,512]{1,0:T(8,128)S(1)} %copy.9.refs_1_), channel_id=1, source_target_pairs={{0,1},{1,0},{2,3},{3,2},{4,5},{5,4},{6,7},{7,6},{8,9},{9,8},{10,11... | collective-permute-start | bytes 786440 | tf_op jit(solution)/shard_map/ppermute | solution.py:231
  8.2 14.4 %collective-permute-start.4 = (f32[128,512]{1,0:T(8,128)S(1)}, f32[128,512]{1,0:T(8,128)S(1)}, u32[]{:S(2)}, u32[]{:S(2)}) collective-permute-start(f32[128,512]{1,0:T(8,128)S(1)} %copy.9.refs_1_), channel_id=1, source_target_pairs={{0,4},{1,5},{2,6},{3,7},{4,0},{5,1},{6,2},{7,3},{8,12},{9,13},{10,... | collective-permute-start | bytes 786440 | tf_op jit(solution)/shard_map/ppermute | solution.py:231
  17.6 9.8 %collective-permute-start.3 = (f32[128,512]{1,0:T(8,128)S(1)}, f32[128,512]{1,0:T(8,128)S(1)}, u32[]{:S(2)}, u32[]{:S(2)}) collective-permute-start(f32[128,512]{1,0:T(8,128)S(1)} %collective-permute-done.2.refs_3_.refs_2_), channel_id=1, source_target_pairs={{0,1},{1,0},{2,3},{3,2},{4,5},{5,4},{6,7},{7,6},{8,9},{9,8},{10,11... | collective-permute-start | bytes 786440 | tf_op jit(solution)/shard_map/ppermute | solution.py:231
  22.6 7.3 %collective-permute-start.6 = (f32[128,512]{1,0:T(8,128)S(1)}, f32[128,512]{1,0:T(8,128)S(1)}, u32[]{:S(2)}, u32[]{:S(2)}) collective-permute-start(f32[128,512]{1,0:T(8,128)S(1)} %copy.10), channel_id=1, source_target_pairs={{0,2},{1,3},{2,0},{3,1},{4,6},{5,7},{6,4},{7,5},{8,10},{9,11},{10,... | collective-permute-start | bytes 786440 | tf_op jit(solution)/shard_map/ppermute | solution.py:231
  22.7 12.2 %collective-permute-start.5 = (f32[128,512]{1,0:T(8,128)S(1)}, f32[128,512]{1,0:T(8,128)S(1)}, u32[]{:S(2)}, u32[]{:S(2)}) collective-permute-start(f32[128,512]{1,0:T(8,128)S(1)} %collective-permute-done.4.refs_0_.refs_4_), channel_id=1, source_target_pairs={{0,1},{1,0},{2,3},{3,2},{4,5},{5,4},{6,7},{7,6},{8,9},{9,8},{10,11... | collective-permute-start | bytes 786440 | tf_op jit(solution)/shard_map/ppermute | solution.py:231
  29.9 7.4 %collective-permute-start.7 = (f32[128,512]{1,0:T(8,128)S(1)}, f32[128,512]{1,0:T(8,128)S(1)}, u32[]{:S(2)}, u32[]{:S(2)}) collective-permute-start(f32[128,512]{1,0:T(8,128)S(1)} %copy.11), channel_id=1, source_target_pairs={{0,1},{1,0},{2,3},{3,2},{4,5},{5,4},{6,7},{7,6},{8,9},{9,8},{10,11... | collective-permute-start | bytes 786440 | tf_op jit(solution)/shard_map/ppermute | solution.py:231
  32.0 8.3 %collective-permute-start.9 = (f32[512,512]{1,0:T(8,128)}, f32[512,512]{1,0:T(8,128)S(1)}, u32[]{:S(2)}, u32[]{:S(2)}) collective-permute-start(f32[512,512]{1,0:T(8,128)} %collective-permute-done.8.refs_1_), channel_id=1, source_target_pairs={{0,8},{8,0},{16,24},{24,16},{1,9},{9,1},{17,25},{25,17},{2,10},{10... | collective-permute-start | bytes 3145736 | tf_op jit(solution)/shard_map/ppermute | solution.py:231
  44.3 4.9 %collective-permute-start.10 = (f32[8,512]{1,0:T(8,128)S(1)}, f32[8,512]{1,0:T(8,128)S(1)}, u32[]{:S(2)}, u32[]{:S(2)}) collective-permute-start(f32[8,512]{1,0:T(8,128)S(1)} %get-tuple-element.55.refs_0_.refs_5_.refs_3_.refs_1_), channel_id=1, source_target_pairs={{0,1},{1,0},{2,3},{3,2},{4,5},{5,4},{6,7},{7,6},{8,9},{9,8},{10,11... | collective-permute-start | bytes 49160 | tf_op jit(solution)/shard_map/ppermute | solution.py:231
  49.3 3.8 %collective-permute-start.11 = (f32[8,512]{1,0:T(8,128)S(1)}, f32[8,512]{1,0:T(8,128)S(1)}, u32[]{:S(2)}, u32[]{:S(2)}) collective-permute-start(f32[8,512]{1,0:T(8,128)S(1)} %hop.3.refs_6_.refs_0_), channel_id=1, source_target_pairs={{0,2},{1,3},{2,0},{3,1},{4,6},{5,7},{6,4},{7,5},{8,10},{9,11},{10,... | collective-permute-start | bytes 49160 | tf_op jit(solution)/shard_map/ppermute | solution.py:231
  53.1 4.7 %collective-permute-start.12 = (f32[8,512]{1,0:T(8,128)S(1)}, f32[8,512]{1,0:T(8,128)S(1)}, u32[]{:S(2)}, u32[]{:S(2)}) collective-permute-start(f32[8,512]{1,0:T(8,128)S(1)} %hop.4.refs_6_.refs_0_), channel_id=1, source_target_pairs={{0,4},{1,5},{2,6},{3,7},{4,0},{5,1},{6,2},{7,3},{8,12},{9,13},{10,... | collective-permute-start | bytes 49160 | tf_op jit(solution)/shard_map/ppermute | solution.py:231
  59.7 4.4 %collective-permute-start.14 = (f32[512,512]{1,0:T(8,128)S(1)}, f32[512,512]{1,0:T(8,128)S(1)}, u32[]{:S(2)}, u32[]{:S(2)}) collective-permute-start(f32[512,512]{1,0:T(8,128)S(1)} %text_far.2.refs_8_.refs_5_), channel_id=1, source_target_pairs={{0,8},{8,0},{16,24},{24,16},{1,9},{9,1},{17,25},{25,17},{2,10},{10... | collective-permute-start | bytes 3145736 | tf_op jit(solution)/shard_map/ppermute | solution.py:231
  61.5 14.4 %collective-permute-start.13 = (f32[4,64,512]{2,1,0:T(8,128)S(1)}, f32[4,64,512]{2,1,0:T(8,128)S(1)}, u32[]{:S(2)}, u32[]{:S(2)}) collective-permute-start(f32[4,64,512]{2,1,0:T(8,128)S(1)} %get-tuple-element.71), channel_id=1, source_target_pairs={{0,1},{1,0},{2,3},{3,2},{4,5},{5,4},{6,7},{7,6},{8,9},{9,8},{10,11... | collective-permute-start | bytes 1572872 | tf_op jit(solution)/shard_map/ppermute | solution.py:231
  64.3 25.7 %collective-permute-start.20 = (f32[512,512]{1,0:T(8,128)S(1)}, f32[512,512]{1,0:T(8,128)S(1)}, u32[]{:S(2)}, u32[]{:S(2)}) collective-permute-start(f32[512,512]{1,0:T(8,128)S(1)} %add.4.refs_5_), channel_id=1, source_target_pairs={{0,16},{8,24},{16,0},{24,8},{1,17},{9,25},{17,1},{25,9},{2,18},{10... | collective-permute-start | bytes 3145736 | tf_op jit(solution)/shard_map/ppermute | solution.py:231
  67.7 8.2 %collective-permute-start.15 = (f32[256,512]{1,0:T(8,128)S(1)}, f32[256,512]{1,0:T(8,128)S(1)}, u32[]{:S(2)}, u32[]{:S(2)}) collective-permute-start(f32[256,512]{1,0:T(8,128)S(1)} %get-tuple-element.72), channel_id=1, source_target_pairs={{0,8},{8,0},{16,24},{24,16},{1,9},{9,1},{17,25},{25,17},{2,10},{10... | collective-permute-start | bytes 1572872 | tf_op jit(solution)/shard_map/ppermute | solution.py:231
  67.8 8.1 %collective-permute-start.16 = (f32[256,512]{1,0:T(8,128)S(1)}, f32[256,512]{1,0:T(8,128)S(1)}, u32[]{:S(2)}, u32[]{:S(2)}) collective-permute-start(f32[256,512]{1,0:T(8,128)S(1)} %get-tuple-element.73), channel_id=1, source_target_pairs={{0,8},{8,0},{16,24},{24,16},{1,9},{9,1},{17,25},{25,17},{2,10},{10... | collective-permute-start | bytes 1572872 | tf_op jit(solution)/shard_map/ppermute | solution.py:231
  76.0 7.1 %collective-permute-start.17 = (f32[64,512]{1,0:T(8,128)S(1)}, f32[64,512]{1,0:T(8,128)S(1)}, u32[]{:S(2)}, u32[]{:S(2)}) collective-permute-start(f32[64,512]{1,0:T(8,128)S(1)} %get-tuple-element.75), channel_id=1, source_target_pairs={{0,2},{1,3},{2,0},{3,1},{4,6},{5,7},{6,4},{7,5},{8,10},{9,11},{10,... | collective-permute-start | bytes 393224 | tf_op jit(solution)/shard_map/ppermute | solution.py:231
  76.5 12.8 %collective-permute-start.18 = (f32[64,512]{1,0:T(8,128)S(1)}, f32[64,512]{1,0:T(8,128)S(1)}, u32[]{:S(2)}, u32[]{:S(2)}) collective-permute-start(f32[64,512]{1,0:T(8,128)S(1)} %get-tuple-element.76), channel_id=1, source_target_pairs={{0,4},{1,5},{2,6},{3,7},{4,0},{5,1},{6,2},{7,3},{8,12},{9,13},{10,... | collective-permute-start | bytes 393224 | tf_op jit(solution)/shard_map/ppermute | solution.py:231
  79.1 10.2 %collective-permute-start.19 = (f32[64,512]{1,0:T(8,128)S(1)}, f32[64,512]{1,0:T(8,128)S(1)}, u32[]{:S(2)}, u32[]{:S(2)}) collective-permute-start(f32[64,512]{1,0:T(8,128)S(1)} %get-tuple-element.77), channel_id=1, source_target_pairs={{0,6},{1,7},{2,4},{3,5},{4,2},{5,3},{6,0},{7,1},{8,14},{9,15},{10,... | collective-permute-start | bytes 393224 | tf_op jit(solution)/shard_map/ppermute | solution.py:231

commit v2 on v1

--- a/solution.py
+++ b/solution.py
@@ -79,18 +79,22 @@
     return min(n_text, max(2, LANES // width))
 
 
-def group_starts(place, group, width, n_text):
-    mine = place[0] - place[0] % group
-    return [pl.multiple_of((mine ^ first) * width, group * width) for first in range(0, n_text, group)]
+def by_distance(value, place, group, lanes):
+    count = value.shape[1] // lanes
+    step = 1
+    while step < count:
+        pieces = [value[:, (i ^ step) * lanes : (i ^ step) * lanes + lanes] for i in range(count)]
+        odd = (place[0] // (group * step)) % 2 == 1
+        value = jnp.where(odd, jnp.concatenate(pieces, axis=1), value)
+        step *= 2
+    return value
 
 
 def split_kernel(n_text, group, place, block, high_out, low_out, across_high, across_low):
     value = block[...]
     across_high[...], across_low[...] = halves(value.T)
     lanes = block.shape[1] // n_text * group
-    for i, start in enumerate(group_starts(place, group, lanes // group, n_text)):
-        columns = slice(i * lanes, (i + 1) * lanes)
-        high_out[:, columns], low_out[:, columns] = halves(block[:, pl.ds(start, lanes)])
+    high_out[...], low_out[...] = halves(by_distance(value, place, group, lanes))
 
 
 def split_block(place, block, n_text):
@@ -178,10 +182,9 @@
 
 def across_kernel(n_text, group, place, high, low, high_out, low_out):
     lanes = high.shape[0] // n_text * group
-    starts = group_starts(place, group, lanes // group, n_text)
     for value, out in ((high, high_out), (low, low_out)):
-        ordered = jnp.concatenate([value[pl.ds(start, lanes), :] for start in starts], axis=0)
-        out[...] = ordered.astype(jnp.float32).T.astype(jnp.bfloat16)
+        across = value[...].astype(jnp.float32).T
+        out[...] = by_distance(across, place, group, lanes).astype(jnp.bfloat16)
 
 
 def weights(sums, plan, grad_dots, scale):
@@ -211,7 +214,8 @@
     out[...] = total[0][...] + term if total else term
 
 
-def finish_kernel(n_text, scale, first, place, estimate, sums, total, plan, grad_dots, high, low, near, far, terms):
+def finish_kernel(n_text, scale, first, place, estimate, sums, total, plan, grad_dots, high, low, *refs):
+    *outs, terms = refs
     frames = sums.shape[1]
     mass = sums[0:1, :]
     drift = sums[1:2, :] / mass - estimate[1:2, :] / estimate[0:1, :]
@@ -221,8 +225,28 @@
     width = total.shape[0] // n_text
     for k in range(n_text):
         here = pl.ds(pl.multiple_of((place[0] ^ k) * width, width), width)
-        block = (scale / mass) * (total[here, frames:] - drift * total[here, :frames])
-        (far if k % 2 else near)[k // 2] = block + terms[here, :]
+        block = (scale / mass) * (total[here, frames:] - drift * total[here, :frames]) + terms[here, :]
+        for half, step in enumerate((1, 2)):
+            columns = slice(half * frames // 2, (half + 1) * frames // 2)
+            order = [i for i in range(n_text) if not i & step]
+            outs[2 * half + (k & step > 0)][order.index(k & ~step)] = block[:, columns]
+
+
+def halve_kernel(pairs, *refs):
+    operands, outs = refs[: 2 * pairs], refs[2 * pairs :]
+    start = 0
+    for kept, came in zip(operands[::2], operands[1::2]):
+        columns = slice(start, start + kept.shape[2])
+        for i in range(kept.shape[0]):
+            outs[i % 2][i // 2, :, columns] = kept[i] + came[i]
+        start += kept.shape[2]
+
+
+def halve(*operands):
+    count, width = operands[0].shape[:2]
+    shape = ((count // 2, width, sum(value.shape[2] for value in operands[::2])), jnp.float32)
+    keep, send = call(functools.partial(halve_kernel, len(operands) // 2), "near", operands, [shape, shape])
+    return (keep, send)
 
 
 def shards(n_speech, n_text, speech_feat, text_feat, text_pot, map_grad):
@@ -298,15 +322,6 @@
         outs,
     )
     plans, dots = (plan_early, plan_late), (dots_early, dots_late)
-    right = call(
-        functools.partial(across_kernel, n_text, group),
-        "frames_first",
-        [place, *left],
-        [(left_shape[0][::-1], jnp.bfloat16)] * 2,
-        places=1,
-        before=[sums],
-    )
-
     estimate = sums
     total = []
     step = 1
@@ -322,6 +337,15 @@
                 )
             ]
         if step < n_text:
+            if step == n_text // 2:
+                right = call(
+                    functools.partial(across_kernel, n_text, group),
+                    "frames_first",
+                    [place, *left],
+                    [(left_shape[0][::-1], jnp.bfloat16)] * 2,
+                    places=1,
+                    before=[sums],
+                )
             crossing = swap(sums, "text", step)
             sums = call(add_kernel, "hop", [sums, crossing], ((8, frames), jnp.float32), before=total)
             step *= 2
@@ -339,7 +363,7 @@
             before=before,
         )
 
-    shape = ((n_text // 2, width, frames), jnp.float32)
+    shape = ((n_text // 2, width, frames // 2), jnp.float32)
 
     others = []
     for r in range(2, n_speech, 2):
@@ -347,33 +371,27 @@
         (part,) = text_part(r, "text_far", [term])
         part = part + swap(term, "speech", 1)
         others.append(swap(part, "speech", r))
-    near, far = call(
+    keep_a, send_a, keep_b, send_b = call(
         functools.partial(finish_kernel, n_text, scale, (half - 1) * rows),
         "finish",
         [place, estimate, sums, *total, plans[1], dots[1], across_highs[-1], across_lows[-1]],
-        [shape, shape],
+        [shape] * 4,
         places=1,
         before=[term],
         scratch=[pltpu.VMEM((feats, frames), jnp.float32)],
     )
     crossed = [swap(piece, "speech", 1) for piece in text_part(1, "text_near", [part], 2)]
-    near = call(
-        pieces_kernel,
-        "near",
-        [near, swap(far, "text", 1)],
-        [((width, frames), jnp.float32)] * (n_text // 2),
-        before=crossed,
-    )
-    speech_terms = [near[0]] + [swap(near[k // 2], "text", k) for k in range(2, n_text, 2)]
+    keep_a, send_a = halve(keep_a, swap(send_a, "text", 1))
+    keep_b, send_b = halve(keep_b, swap(send_b, "text", 2))
+    keep, send = halve(keep_a, swap(send_a, "text", 2), keep_b, swap(send_b, "text", 1))
+    step = 4
+    while 2 * step < n_text:
+        keep, send = halve(keep, swap(send, "text", step))
+        step *= 2
     (own,) = text_part(0, "text_near", [part])
     text_grad = call(sum_kernel, "add", [own, *others, *crossed], ((rows, feats), jnp.float32))
-    speech_block = call(add_kernel, "join", speech_terms, ((width, frames), jnp.float32), before=[own])
+    speech_block = call(add_kernel, "join", [keep[0], swap(send[0], "text", step)], ((width, frames), jnp.float32), before=[own])
     return (speech_block.T, text_grad)
-
-
-def pieces_kernel(left, right, *outs):
-    for i, out in enumerate(outs):
-        out[...] = left[i] + right[i]
 
 
 def sum_kernel(*refs):

time: 91.3 us -> 89.1 us (0.976)
  waiting for transfers between devices: 29.9 us -> 25.5 us
  starting transfers between devices: 25.2 us -> 28.4 us
    ppermute x21 -> x22, waiting for transfers between devices: 29.9 us -> 25.5 us  [swap(): return lax.ppermute(value, axis, [(i, i ^ k) for i in range(count)])]
    ppermute x21 -> x22, starting transfers between devices: 25.2 us -> 28.4 us  [swap(): return lax.ppermute(value, axis, [(i, i ^ k) for i in range(count)])]
    pallas_call x27 -> x29, Pallas kernels: 33.7 us -> 32.8 us  [call(): pl.pallas_call(body, in_specs=[IN_SMEM] * places + [IN_VMEM] * (count - p...]
  transfers between devices with their start and end apart: 21 -> 22, of which waited for: 9 -> 11; matrix products, arithmetic and copies ran while one was open for 1% -> 1% of each run, Pallas kernels for 29% -> 29%
where the time goes in v2:
time: 89.1 us; the launch traced here: 88.9 us
  Pallas kernels  32.8 us (37%)
  starting transfers between devices  28.4 us (32%)
  waiting for transfers between devices  25.5 us (29%)
  other arithmetic  1.27 us (1%)
  between operations  0.9 us (1%)
    pallas_call x29, Pallas kernels, call(): pl.pallas_call(body, in_specs=[IN_SMEM] * places + [IN_VMEM] * (count - p...  32.8 us
    ppermute x22, starting transfers between devices, swap(): return lax.ppermute(value, axis, [(i, i ^ k) for i in range(count)])  28.4 us
    ppermute x22, waiting for transfers between devices, swap(): return lax.ppermute(value, axis, [(i, i ^ k) for i in range(count)])  25.5 us
  transfers between devices with their start and end apart: 22, of which 11 were waited for; matrix products, arithmetic and copies ran while one was open for 1% of the time, Pallas kernels for 29%

profile of v2, /device:TPU:0, one launch (start us, length us, event | category | flops | bytes accessed | tf_op | source)
XLA Modules:
  0.0 88.9 jit_solution(17795052796049340205)
XLA Ops:
  0.7 0.5 collective-permute-start
  1.2 2.6 %collective-permute-start.8 = (f32[512,512]{1,0:T(8,128)}, f32[512,512]{1,0:T(8,128)}, u32[]{:S(2)}, u32[]{:S(2)}) collective-permute-start(f32[512,512]{1,0:T(8,128)} %refs_1_.1), channel_id=1, source_target_pairs={{0,16},{8,24},{16,0},{24,8},{1,17},{9,25},{17,1},{25,9},{2,18},{10... | collective-permute-start | bytes 3145736 | tf_op jit(solution)/shard_map/ppermute | solution.py:255
  3.8 1.0 %pad_maximum_fusion.refs_0_ = f32[128,512]{1,0:T(8,128)S(1)} fusion(f32[64,512]{1,0:T(8,128)} %bitcast.9, f32[64,512]{1,0:T(8,128)} %bitcast.10), kind=kLoop, calls=%fused_computation | loop fusion | flops 65536 | bytes 524288 | tf_op jit(solution)/shard_map/concatenate | solution.py:273
  4.8 1.9 %collective-permute-start.2 = (f32[128,512]{1,0:T(8,128)S(1)}, f32[128,512]{1,0:T(8,128)S(1)}, u32[]{:S(2)}, u32[]{:S(2)}) collective-permute-start(f32[128,512]{1,0:T(8,128)S(1)} %copy.9.refs_1_), channel_id=1, source_target_pairs={{0,2},{1,3},{2,0},{3,1},{4,6},{5,7},{6,4},{7,5},{8,10},{9,11},{10,... | collective-permute-start | bytes 786440 | tf_op jit(solution)/shard_map/ppermute | solution.py:255
  6.7 1.5 %collective-permute-start.1 = (f32[128,512]{1,0:T(8,128)S(1)}, f32[128,512]{1,0:T(8,128)S(1)}, u32[]{:S(2)}, u32[]{:S(2)}) collective-permute-start(f32[128,512]{1,0:T(8,128)S(1)} %copy.9.refs_1_), channel_id=1, source_target_pairs={{0,1},{1,0},{2,3},{3,2},{4,5},{5,4},{6,7},{7,6},{8,9},{9,8},{10,11... | collective-permute-start | bytes 786440 | tf_op jit(solution)/shard_map/ppermute | solution.py:255
  8.2 2.6 %collective-permute-start.4 = (f32[128,512]{1,0:T(8,128)S(1)}, f32[128,512]{1,0:T(8,128)S(1)}, u32[]{:S(2)}, u32[]{:S(2)}) collective-permute-start(f32[128,512]{1,0:T(8,128)S(1)} %copy.9.refs_1_), channel_id=1, source_target_pairs={{0,4},{1,5},{2,6},{3,7},{4,0},{5,1},{6,2},{7,3},{8,12},{9,13},{10,... | collective-permute-start | bytes 786440 | tf_op jit(solution)/shard_map/ppermute | solution.py:255
  10.8 0.1 pad_add_fusion.refs_0_
  10.9 0.9 offsets.1.refs_3_.refs_1_.refs_0_
  11.8 0.9 %split.4 = (bf16[512,512]{1,0:T(8,128)(2,1)S(1)}, bf16[512,512]{1,0:T(8,128)(2,1)S(1)}, bf16[512,512]{1,0:T(8,128)(2,1)S(1)}, bf16[512,512]{1,0:T(8,128)(2,1)S(1)}) custom-call(s32[2]{0:T(128)S(1)} %pad_add_fusion.refs_0_, f32[512,512]{1,0:T(8,128)S(1)} %copy-done), custom_call_target="tpu_custom_call" | custom-call | flops 1000000000 | tf_op jit(solution)/shard_map/split/pallas_call | solution.py:55
  12.7 4.9 %collective-permute-done.2.refs_3_.refs_2_ = f32[128,512]{1,0:T(8,128)S(1)} collective-permute-done((f32[128,512]{1,0:T(8,128)S(1)}, f32[128,512]{1,0:T(8,128)S(1)}, u32[]{:S(2)}, u32[]{:S(2)}) %collective-permute-start.2) | collective-permute-done | bytes 262176 | tf_op jit(solution)/shard_map/ppermute | solution.py:255
  17.6 2.6 %collective-permute-start.3 = (f32[128,512]{1,0:T(8,128)S(1)}, f32[128,512]{1,0:T(8,128)S(1)}, u32[]{:S(2)}, u32[]{:S(2)}) collective-permute-start(f32[128,512]{1,0:T(8,128)S(1)} %collective-permute-done.2.refs_3_.refs_2_), channel_id=1, source_target_pairs={{0,1},{1,0},{2,3},{3,2},{4,5},{5,4},{6,7},{7,6},{8,9},{9,8},{10,11... | collective-permute-start | bytes 786440 | tf_op jit(solution)/shard_map/ppermute | solution.py:255
  20.2 0.9 %split.5 = (bf16[512,512]{1,0:T(8,128)(2,1)S(1)}, bf16[512,512]{1,0:T(8,128)(2,1)S(1)}, bf16[512,512]{1,0:T(8,128)(2,1)S(1)}, bf16[512,512]{1,0:T(8,128)(2,1)S(1)}) custom-call(s32[2]{0:T(128)S(1)} %pad_add_fusion.refs_0_, f32[512,512]{1,0:T(8,128)S(1)} %collective-permute-done.refs_1_), custom_call_target="tpu_custom_call" | custom-call | flops 1000000000 | tf_op jit(solution)/shard_map/split/pallas_call | solution.py:55
  21.1 0.0 collective-permute-done.1.refs_2_.refs_1_
  21.1 1.4 %collective-permute-done.4.refs_0_.refs_4_ = f32[128,512]{1,0:T(8,128)S(1)} collective-permute-done((f32[128,512]{1,0:T(8,128)S(1)}, f32[128,512]{1,0:T(8,128)S(1)}, u32[]{:S(2)}, u32[]{:S(2)}) %collective-permute-start.4) | collective-permute-done | bytes 262176 | tf_op jit(solution)/shard_map/ppermute | solution.py:255
  22.6 0.1 collective-permute-start.6
  22.7 0.7 collective-permute-start.5
  23.4 4.0 %collective-permute-done.3.refs_4_ = f32[128,512]{1,0:T(8,128)S(1)} collective-permute-done((f32[128,512]{1,0:T(8,128)S(1)}, f32[128,512]{1,0:T(8,128)S(1)}, u32[]{:S(2)}, u32[]{:S(2)}) %collective-permute-start.3) | collective-permute-done | bytes 262176 | tf_op jit(solution)/shard_map/ppermute | solution.py:255
  27.4 2.5 %plan_part.1 = (f32[512,1024]{1,0:T(8,128)S(1)}, f32[512,1024]{1,0:T(8,128)S(1)}, bf16[256,1024]{1,0:T(8,128)(2,1)S(1)}, bf16[256,1024]{1,0:T(8,128)(2,1)S(1)}) custom-call(s32[2]{0:T(128)S(1)} %pad_add_fusion.refs_0_, f32[128,512]{1,0:T(8,128)S(1)} %copy.9.refs_1_, f32[128,512]{1,0:T(8,128)S(1)} %collective-permute-done.1.refs_2_.refs_1_, ...), custom_call_target="tpu_custom_call" | custom-call | flops 1000000000 | tf_op jit(solution)/shard_map/plan_part/pallas_call | solution.py:55
  29.9 0.0 collective-permute-done.6.refs_0_.refs_6_
  29.9 2.1 %collective-permute-start.7 = (f32[128,512]{1,0:T(8,128)S(1)}, f32[128,512]{1,0:T(8,128)S(1)}, u32[]{:S(2)}, u32[]{:S(2)}) collective-permute-start(f32[128,512]{1,0:T(8,128)S(1)} %copy.11), channel_id=1, source_target_pairs={{0,1},{1,0},{2,3},{3,2},{4,5},{5,4},{6,7},{7,6},{8,9},{9,8},{10,11... | collective-permute-start | bytes 786440 | tf_op jit(solution)/shard_map/ppermute | solution.py:255
  32.0 0.0 collective-permute-done.8.refs_1_
  32.0 0.0 collective-permute-start.9
  32.0 1.6 %split.6 = (bf16[512,512]{1,0:T(8,128)(2,1)S(1)}, bf16[512,512]{1,0:T(8,128)(2,1)S(1)}, bf16[512,512]{1,0:T(8,128)(2,1)S(1)}, bf16[512,512]{1,0:T(8,128)(2,1)S(1)}) custom-call(s32[2]{0:T(128)S(1)} %pad_add_fusion.refs_0_, f32[512,512]{1,0:T(8,128)} %collective-permute-done.8.refs_1_), custom_call_target="tpu_custom_call" | custom-call | flops 1000000000 | tf_op jit(solution)/shard_map/split/pallas_call | solution.py:55
  33.6 1.0 %plan_more.1.refs_4_ = f32[512,1024]{1,0:T(8,128)S(1)} custom-call(bf16[256,1024]{1,0:T(8,128)(2,1)S(1)} %get-tuple-element.48.refs_1_.refs_2_.refs_0_, bf16[256,1024]{1,0:T(8,128)(2,1)S(1)} %get-tuple-element.49.refs_3_.refs_1_, bf16[512,512]{1,0:T(8,128)(2,1)S(1)} %get-tuple-element.55.refs_2_.refs_5_, bf16[512,512]{1,0:T(8,128)(2,1)S(1)} %get-tuple-element.56.refs_3_.refs_7_), custom_call_target="tpu_custom_call" | custom-call | flops 1000000000 | tf_op jit(solution)/shard_map/plan_more/pallas_call | solution.py:55
  34.6 0.0 collective-permute-done.5.refs_5_
  34.6 2.7 %collective-permute-done.7.refs_7_ = f32[128,512]{1,0:T(8,128)S(1)} collective-permute-done((f32[128,512]{1,0:T(8,128)S(1)}, f32[128,512]{1,0:T(8,128)S(1)}, u32[]{:S(2)}, u32[]{:S(2)}) %collective-permute-start.7) | collective-permute-done | bytes 262176 | tf_op jit(solution)/shard_map/ppermute | solution.py:255
  37.3 2.9 %plan_early.1 = (f32[1024,512]{1,0:T(8,128)S(1)}, f32[1024,512]{1,0:T(8,128)S(1)}, f32[8,512]{1,0:T(8,128)S(1)}, bf16[512,1024]{1,0:T(8,128)(2,1)S(1)}, bf16[512,1024]{1,0:T(8,128)(2,1)S(1)}) custom-call(s32[2]{0:T(128)S(1)} %pad_add_fusion.refs_0_, f32[2048,128]{1,0:T(8,128)S(1)} %offsets.1.refs_3_.refs_1_.refs_0_, ...), custom_call_target="tpu_custom_call" | custom-call | flops 99999997952 | tf_op jit(solution)/shard_map/plan_early/pallas_call | solution.py:55
  40.3 0.0 collective-permute-done.9.refs_1_
  40.3 0.9 %split.7 = (bf16[512,512]{1,0:T(8,128)(2,1)S(1)}, bf16[512,512]{1,0:T(8,128)(2,1)S(1)}, bf16[512,512]{1,0:T(8,128)(2,1)S(1)}, bf16[512,512]{1,0:T(8,128)(2,1)S(1)}) custom-call(s32[2]{0:T(128)S(1)} %pad_add_fusion.refs_0_, f32[512,512]{1,0:T(8,128)S(1)} %collective-permute-done.9.refs_1_), custom_call_target="tpu_custom_call" | custom-call | flops 1000000000 | tf_op jit(solution)/shard_map/split/pallas_call | solution.py:55
  41.2 2.8 %plan_late.1 = (f32[1024,512]{1,0:T(8,128)S(1)}, f32[1024,512]{1,0:T(8,128)S(1)}, f32[8,512]{1,0:T(8,128)S(1)}) custom-call(f32[2048,128]{1,0:T(8,128)S(1)} %offsets.1.refs_3_.refs_1_.refs_0_, f32[8,512]{1,0:T(8,128)S(1)} %get-tuple-element.52.refs_1_, bf16[512,1024]{1,0:T(8,128)(2,1)S(1)} %get-tuple-element.53.refs_2_.refs_1_, ...), custom_call_target="tpu_custom_call" | custom-call | flops 3000000000 | tf_op jit(solution)/shard_map/plan_late/pallas_call | solution.py:55
  44.0 1.8 %collective-permute-start.10 = (f32[8,512]{1,0:T(8,128)S(1)}, f32[8,512]{1,0:T(8,128)S(1)}, u32[]{:S(2)}, u32[]{:S(2)}) collective-permute-start(f32[8,512]{1,0:T(8,128)S(1)} %get-tuple-element.59.refs_0_.refs_5_.refs_1_), channel_id=1, source_target_pairs={{0,1},{1,0},{2,3},{3,2},{4,5},{5,4},{6,7},{7,6},{8,9},{9,8},{10,11... | collective-permute-start | bytes 49160 | tf_op jit(solution)/shard_map/ppermute | solution.py:255
  45.8 1.8 %moments.3.refs_2_.refs_5_ = f32[512,1024]{1,0:T(8,128)S(1)} custom-call(f32[8,512]{1,0:T(8,128)S(1)} %get-tuple-element.59.refs_0_.refs_5_.refs_1_, f32[1024,512]{1,0:T(8,128)S(1)} %get-tuple-element.60.refs_1_, f32[1024,512]{1,0:T(8,128)S(1)} %get-tuple-element.61.refs_2_, bf16[512,512]{1,0:T(8,128)(2,1)S(1)} %get-tuple-element.62.refs_3_, ...), custom_call_target="tpu_custom_call" | custom-call | flops 3000000000 | tf_op jit(solution)/shard_map/moments/pallas_call | solution.py:55
  47.7 0.1 collective-permute-done.10.refs_1_
  47.8 0.0 collective-permute-start.11
  47.8 1.9 %moments.4.refs_2_.refs_5_ = f32[512,1024]{1,0:T(8,128)S(1)} custom-call(f32[8,512]{1,0:T(8,128)S(1)} %get-tuple-element.59.refs_0_.refs_5_.refs_1_, f32[1024,512]{1,0:T(8,128)S(1)} %get-tuple-element.60.refs_1_, f32[1024,512]{1,0:T(8,128)S(1)} %get-tuple-element.61.refs_2_, bf16[512,512]{1,0:T(8,128)(2,1)S(1)} %get-tuple-element.64.refs_3_, ...), custom_call_target="tpu_custom_call" | custom-call | flops 3000000000 | tf_op jit(solution)/shard_map/moments/pallas_call | solution.py:55
  49.7 1.9 %collective-permute-done.11.refs_1_ = f32[8,512]{1,0:T(8,128)S(1)} collective-permute-done((f32[8,512]{1,0:T(8,128)S(1)}, f32[8,512]{1,0:T(8,128)S(1)}, u32[]{:S(2)}, u32[]{:S(2)}) %collective-permute-start.11) | collective-permute-done | bytes 16416 | tf_op jit(solution)/shard_map/ppermute | solution.py:255
  51.6 1.3 %collective-permute-start.12 = (f32[8,512]{1,0:T(8,128)S(1)}, f32[8,512]{1,0:T(8,128)S(1)}, u32[]{:S(2)}, u32[]{:S(2)}) collective-permute-start(f32[8,512]{1,0:T(8,128)S(1)} %hop.4.refs_6_.refs_0_.refs_3_), channel_id=1, source_target_pairs={{0,4},{1,5},{2,6},{3,7},{4,0},{5,1},{6,2},{7,3},{8,12},{9,13},{10,... | collective-permute-start | bytes 49160 | tf_op jit(solution)/shard_map/ppermute | solution.py:255
  52.9 2.1 %moments.5.refs_2_.refs_3_ = f32[512,1024]{1,0:T(8,128)S(1)} custom-call(f32[8,512]{1,0:T(8,128)S(1)} %get-tuple-element.59.refs_0_.refs_5_.refs_1_, f32[1024,512]{1,0:T(8,128)S(1)} %get-tuple-element.66.refs_1_.refs_4_, f32[1024,512]{1,0:T(8,128)S(1)} %get-tuple-element.67.refs_2_.refs_5_, bf16[512,512]{1,0:T(8,128)(2,1)S(1)} %get-tuple-element.68.refs_3_, ...), custom_call_target="tpu_custom_call" | custom-call | flops 3000000000 | tf_op jit(solution)/shard_map/moments/pallas_call | solution.py:55
  54.9 1.5 %frames_first.1 = (bf16[1024,512]{1,0:T(8,128)(2,1)S(1)}, bf16[1024,512]{1,0:T(8,128)(2,1)S(1)}) custom-call(s32[2]{0:T(128)S(1)} %pad_add_fusion.refs_0_, bf16[512,1024]{1,0:T(8,128)(2,1)S(1)} %get-tuple-element.53.refs_2_.refs_1_, bf16[512,1024]{1,0:T(8,128)(2,1)S(1)} %get-tuple-element.54.refs_3_.refs_2_, f32[8,512]{1,0:T(8,128)S(1)} %hop.4.refs_6_.refs_0_.refs_3_), custom_call_target="tpu_custom_call" | custom-call | flops 1000000000 | tf_op jit(solution)/shard_map/frames_first/pallas_call | solution.py:55
  56.5 1.8 %text_far.2.refs_8_.refs_5_ = f32[512,512]{1,0:T(8,128)S(1)} custom-call(f32[8,512]{1,0:T(8,128)S(1)} %hop.5.refs_0_.refs_2_, f32[1024,512]{1,0:T(8,128)S(1)} %get-tuple-element.66.refs_1_.refs_4_, f32[1024,512]{1,0:T(8,128)S(1)} %get-tuple-element.67.refs_2_.refs_5_, bf16[1024,512]{1,0:T(8,128)(2,1)S(1)} %get-tuple-element.72.refs_3_, ...), custom_call_target="tpu_custom_call" | custom-call | flops 3000000000 | tf_op jit(solution)/shard_map/text_far/pallas_call | solution.py:55
  58.3 0.1 collective-permute-start.18
  58.4 1.8 %text_far.3 = f32[512,512]{1,0:T(8,128)S(1)} custom-call(f32[8,512]{1,0:T(8,128)S(1)} %hop.5.refs_0_.refs_2_, f32[1024,512]{1,0:T(8,128)S(1)} %get-tuple-element.66.refs_1_.refs_4_, f32[1024,512]{1,0:T(8,128)S(1)} %get-tuple-element.67.refs_2_.refs_5_, bf16[1024,512]{1,0:T(8,128)(2,1)S(1)} %get-tuple-element.72.refs_3_, ...), custom_call_target="tpu_custom_call" | custom-call | flops 3000000000 | tf_op jit(solution)/shard_map/text_far/pallas_call | solution.py:55
  60.2 0.8 collective-permute-done.18
  61.0 0.2 add.4.refs_5_
  61.2 1.6 %collective-permute-start.19 = (f32[512,512]{1,0:T(8,128)S(1)}, f32[512,512]{1,0:T(8,128)S(1)}, u32[]{:S(2)}, u32[]{:S(2)}) collective-permute-start(f32[512,512]{1,0:T(8,128)S(1)} %add.4.refs_5_), channel_id=1, source_target_pairs={{0,16},{8,24},{16,0},{24,8},{1,17},{9,25},{17,1},{25,9},{2,18},{10... | collective-permute-start | bytes 3145736 | tf_op jit(solution)/shard_map/ppermute | solution.py:255
  62.8 1.8 %finish.1 = (f32[4,64,256]{2,1,0:T(8,128)S(1)}, f32[4,64,256]{2,1,0:T(8,128)S(1)}, f32[4,64,256]{2,1,0:T(8,128)S(1)}, f32[4,64,256]{2,1,0:T(8,128)S(1)}) custom-call(s32[2]{0:T(128)S(1)} %pad_add_fusion.refs_0_, f32[8,512]{1,0:T(8,128)S(1)} %get-tuple-element.59.refs_0_.refs_5_.refs_1_, f32[8,512]{1,0:T(8,128)S(1)} %hop.5.refs_0_.refs_2_, ...), custom_call_target="tpu_custom_call" | custom-call | flops 1000000000 | tf_op jit(solution)/shard_map/finish/pallas_call | solution.py:55
  64.6 1.8 %collective-permute-start.13 = (f32[4,64,256]{2,1,0:T(8,128)S(1)}, f32[4,64,256]{2,1,0:T(8,128)S(1)}, u32[]{:S(2)}, u32[]{:S(2)}) collective-permute-start(f32[4,64,256]{2,1,0:T(8,128)S(1)} %get-tuple-element.75), channel_id=1, source_target_pairs={{0,1},{1,0},{2,3},{3,2},{4,5},{5,4},{6,7},{7,6},{8,9},{9,8},{10,11... | collective-permute-start | bytes 786440 | tf_op jit(solution)/shard_map/ppermute | solution.py:255
  66.4 1.8 %collective-permute-start.15 = (f32[4,64,256]{2,1,0:T(8,128)S(1)}, f32[4,64,256]{2,1,0:T(8,128)S(1)}, u32[]{:S(2)}, u32[]{:S(2)}) collective-permute-start(f32[4,64,256]{2,1,0:T(8,128)S(1)} %get-tuple-element.79), channel_id=1, source_target_pairs={{0,2},{1,3},{2,0},{3,1},{4,6},{5,7},{6,4},{7,5},{8,10},{9,11},{10,... | collective-permute-start | bytes 786440 | tf_op jit(solution)/shard_map/ppermute | solution.py:255
  68.2 1.8 %text_near.3 = (f32[256,512]{1,0:T(8,128)S(1)}, f32[256,512]{1,0:T(8,128)S(1)}) custom-call(f32[8,512]{1,0:T(8,128)S(1)} %hop.5.refs_0_.refs_2_, f32[1024,512]{1,0:T(8,128)S(1)} %get-tuple-element.60.refs_1_, f32[1024,512]{1,0:T(8,128)S(1)} %get-tuple-element.61.refs_2_, bf16[1024,512]{1,0:T(8,128)(2,1)S(1)} %get-tuple-element.72.refs_3_, ...), custom_call_target="tpu_custom_call" | custom-call | flops 3000000000 | tf_op jit(solution)/shard_map/text_near/pallas_call | solution.py:55
  70.0 0.1 collective-permute-start.20
  70.1 0.5 collective-permute-start.21
  70.6 2.2 %collective-permute-done.13.refs_1_ = f32[4,64,256]{2,1,0:T(8,128)S(1)} collective-permute-done((f32[4,64,256]{2,1,0:T(8,128)S(1)}, f32[4,64,256]{2,1,0:T(8,128)S(1)}, u32[]{:S(2)}, u32[]{:S(2)}) %collective-permute-start.13) | collective-permute-done | bytes 262176 | tf_op jit(solution)/shard_map/ppermute | solution.py:255
  72.8 1.8 %collective-permute-start.14 = (f32[2,64,256]{2,1,0:T(8,128)S(1)}, f32[2,64,256]{2,1,0:T(8,128)S(1)}, u32[]{:S(2)}, u32[]{:S(2)}) collective-permute-start(f32[2,64,256]{2,1,0:T(8,128)S(1)} %get-tuple-element.77), channel_id=1, source_target_pairs={{0,2},{1,3},{2,0},{3,1},{4,6},{5,7},{6,4},{7,5},{8,10},{9,11},{10,... | collective-permute-start | bytes 393224 | tf_op jit(solution)/shard_map/ppermute | solution.py:255
  74.7 1.8 %collective-permute-start.16 = (f32[2,64,256]{2,1,0:T(8,128)S(1)}, f32[2,64,256]{2,1,0:T(8,128)S(1)}, u32[]{:S(2)}, u32[]{:S(2)}) collective-permute-start(f32[2,64,256]{2,1,0:T(8,128)S(1)} %get-tuple-element.81), channel_id=1, source_target_pairs={{0,1},{1,0},{2,3},{3,2},{4,5},{5,4},{6,7},{7,6},{8,9},{9,8},{10,11... | collective-permute-start | bytes 393224 | tf_op jit(solution)/shard_map/ppermute | solution.py:255
  76.5 1.4 %collective-permute-done.14.refs_1_ = f32[2,64,256]{2,1,0:T(8,128)S(1)} collective-permute-done((f32[2,64,256]{2,1,0:T(8,128)S(1)}, f32[2,64,256]{2,1,0:T(8,128)S(1)}, u32[]{:S(2)}, u32[]{:S(2)}) %collective-permute-start.14) | collective-permute-done | bytes 131104 | tf_op jit(solution)/shard_map/ppermute | solution.py:255
  77.8 1.9 %collective-permute-done.16.refs_3_ = f32[2,64,256]{2,1,0:T(8,128)S(1)} collective-permute-done((f32[2,64,256]{2,1,0:T(8,128)S(1)}, f32[2,64,256]{2,1,0:T(8,128)S(1)}, u32[]{:S(2)}, u32[]{:S(2)}) %collective-permute-start.16) | collective-permute-done | bytes 131104 | tf_op jit(solution)/shard_map/ppermute | solution.py:255
  79.7 1.3 %collective-permute-start.17 = (f32[64,512]{1,0:T(8,128)S(1)}, f32[64,512]{1,0:T(8,128)S(1)}, u32[]{:S(2)}, u32[]{:S(2)}) collective-permute-start(f32[64,512]{1,0:T(8,128)S(1)} %bitcast.8), channel_id=1, source_target_pairs={{0,4},{1,5},{2,6},{3,7},{4,0},{5,1},{6,2},{7,3},{8,12},{9,13},{10,... | collective-permute-start | bytes 393224 | tf_op jit(solution)/shard_map/ppermute | solution.py:255
  81.1 1.8 %text_near.2.refs_2_.refs_0_ = f32[512,512]{1,0:T(8,128)S(1)} custom-call(f32[8,512]{1,0:T(8,128)S(1)} %hop.5.refs_0_.refs_2_, f32[1024,512]{1,0:T(8,128)S(1)} %get-tuple-element.60.refs_1_, f32[1024,512]{1,0:T(8,128)S(1)} %get-tuple-element.61.refs_2_, bf16[1024,512]{1,0:T(8,128)(2,1)S(1)} %get-tuple-element.72.refs_3_, ...), custom_call_target="tpu_custom_call" | custom-call | flops 3000000000 | tf_op jit(solution)/shard_map/text_near/pallas_call | solution.py:55
  82.9 4.2 %collective-permute-done.17.refs_1_ = f32[64,512]{1,0:T(8,128)S(1)} collective-permute-done((f32[64,512]{1,0:T(8,128)S(1)}, f32[64,512]{1,0:T(8,128)S(1)}, u32[]{:S(2)}, u32[]{:S(2)}) %collective-permute-start.17) | collective-permute-done | bytes 131104 | tf_op jit(solution)/shard_map/ppermute | solution.py:255
  87.1 0.7 join.1
  87.8 0.0 collective-permute-done.20.refs_2_
  87.8 0.0 collective-permute-done.21.refs_3_
  87.8 0.0 collective-permute-done.19.refs_1_
  87.8 1.2 %add.7 = f32[512,512]{1,0:T(8,128)} custom-call(f32[512,512]{1,0:T(8,128)S(1)} %text_near.2.refs_2_.refs_0_, f32[512,512]{1,0:T(8,128)S(1)} %collective-permute-done.19.refs_1_, f32[256,512]{1,0:T(8,128)S(1)} %collective-permute-done.20.refs_2_, f32[256,512]{1,0:T(8,128)S(1)} %collective-permute-done.21.refs_3_), custom_call_target="tpu_custom_call" | custom-call | flops 99999997952 | tf_op jit(solution)/shard_map/add/pallas_call | solution.py:55
  (17 shorter events, 0.2 us)
Async XLA Ops:
  0.6 11.1 %copy-start = (f32[512,512]{1,0:T(8,128)S(1)}, f32[512,512]{1,0:T(8,128)}, u32[]{:S(2)}) copy-start(f32[512,512]{1,0:T(8,128)} %refs_1_.1) | copy-start | bytes 3145732
  0.6 6.1 %copy-start.1 = (f32[2048]{0:T(1024)S(1)}, f32[2048]{0:T(1024)}, u32[]{:S(2)}) copy-start(f32[2048]{0:T(1024)} %param.6) | copy-start | bytes 24580
  0.7 4.1 %collective-permute-start = (f32[512,512]{1,0:T(8,128)}, f32[512,512]{1,0:T(8,128)S(1)}, u32[]{:S(2)}, u32[]{:S(2)}) collective-permute-start(f32[512,512]{1,0:T(8,128)} %refs_1_.1), channel_id=1, source_target_pairs={{0,8},{8,0},{16,24},{24,16},{1,9},{9,1},{17,25},{25,17},{2,10},{10... | collective-permute-start | bytes 3145736 | tf_op jit(solution)/shard_map/ppermute | solution.py:255
  1.2 30.9 %collective-permute-start.8 = (f32[512,512]{1,0:T(8,128)}, f32[512,512]{1,0:T(8,128)}, u32[]{:S(2)}, u32[]{:S(2)}) collective-permute-start(f32[512,512]{1,0:T(8,128)} %refs_1_.1), channel_id=1, source_target_pairs={{0,16},{8,24},{16,0},{24,8},{1,17},{9,25},{17,1},{25,9},{2,18},{10... | collective-permute-start | bytes 3145736 | tf_op jit(solution)/shard_map/ppermute | solution.py:255
  4.8 12.8 %collective-permute-start.2 = (f32[128,512]{1,0:T(8,128)S(1)}, f32[128,512]{1,0:T(8,128)S(1)}, u32[]{:S(2)}, u32[]{:S(2)}) collective-permute-start(f32[128,512]{1,0:T(8,128)S(1)} %copy.9.refs_1_), channel_id=1, source_target_pairs={{0,2},{1,3},{2,0},{3,1},{4,6},{5,7},{6,4},{7,5},{8,10},{9,11},{10,... | collective-permute-start | bytes 786440 | tf_op jit(solution)/shard_map/ppermute | solution.py:255
  6.7 14.4 %collective-permute-start.1 = (f32[128,512]{1,0:T(8,128)S(1)}, f32[128,512]{1,0:T(8,128)S(1)}, u32[]{:S(2)}, u32[]{:S(2)}) collective-permute-start(f32[128,512]{1,0:T(8,128)S(1)} %copy.9.refs_1_), channel_id=1, source_target_pairs={{0,1},{1,0},{2,3},{3,2},{4,5},{5,4},{6,7},{7,6},{8,9},{9,8},{10,11... | collective-permute-start | bytes 786440 | tf_op jit(solution)/shard_map/ppermute | solution.py:255
  8.2 14.4 %collective-permute-start.4 = (f32[128,512]{1,0:T(8,128)S(1)}, f32[128,512]{1,0:T(8,128)S(1)}, u32[]{:S(2)}, u32[]{:S(2)}) collective-permute-start(f32[128,512]{1,0:T(8,128)S(1)} %copy.9.refs_1_), channel_id=1, source_target_pairs={{0,4},{1,5},{2,6},{3,7},{4,0},{5,1},{6,2},{7,3},{8,12},{9,13},{10,... | collective-permute-start | bytes 786440 | tf_op jit(solution)/shard_map/ppermute | solution.py:255
  17.6 9.8 %collective-permute-start.3 = (f32[128,512]{1,0:T(8,128)S(1)}, f32[128,512]{1,0:T(8,128)S(1)}, u32[]{:S(2)}, u32[]{:S(2)}) collective-permute-start(f32[128,512]{1,0:T(8,128)S(1)} %collective-permute-done.2.refs_3_.refs_2_), channel_id=1, source_target_pairs={{0,1},{1,0},{2,3},{3,2},{4,5},{5,4},{6,7},{7,6},{8,9},{9,8},{10,11... | collective-permute-start | bytes 786440 | tf_op jit(solution)/shard_map/ppermute | solution.py:255
  22.6 7.3 %collective-permute-start.6 = (f32[128,512]{1,0:T(8,128)S(1)}, f32[128,512]{1,0:T(8,128)S(1)}, u32[]{:S(2)}, u32[]{:S(2)}) collective-permute-start(f32[128,512]{1,0:T(8,128)S(1)} %copy.10), channel_id=1, source_target_pairs={{0,2},{1,3},{2,0},{3,1},{4,6},{5,7},{6,4},{7,5},{8,10},{9,11},{10,... | collective-permute-start | bytes 786440 | tf_op jit(solution)/shard_map/ppermute | solution.py:255
  22.7 12.0 %collective-permute-start.5 = (f32[128,512]{1,0:T(8,128)S(1)}, f32[128,512]{1,0:T(8,128)S(1)}, u32[]{:S(2)}, u32[]{:S(2)}) collective-permute-start(f32[128,512]{1,0:T(8,128)S(1)} %collective-permute-done.4.refs_0_.refs_4_), channel_id=1, source_target_pairs={{0,1},{1,0},{2,3},{3,2},{4,5},{5,4},{6,7},{7,6},{8,9},{9,8},{10,11... | collective-permute-start | bytes 786440 | tf_op jit(solution)/shard_map/ppermute | solution.py:255
  29.9 7.4 %collective-permute-start.7 = (f32[128,512]{1,0:T(8,128)S(1)}, f32[128,512]{1,0:T(8,128)S(1)}, u32[]{:S(2)}, u32[]{:S(2)}) collective-permute-start(f32[128,512]{1,0:T(8,128)S(1)} %copy.11), channel_id=1, source_target_pairs={{0,1},{1,0},{2,3},{3,2},{4,5},{5,4},{6,7},{7,6},{8,9},{9,8},{10,11... | collective-permute-start | bytes 786440 | tf_op jit(solution)/shard_map/ppermute | solution.py:255
  32.0 8.2 %collective-permute-start.9 = (f32[512,512]{1,0:T(8,128)}, f32[512,512]{1,0:T(8,128)S(1)}, u32[]{:S(2)}, u32[]{:S(2)}) collective-permute-start(f32[512,512]{1,0:T(8,128)} %collective-permute-done.8.refs_1_), channel_id=1, source_target_pairs={{0,8},{8,0},{16,24},{24,16},{1,9},{9,1},{17,25},{25,17},{2,10},{10... | collective-permute-start | bytes 3145736 | tf_op jit(solution)/shard_map/ppermute | solution.py:255
  44.0 3.8 %collective-permute-start.10 = (f32[8,512]{1,0:T(8,128)S(1)}, f32[8,512]{1,0:T(8,128)S(1)}, u32[]{:S(2)}, u32[]{:S(2)}) collective-permute-start(f32[8,512]{1,0:T(8,128)S(1)} %get-tuple-element.59.refs_0_.refs_5_.refs_1_), channel_id=1, source_target_pairs={{0,1},{1,0},{2,3},{3,2},{4,5},{5,4},{6,7},{7,6},{8,9},{9,8},{10,11... | collective-permute-start | bytes 49160 | tf_op jit(solution)/shard_map/ppermute | solution.py:255
  47.8 3.8 %collective-permute-start.11 = (f32[8,512]{1,0:T(8,128)S(1)}, f32[8,512]{1,0:T(8,128)S(1)}, u32[]{:S(2)}, u32[]{:S(2)}) collective-permute-start(f32[8,512]{1,0:T(8,128)S(1)} %hop.3.refs_6_.refs_0_), channel_id=1, source_target_pairs={{0,2},{1,3},{2,0},{3,1},{4,6},{5,7},{6,4},{7,5},{8,10},{9,11},{10,... | collective-permute-start | bytes 49160 | tf_op jit(solution)/shard_map/ppermute | solution.py:255
  51.6 4.9 %collective-permute-start.12 = (f32[8,512]{1,0:T(8,128)S(1)}, f32[8,512]{1,0:T(8,128)S(1)}, u32[]{:S(2)}, u32[]{:S(2)}) collective-permute-start(f32[8,512]{1,0:T(8,128)S(1)} %hop.4.refs_6_.refs_0_.refs_3_), channel_id=1, source_target_pairs={{0,4},{1,5},{2,6},{3,7},{4,0},{5,1},{6,2},{7,3},{8,12},{9,13},{10,... | collective-permute-start | bytes 49160 | tf_op jit(solution)/shard_map/ppermute | solution.py:255
  58.3 2.7 %collective-permute-start.18 = (f32[512,512]{1,0:T(8,128)S(1)}, f32[512,512]{1,0:T(8,128)S(1)}, u32[]{:S(2)}, u32[]{:S(2)}) collective-permute-start(f32[512,512]{1,0:T(8,128)S(1)} %text_far.2.refs_8_.refs_5_), channel_id=1, source_target_pairs={{0,8},{8,0},{16,24},{24,16},{1,9},{9,1},{17,25},{25,17},{2,10},{10... | collective-permute-start | bytes 3145736 | tf_op jit(solution)/shard_map/ppermute | solution.py:255
  61.2 26.5 %collective-permute-start.19 = (f32[512,512]{1,0:T(8,128)S(1)}, f32[512,512]{1,0:T(8,128)S(1)}, u32[]{:S(2)}, u32[]{:S(2)}) collective-permute-start(f32[512,512]{1,0:T(8,128)S(1)} %add.4.refs_5_), channel_id=1, source_target_pairs={{0,16},{8,24},{16,0},{24,8},{1,17},{9,25},{17,1},{25,9},{2,18},{10... | collective-permute-start | bytes 3145736 | tf_op jit(solution)/shard_map/ppermute | solution.py:255
  64.6 8.1 %collective-permute-start.13 = (f32[4,64,256]{2,1,0:T(8,128)S(1)}, f32[4,64,256]{2,1,0:T(8,128)S(1)}, u32[]{:S(2)}, u32[]{:S(2)}) collective-permute-start(f32[4,64,256]{2,1,0:T(8,128)S(1)} %get-tuple-element.75), channel_id=1, source_target_pairs={{0,1},{1,0},{2,3},{3,2},{4,5},{5,4},{6,7},{7,6},{8,9},{9,8},{10,11... | collective-permute-start | bytes 786440 | tf_op jit(solution)/shard_map/ppermute | solution.py:255
  66.4 8.2 %collective-permute-start.15 = (f32[4,64,256]{2,1,0:T(8,128)S(1)}, f32[4,64,256]{2,1,0:T(8,128)S(1)}, u32[]{:S(2)}, u32[]{:S(2)}) collective-permute-start(f32[4,64,256]{2,1,0:T(8,128)S(1)} %get-tuple-element.79), channel_id=1, source_target_pairs={{0,2},{1,3},{2,0},{3,1},{4,6},{5,7},{6,4},{7,5},{8,10},{9,11},{10,... | collective-permute-start | bytes 786440 | tf_op jit(solution)/shard_map/ppermute | solution.py:255
  70.0 17.7 %collective-permute-start.20 = (f32[256,512]{1,0:T(8,128)S(1)}, f32[256,512]{1,0:T(8,128)S(1)}, u32[]{:S(2)}, u32[]{:S(2)}) collective-permute-start(f32[256,512]{1,0:T(8,128)S(1)} %get-tuple-element.84), channel_id=1, source_target_pairs={{0,8},{8,0},{16,24},{24,16},{1,9},{9,1},{17,25},{25,17},{2,10},{10... | collective-permute-start | bytes 1572872 | tf_op jit(solution)/shard_map/ppermute | solution.py:255
  70.1 17.7 %collective-permute-start.21 = (f32[256,512]{1,0:T(8,128)S(1)}, f32[256,512]{1,0:T(8,128)S(1)}, u32[]{:S(2)}, u32[]{:S(2)}) collective-permute-start(f32[256,512]{1,0:T(8,128)S(1)} %get-tuple-element.85), channel_id=1, source_target_pairs={{0,8},{8,0},{16,24},{24,16},{1,9},{9,1},{17,25},{25,17},{2,10},{10... | collective-permute-start | bytes 1572872 | tf_op jit(solution)/shard_map/ppermute | solution.py:255
  72.8 5.0 %collective-permute-start.14 = (f32[2,64,256]{2,1,0:T(8,128)S(1)}, f32[2,64,256]{2,1,0:T(8,128)S(1)}, u32[]{:S(2)}, u32[]{:S(2)}) collective-permute-start(f32[2,64,256]{2,1,0:T(8,128)S(1)} %get-tuple-element.77), channel_id=1, source_target_pairs={{0,2},{1,3},{2,0},{3,1},{4,6},{5,7},{6,4},{7,5},{8,10},{9,11},{10,... | collective-permute-start | bytes 393224 | tf_op jit(solution)/shard_map/ppermute | solution.py:255
  74.7 5.0 %collective-permute-start.16 = (f32[2,64,256]{2,1,0:T(8,128)S(1)}, f32[2,64,256]{2,1,0:T(8,128)S(1)}, u32[]{:S(2)}, u32[]{:S(2)}) collective-permute-start(f32[2,64,256]{2,1,0:T(8,128)S(1)} %get-tuple-element.81), channel_id=1, source_target_pairs={{0,1},{1,0},{2,3},{3,2},{4,5},{5,4},{6,7},{7,6},{8,9},{9,8},{10,11... | collective-permute-start | bytes 393224 | tf_op jit(solution)/shard_map/ppermute | solution.py:255
  79.7 7.3 %collective-permute-start.17 = (f32[64,512]{1,0:T(8,128)S(1)}, f32[64,512]{1,0:T(8,128)S(1)}, u32[]{:S(2)}, u32[]{:S(2)}) collective-permute-start(f32[64,512]{1,0:T(8,128)S(1)} %bitcast.8), channel_id=1, source_target_pairs={{0,4},{1,5},{2,6},{3,7},{4,0},{5,1},{6,2},{7,3},{8,12},{9,13},{10,... | collective-permute-start | bytes 393224 | tf_op jit(solution)/shard_map/ppermute | solution.py:255

commit v3 on v2

--- a/solution.py
+++ b/solution.py
@@ -15,9 +15,6 @@
     "plan_part": SHORT,
     "plan_more": SHORT,
     "moments": 3 * SHORT,
-    "text_far": 3 * SHORT,
-    "text_near": 3 * SHORT,
-    "finish": SHORT,
     "frames_first": SHORT,
     "split": SHORT,
     "offsets": SHORT // 10,
@@ -194,13 +191,16 @@
     return (shared, weighted)
 
 
-def text_kernel(scale, first, sums, plan, grad_dots, right_high, right_low, *outs):
+def text_kernel(scale, first, pieces, sums, plan, grad_dots, right_high, right_low, *refs):
+    came, outs = refs[:pieces], refs[pieces:]
     rows = len(outs) * outs[0].shape[0]
     here = slice(first, first + rows)
     shared, weighted = weights(sums, plan[here, :], grad_dots[here, :], scale)
     shared, weighted = halves(shared), halves(weighted)
     left = [jnp.concatenate([w, s], axis=1) for w, s in zip(weighted, shared)]
     terms = dot3(left, (right_high[...], right_low[...]))
+    if came:
+        terms = terms + jnp.concatenate([piece[...] for piece in came], axis=0)
     for i, out in enumerate(outs):
         out[...] = terms[i * out.shape[0] : (i + 1) * out.shape[0], :]
 
@@ -214,14 +214,17 @@
     out[...] = total[0][...] + term if total else term
 
 
-def finish_kernel(n_text, scale, first, place, estimate, sums, total, plan, grad_dots, high, low, *refs):
-    *outs, terms = refs
+def finish_kernel(n_text, scale, firsts, place, estimate, sums, total, plan, grad_dots, *refs):
+    blocks, outs, terms = refs[: 2 * len(firsts)], refs[2 * len(firsts) : -1], refs[-1]
     frames = sums.shape[1]
     mass = sums[0:1, :]
     drift = sums[1:2, :] / mass - estimate[1:2, :] / estimate[0:1, :]
-    here = slice(first, first + high.shape[1])
-    _, weighted = weights(sums, plan[here, :], grad_dots[here, :], scale)
-    terms[...] = dot3((high[...], low[...]), halves(weighted))
+    for i, first in enumerate(firsts):
+        high, low = blocks[2 * i : 2 * i + 2]
+        here = slice(first, first + high.shape[1])
+        _, weighted = weights(sums, plan[here, :], grad_dots[here, :], scale)
+        term = dot3((high[...], low[...]), halves(weighted))
+        terms[...] = terms[...] + term if i else term
     width = total.shape[0] // n_text
     for k in range(n_text):
         here = pl.ds(pl.multiple_of((place[0] ^ k) * width, width), width)
@@ -353,18 +356,19 @@
         sums = sums + swap(sums, "text", step)
         step *= 2
 
-    def text_part(r, name, before, pieces=1):
+    def text_part(r, name, before, pieces=1, came=()):
         late, first = divmod(r * rows, half * rows)
         return call(
-            functools.partial(text_kernel, scale, first),
+            functools.partial(text_kernel, scale, first, len(came)),
             name,
-            [sums, plans[late], dots[late], *right],
+            [sums, plans[late], dots[late], *right, *came],
             [((rows // pieces, feats), jnp.float32)] * pieces,
             before=before,
         )
 
     shape = ((n_text // 2, width, frames // 2), jnp.float32)
 
+    direct = range(n_speech - 1, n_speech)
     others = []
     for r in range(2, n_speech, 2):
         (term,) = text_part(r + 1, "text_far", [])
@@ -372,15 +376,15 @@
         part = part + swap(term, "speech", 1)
         others.append(swap(part, "speech", r))
     keep_a, send_a, keep_b, send_b = call(
-        functools.partial(finish_kernel, n_text, scale, (half - 1) * rows),
+        functools.partial(finish_kernel, n_text, scale, [(r - half) * rows for r in direct]),
         "finish",
-        [place, estimate, sums, *total, plans[1], dots[1], across_highs[-1], across_lows[-1]],
+        [place, estimate, sums, *total, plans[1], dots[1], *(across for r in direct for across in split[r][2:])],
         [shape] * 4,
         places=1,
         before=[term],
         scratch=[pltpu.VMEM((feats, frames), jnp.float32)],
     )
-    crossed = [swap(piece, "speech", 1) for piece in text_part(1, "text_near", [part], 2)]
+    crossed = [swap(piece, "speech", 1) for piece in text_part(1, "text_near", [keep_a], 2)]
     keep_a, send_a = halve(keep_a, swap(send_a, "text", 1))
     keep_b, send_b = halve(keep_b, swap(send_b, "text", 2))
     keep, send = halve(keep_a, swap(send_a, "text", 2), keep_b, swap(send_b, "text", 1))
@@ -388,23 +392,20 @@
     while 2 * step < n_text:
         keep, send = halve(keep, swap(send, "text", step))
         step *= 2
-    (own,) = text_part(0, "text_near", [part])
-    text_grad = call(sum_kernel, "add", [own, *others, *crossed], ((rows, feats), jnp.float32))
-    speech_block = call(add_kernel, "join", [keep[0], swap(send[0], "text", step)], ((width, frames), jnp.float32), before=[own])
+    (own,) = text_part(0, "text_near", [part], came=crossed)
+    text_grad, speech_block = call(
+        last_kernel,
+        "add",
+        [keep[0], swap(send[0], "text", step), own, *others],
+        [((rows, feats), jnp.float32), ((width, frames), jnp.float32)],
+    )
     return (speech_block.T, text_grad)
 
 
-def sum_kernel(*refs):
-    *terms, out = refs
-    rows = out.shape[0]
-    total = terms[0][...]
-    pieces = [term for term in terms if term.shape[0] < rows]
-    for term in terms[1 : len(terms) - len(pieces)]:
-        total = total + term[...]
-    count = rows // len(pieces)
-    for i, piece in enumerate(pieces):
-        here = slice(i * count, (i + 1) * count)
-        out[here, :] = total[here, :] + piece[...]
+def last_kernel(kept, came, *refs):
+    *terms, text_out, speech_out = refs
+    speech_out[...] = kept[...] + came[...]
+    add_kernel(*terms, text_out)
 
 
 def solution(mesh):

time: 89.1 us -> 88.5 us (level)
    pallas_call x29 -> x28, Pallas kernels: 32.8 us -> 32.3 us  [call(): pl.pallas_call(body, in_specs=[IN_SMEM] * places + [IN_VMEM] * (count - p...]
where the time goes in v3:
time: 88.5 us; the launch traced here: 88.3 us
  Pallas kernels  32.3 us (36%)
  starting transfers between devices  28.4 us (32%)
  waiting for transfers between devices  25.4 us (29%)
  other arithmetic  1.27 us (1%)
  between operations  0.9 us (1%)
    pallas_call x28, Pallas kernels, call(): pl.pallas_call(body, in_specs=[IN_SMEM] * places + [IN_VMEM] * (count - p...  32.3 us
    ppermute x22, starting transfers between devices, swap(): return lax.ppermute(value, axis, [(i, i ^ k) for i in range(count)])  28.4 us
    ppermute x22, waiting for transfers between devices, swap(): return lax.ppermute(value, axis, [(i, i ^ k) for i in range(count)])  25.4 us
  transfers between devices with their start and end apart: 22, of which 11 were waited for; matrix products, arithmetic and copies ran while one was open for 1% of the time, Pallas kernels for 29%

profile of v3, /device:TPU:0, one launch (start us, length us, event | category | flops | bytes accessed | tf_op | source)
XLA Modules:
  0.0 88.3 jit_solution(16416407821054931810)
XLA Ops:
  0.7 0.5 collective-permute-start
  1.2 2.6 %collective-permute-start.8 = (f32[512,512]{1,0:T(8,128)}, f32[512,512]{1,0:T(8,128)}, u32[]{:S(2)}, u32[]{:S(2)}) collective-permute-start(f32[512,512]{1,0:T(8,128)} %refs_1_.1), channel_id=1, source_target_pairs={{0,16},{8,24},{16,0},{24,8},{1,17},{9,25},{17,1},{25,9},{2,18},{10... | collective-permute-start | bytes 3145736 | tf_op jit(solution)/shard_map/ppermute | solution.py:258
  3.8 1.0 %pad_maximum_fusion.refs_0_ = f32[128,512]{1,0:T(8,128)S(1)} fusion(f32[64,512]{1,0:T(8,128)} %bitcast.9, f32[64,512]{1,0:T(8,128)} %bitcast.10), kind=kLoop, calls=%fused_computation | loop fusion | flops 65536 | bytes 524288 | tf_op jit(solution)/shard_map/concatenate | solution.py:276
  4.8 1.9 %collective-permute-start.2 = (f32[128,512]{1,0:T(8,128)S(1)}, f32[128,512]{1,0:T(8,128)S(1)}, u32[]{:S(2)}, u32[]{:S(2)}) collective-permute-start(f32[128,512]{1,0:T(8,128)S(1)} %copy.9.refs_1_), channel_id=1, source_target_pairs={{0,2},{1,3},{2,0},{3,1},{4,6},{5,7},{6,4},{7,5},{8,10},{9,11},{10,... | collective-permute-start | bytes 786440 | tf_op jit(solution)/shard_map/ppermute | solution.py:258
  6.7 1.5 %collective-permute-start.1 = (f32[128,512]{1,0:T(8,128)S(1)}, f32[128,512]{1,0:T(8,128)S(1)}, u32[]{:S(2)}, u32[]{:S(2)}) collective-permute-start(f32[128,512]{1,0:T(8,128)S(1)} %copy.9.refs_1_), channel_id=1, source_target_pairs={{0,1},{1,0},{2,3},{3,2},{4,5},{5,4},{6,7},{7,6},{8,9},{9,8},{10,11... | collective-permute-start | bytes 786440 | tf_op jit(solution)/shard_map/ppermute | solution.py:258
  8.2 2.6 %collective-permute-start.4 = (f32[128,512]{1,0:T(8,128)S(1)}, f32[128,512]{1,0:T(8,128)S(1)}, u32[]{:S(2)}, u32[]{:S(2)}) collective-permute-start(f32[128,512]{1,0:T(8,128)S(1)} %copy.9.refs_1_), channel_id=1, source_target_pairs={{0,4},{1,5},{2,6},{3,7},{4,0},{5,1},{6,2},{7,3},{8,12},{9,13},{10,... | collective-permute-start | bytes 786440 | tf_op jit(solution)/shard_map/ppermute | solution.py:258
  10.8 0.1 pad_add_fusion.refs_0_
  10.9 0.9 offsets.1.refs_3_.refs_1_.refs_0_
  11.8 0.9 %split.4 = (bf16[512,512]{1,0:T(8,128)(2,1)S(1)}, bf16[512,512]{1,0:T(8,128)(2,1)S(1)}, bf16[512,512]{1,0:T(8,128)(2,1)S(1)}, bf16[512,512]{1,0:T(8,128)(2,1)S(1)}) custom-call(s32[2]{0:T(128)S(1)} %pad_add_fusion.refs_0_, f32[512,512]{1,0:T(8,128)S(1)} %copy-done), custom_call_target="tpu_custom_call" | custom-call | flops 1000000000 | tf_op jit(solution)/shard_map/split/pallas_call | solution.py:52
  12.7 4.9 %collective-permute-done.2.refs_3_.refs_2_ = f32[128,512]{1,0:T(8,128)S(1)} collective-permute-done((f32[128,512]{1,0:T(8,128)S(1)}, f32[128,512]{1,0:T(8,128)S(1)}, u32[]{:S(2)}, u32[]{:S(2)}) %collective-permute-start.2) | collective-permute-done | bytes 262176 | tf_op jit(solution)/shard_map/ppermute | solution.py:258
  17.6 2.6 %collective-permute-start.3 = (f32[128,512]{1,0:T(8,128)S(1)}, f32[128,512]{1,0:T(8,128)S(1)}, u32[]{:S(2)}, u32[]{:S(2)}) collective-permute-start(f32[128,512]{1,0:T(8,128)S(1)} %collective-permute-done.2.refs_3_.refs_2_), channel_id=1, source_target_pairs={{0,1},{1,0},{2,3},{3,2},{4,5},{5,4},{6,7},{7,6},{8,9},{9,8},{10,11... | collective-permute-start | bytes 786440 | tf_op jit(solution)/shard_map/ppermute | solution.py:258
  20.2 0.9 %split.5 = (bf16[512,512]{1,0:T(8,128)(2,1)S(1)}, bf16[512,512]{1,0:T(8,128)(2,1)S(1)}, bf16[512,512]{1,0:T(8,128)(2,1)S(1)}, bf16[512,512]{1,0:T(8,128)(2,1)S(1)}) custom-call(s32[2]{0:T(128)S(1)} %pad_add_fusion.refs_0_, f32[512,512]{1,0:T(8,128)S(1)} %collective-permute-done.refs_1_), custom_call_target="tpu_custom_call" | custom-call | flops 1000000000 | tf_op jit(solution)/shard_map/split/pallas_call | solution.py:52
  21.1 0.0 collective-permute-done.1.refs_2_.refs_1_
  21.1 1.4 %collective-permute-done.4.refs_0_.refs_4_ = f32[128,512]{1,0:T(8,128)S(1)} collective-permute-done((f32[128,512]{1,0:T(8,128)S(1)}, f32[128,512]{1,0:T(8,128)S(1)}, u32[]{:S(2)}, u32[]{:S(2)}) %collective-permute-start.4) | collective-permute-done | bytes 262176 | tf_op jit(solution)/shard_map/ppermute | solution.py:258
  22.6 0.1 collective-permute-start.6
  22.7 0.7 collective-permute-start.5
  23.4 4.0 %collective-permute-done.3.refs_4_ = f32[128,512]{1,0:T(8,128)S(1)} collective-permute-done((f32[128,512]{1,0:T(8,128)S(1)}, f32[128,512]{1,0:T(8,128)S(1)}, u32[]{:S(2)}, u32[]{:S(2)}) %collective-permute-start.3) | collective-permute-done | bytes 262176 | tf_op jit(solution)/shard_map/ppermute | solution.py:258
  27.4 2.5 %plan_part.1 = (f32[512,1024]{1,0:T(8,128)S(1)}, f32[512,1024]{1,0:T(8,128)S(1)}, bf16[256,1024]{1,0:T(8,128)(2,1)S(1)}, bf16[256,1024]{1,0:T(8,128)(2,1)S(1)}) custom-call(s32[2]{0:T(128)S(1)} %pad_add_fusion.refs_0_, f32[128,512]{1,0:T(8,128)S(1)} %copy.9.refs_1_, f32[128,512]{1,0:T(8,128)S(1)} %collective-permute-done.1.refs_2_.refs_1_, ...), custom_call_target="tpu_custom_call" | custom-call | flops 1000000000 | tf_op jit(solution)/shard_map/plan_part/pallas_call | solution.py:52
  29.9 0.0 collective-permute-done.6.refs_0_.refs_6_
  29.9 2.1 %collective-permute-start.7 = (f32[128,512]{1,0:T(8,128)S(1)}, f32[128,512]{1,0:T(8,128)S(1)}, u32[]{:S(2)}, u32[]{:S(2)}) collective-permute-start(f32[128,512]{1,0:T(8,128)S(1)} %copy.11), channel_id=1, source_target_pairs={{0,1},{1,0},{2,3},{3,2},{4,5},{5,4},{6,7},{7,6},{8,9},{9,8},{10,11... | collective-permute-start | bytes 786440 | tf_op jit(solution)/shard_map/ppermute | solution.py:258
  32.0 0.0 collective-permute-done.8.refs_1_
  32.0 0.0 collective-permute-start.9
  32.0 1.6 %split.6 = (bf16[512,512]{1,0:T(8,128)(2,1)S(1)}, bf16[512,512]{1,0:T(8,128)(2,1)S(1)}, bf16[512,512]{1,0:T(8,128)(2,1)S(1)}, bf16[512,512]{1,0:T(8,128)(2,1)S(1)}) custom-call(s32[2]{0:T(128)S(1)} %pad_add_fusion.refs_0_, f32[512,512]{1,0:T(8,128)} %collective-permute-done.8.refs_1_), custom_call_target="tpu_custom_call" | custom-call | flops 1000000000 | tf_op jit(solution)/shard_map/split/pallas_call | solution.py:52
  33.6 1.0 %plan_more.1.refs_4_ = f32[512,1024]{1,0:T(8,128)S(1)} custom-call(bf16[256,1024]{1,0:T(8,128)(2,1)S(1)} %get-tuple-element.50.refs_1_.refs_2_.refs_0_, bf16[256,1024]{1,0:T(8,128)(2,1)S(1)} %get-tuple-element.51.refs_3_.refs_1_, bf16[512,512]{1,0:T(8,128)(2,1)S(1)} %get-tuple-element.57.refs_2_.refs_5_, bf16[512,512]{1,0:T(8,128)(2,1)S(1)} %get-tuple-element.58.refs_3_.refs_7_), custom_call_target="tpu_custom_call" | custom-call | flops 1000000000 | tf_op jit(solution)/shard_map/plan_more/pallas_call | solution.py:52
  34.6 0.0 collective-permute-done.5.refs_5_
  34.6 2.7 %collective-permute-done.7.refs_7_ = f32[128,512]{1,0:T(8,128)S(1)} collective-permute-done((f32[128,512]{1,0:T(8,128)S(1)}, f32[128,512]{1,0:T(8,128)S(1)}, u32[]{:S(2)}, u32[]{:S(2)}) %collective-permute-start.7) | collective-permute-done | bytes 262176 | tf_op jit(solution)/shard_map/ppermute | solution.py:258
  37.3 2.9 %plan_early.1 = (f32[1024,512]{1,0:T(8,128)S(1)}, f32[1024,512]{1,0:T(8,128)S(1)}, f32[8,512]{1,0:T(8,128)S(1)}, bf16[512,1024]{1,0:T(8,128)(2,1)S(1)}, bf16[512,1024]{1,0:T(8,128)(2,1)S(1)}) custom-call(s32[2]{0:T(128)S(1)} %pad_add_fusion.refs_0_, f32[2048,128]{1,0:T(8,128)S(1)} %offsets.1.refs_3_.refs_1_.refs_0_, ...), custom_call_target="tpu_custom_call" | custom-call | flops 99999997952 | tf_op jit(solution)/shard_map/plan_early/pallas_call | solution.py:52
  40.2 0.0 collective-permute-done.9.refs_1_
  40.3 0.9 %split.7 = (bf16[512,512]{1,0:T(8,128)(2,1)S(1)}, bf16[512,512]{1,0:T(8,128)(2,1)S(1)}, bf16[512,512]{1,0:T(8,128)(2,1)S(1)}, bf16[512,512]{1,0:T(8,128)(2,1)S(1)}) custom-call(s32[2]{0:T(128)S(1)} %pad_add_fusion.refs_0_, f32[512,512]{1,0:T(8,128)S(1)} %collective-permute-done.9.refs_1_), custom_call_target="tpu_custom_call" | custom-call | flops 1000000000 | tf_op jit(solution)/shard_map/split/pallas_call | solution.py:52
  41.2 2.9 %plan_late.1 = (f32[1024,512]{1,0:T(8,128)S(1)}, f32[1024,512]{1,0:T(8,128)S(1)}, f32[8,512]{1,0:T(8,128)S(1)}) custom-call(f32[2048,128]{1,0:T(8,128)S(1)} %offsets.1.refs_3_.refs_1_.refs_0_, f32[8,512]{1,0:T(8,128)S(1)} %get-tuple-element.54.refs_1_, bf16[512,1024]{1,0:T(8,128)(2,1)S(1)} %get-tuple-element.55.refs_2_.refs_1_, ...), custom_call_target="tpu_custom_call" | custom-call | flops 3000000000 | tf_op jit(solution)/shard_map/plan_late/pallas_call | solution.py:52
  44.0 1.8 %collective-permute-start.10 = (f32[8,512]{1,0:T(8,128)S(1)}, f32[8,512]{1,0:T(8,128)S(1)}, u32[]{:S(2)}, u32[]{:S(2)}) collective-permute-start(f32[8,512]{1,0:T(8,128)S(1)} %get-tuple-element.61.refs_0_.refs_5_.refs_1_), channel_id=1, source_target_pairs={{0,1},{1,0},{2,3},{3,2},{4,5},{5,4},{6,7},{7,6},{8,9},{9,8},{10,11... | collective-permute-start | bytes 49160 | tf_op jit(solution)/shard_map/ppermute | solution.py:258
  45.8 1.9 %moments.3.refs_2_.refs_5_ = f32[512,1024]{1,0:T(8,128)S(1)} custom-call(f32[8,512]{1,0:T(8,128)S(1)} %get-tuple-element.61.refs_0_.refs_5_.refs_1_, f32[1024,512]{1,0:T(8,128)S(1)} %get-tuple-element.62.refs_1_, f32[1024,512]{1,0:T(8,128)S(1)} %get-tuple-element.63.refs_2_, bf16[512,512]{1,0:T(8,128)(2,1)S(1)} %get-tuple-element.64.refs_3_, ...), custom_call_target="tpu_custom_call" | custom-call | flops 3000000000 | tf_op jit(solution)/shard_map/moments/pallas_call | solution.py:52
  47.7 0.1 collective-permute-done.10.refs_1_
  47.8 0.0 collective-permute-start.11
  47.8 1.9 %moments.4.refs_2_.refs_5_ = f32[512,1024]{1,0:T(8,128)S(1)} custom-call(f32[8,512]{1,0:T(8,128)S(1)} %get-tuple-element.61.refs_0_.refs_5_.refs_1_, f32[1024,512]{1,0:T(8,128)S(1)} %get-tuple-element.62.refs_1_, f32[1024,512]{1,0:T(8,128)S(1)} %get-tuple-element.63.refs_2_, bf16[512,512]{1,0:T(8,128)(2,1)S(1)} %get-tuple-element.66.refs_3_, ...), custom_call_target="tpu_custom_call" | custom-call | flops 3000000000 | tf_op jit(solution)/shard_map/moments/pallas_call | solution.py:52
  49.8 1.8 %collective-permute-done.11.refs_1_ = f32[8,512]{1,0:T(8,128)S(1)} collective-permute-done((f32[8,512]{1,0:T(8,128)S(1)}, f32[8,512]{1,0:T(8,128)S(1)}, u32[]{:S(2)}, u32[]{:S(2)}) %collective-permute-start.11) | collective-permute-done | bytes 16416 | tf_op jit(solution)/shard_map/ppermute | solution.py:258
  51.6 1.3 %collective-permute-start.12 = (f32[8,512]{1,0:T(8,128)S(1)}, f32[8,512]{1,0:T(8,128)S(1)}, u32[]{:S(2)}, u32[]{:S(2)}) collective-permute-start(f32[8,512]{1,0:T(8,128)S(1)} %hop.4.refs_6_.refs_0_.refs_3_), channel_id=1, source_target_pairs={{0,4},{1,5},{2,6},{3,7},{4,0},{5,1},{6,2},{7,3},{8,12},{9,13},{10,... | collective-permute-start | bytes 49160 | tf_op jit(solution)/shard_map/ppermute | solution.py:258
  52.9 2.1 %moments.5.refs_2_.refs_3_ = f32[512,1024]{1,0:T(8,128)S(1)} custom-call(f32[8,512]{1,0:T(8,128)S(1)} %get-tuple-element.61.refs_0_.refs_5_.refs_1_, f32[1024,512]{1,0:T(8,128)S(1)} %get-tuple-element.68.refs_1_.refs_4_, f32[1024,512]{1,0:T(8,128)S(1)} %get-tuple-element.69.refs_2_.refs_5_, bf16[512,512]{1,0:T(8,128)(2,1)S(1)} %get-tuple-element.70.refs_3_, ...), custom_call_target="tpu_custom_call" | custom-call | flops 3000000000 | tf_op jit(solution)/shard_map/moments/pallas_call | solution.py:52
  55.0 1.5 %frames_first.1 = (bf16[1024,512]{1,0:T(8,128)(2,1)S(1)}, bf16[1024,512]{1,0:T(8,128)(2,1)S(1)}) custom-call(s32[2]{0:T(128)S(1)} %pad_add_fusion.refs_0_, bf16[512,1024]{1,0:T(8,128)(2,1)S(1)} %get-tuple-element.55.refs_2_.refs_1_, bf16[512,1024]{1,0:T(8,128)(2,1)S(1)} %get-tuple-element.56.refs_3_.refs_2_, f32[8,512]{1,0:T(8,128)S(1)} %hop.4.refs_6_.refs_0_.refs_3_), custom_call_target="tpu_custom_call" | custom-call | flops 1000000000 | tf_op jit(solution)/shard_map/frames_first/pallas_call | solution.py:52
  56.5 0.0 collective-permute-done.12.refs_1_
  56.5 1.9 %text_far.2.refs_8_.refs_5_ = f32[512,512]{1,0:T(8,128)S(1)} custom-call(f32[8,512]{1,0:T(8,128)S(1)} %hop.5.refs_0_.refs_2_, f32[1024,512]{1,0:T(8,128)S(1)} %get-tuple-element.68.refs_1_.refs_4_, f32[1024,512]{1,0:T(8,128)S(1)} %get-tuple-element.69.refs_2_.refs_5_, bf16[1024,512]{1,0:T(8,128)(2,1)S(1)} %get-tuple-element.74.refs_3_, ...), custom_call_target="tpu_custom_call" | custom-call | tf_op jit(solution)/shard_map/text_far/pallas_call | solution.py:52
  58.4 0.1 collective-permute-start.20
  58.5 1.9 %text_far.3 = f32[512,512]{1,0:T(8,128)S(1)} custom-call(f32[8,512]{1,0:T(8,128)S(1)} %hop.5.refs_0_.refs_2_, f32[1024,512]{1,0:T(8,128)S(1)} %get-tuple-element.68.refs_1_.refs_4_, f32[1024,512]{1,0:T(8,128)S(1)} %get-tuple-element.69.refs_2_.refs_5_, bf16[1024,512]{1,0:T(8,128)(2,1)S(1)} %get-tuple-element.74.refs_3_, ...), custom_call_target="tpu_custom_call" | custom-call | tf_op jit(solution)/shard_map/text_far/pallas_call | solution.py:52
  60.3 0.8 collective-permute-done.20
  61.1 0.2 add.4.refs_7_
  61.3 1.6 %collective-permute-start.21 = (f32[512,512]{1,0:T(8,128)S(1)}, f32[512,512]{1,0:T(8,128)S(1)}, u32[]{:S(2)}, u32[]{:S(2)}) collective-permute-start(f32[512,512]{1,0:T(8,128)S(1)} %add.4.refs_7_), channel_id=1, source_target_pairs={{0,16},{8,24},{16,0},{24,8},{1,17},{9,25},{17,1},{25,9},{2,18},{10... | collective-permute-start | bytes 3145736 | tf_op jit(solution)/shard_map/ppermute | solution.py:258
  62.9 1.8 %finish.1 = (f32[4,64,256]{2,1,0:T(8,128)S(1)}, f32[4,64,256]{2,1,0:T(8,128)S(1)}, f32[4,64,256]{2,1,0:T(8,128)S(1)}, f32[4,64,256]{2,1,0:T(8,128)S(1)}) custom-call(s32[2]{0:T(128)S(1)} %pad_add_fusion.refs_0_, f32[8,512]{1,0:T(8,128)S(1)} %get-tuple-element.61.refs_0_.refs_5_.refs_1_, f32[8,512]{1,0:T(8,128)S(1)} %hop.5.refs_0_.refs_2_, ...), custom_call_target="tpu_custom_call" | custom-call | tf_op jit(solution)/shard_map/finish/pallas_call | solution.py:52
  64.7 1.8 %collective-permute-start.13 = (f32[4,64,256]{2,1,0:T(8,128)S(1)}, f32[4,64,256]{2,1,0:T(8,128)S(1)}, u32[]{:S(2)}, u32[]{:S(2)}) collective-permute-start(f32[4,64,256]{2,1,0:T(8,128)S(1)} %get-tuple-element.77), channel_id=1, source_target_pairs={{0,1},{1,0},{2,3},{3,2},{4,5},{5,4},{6,7},{7,6},{8,9},{9,8},{10,11... | collective-permute-start | bytes 786440 | tf_op jit(solution)/shard_map/ppermute | solution.py:258
  66.5 1.7 %collective-permute-start.15 = (f32[4,64,256]{2,1,0:T(8,128)S(1)}, f32[4,64,256]{2,1,0:T(8,128)S(1)}, u32[]{:S(2)}, u32[]{:S(2)}) collective-permute-start(f32[4,64,256]{2,1,0:T(8,128)S(1)} %get-tuple-element.81), channel_id=1, source_target_pairs={{0,2},{1,3},{2,0},{3,1},{4,6},{5,7},{6,4},{7,5},{8,10},{9,11},{10,... | collective-permute-start | bytes 786440 | tf_op jit(solution)/shard_map/ppermute | solution.py:258
  68.3 1.8 %text_near.2 = (f32[256,512]{1,0:T(8,128)S(1)}, f32[256,512]{1,0:T(8,128)S(1)}) custom-call(f32[8,512]{1,0:T(8,128)S(1)} %hop.5.refs_0_.refs_2_, f32[1024,512]{1,0:T(8,128)S(1)} %get-tuple-element.62.refs_1_, f32[1024,512]{1,0:T(8,128)S(1)} %get-tuple-element.63.refs_2_, bf16[1024,512]{1,0:T(8,128)(2,1)S(1)} %get-tuple-element.74.refs_3_, ...), custom_call_target="tpu_custom_call" | custom-call | tf_op jit(solution)/shard_map/text_near/pallas_call | solution.py:52
  70.1 0.1 collective-permute-start.18
  70.2 0.5 collective-permute-start.19
  70.7 2.2 %collective-permute-done.13.refs_1_ = f32[4,64,256]{2,1,0:T(8,128)S(1)} collective-permute-done((f32[4,64,256]{2,1,0:T(8,128)S(1)}, f32[4,64,256]{2,1,0:T(8,128)S(1)}, u32[]{:S(2)}, u32[]{:S(2)}) %collective-permute-start.13) | collective-permute-done | bytes 262176 | tf_op jit(solution)/shard_map/ppermute | solution.py:258
  72.9 1.8 %collective-permute-start.14 = (f32[2,64,256]{2,1,0:T(8,128)S(1)}, f32[2,64,256]{2,1,0:T(8,128)S(1)}, u32[]{:S(2)}, u32[]{:S(2)}) collective-permute-start(f32[2,64,256]{2,1,0:T(8,128)S(1)} %get-tuple-element.79), channel_id=1, source_target_pairs={{0,2},{1,3},{2,0},{3,1},{4,6},{5,7},{6,4},{7,5},{8,10},{9,11},{10,... | collective-permute-start | bytes 393224 | tf_op jit(solution)/shard_map/ppermute | solution.py:258
  74.7 0.0 collective-permute-done.15.refs_1_
  74.7 1.8 %collective-permute-start.16 = (f32[2,64,256]{2,1,0:T(8,128)S(1)}, f32[2,64,256]{2,1,0:T(8,128)S(1)}, u32[]{:S(2)}, u32[]{:S(2)}) collective-permute-start(f32[2,64,256]{2,1,0:T(8,128)S(1)} %get-tuple-element.83), channel_id=1, source_target_pairs={{0,1},{1,0},{2,3},{3,2},{4,5},{5,4},{6,7},{7,6},{8,9},{9,8},{10,11... | collective-permute-start | bytes 393224 | tf_op jit(solution)/shard_map/ppermute | solution.py:258
  76.5 1.4 %collective-permute-done.14.refs_1_ = f32[2,64,256]{2,1,0:T(8,128)S(1)} collective-permute-done((f32[2,64,256]{2,1,0:T(8,128)S(1)}, f32[2,64,256]{2,1,0:T(8,128)S(1)}, u32[]{:S(2)}, u32[]{:S(2)}) %collective-permute-start.14) | collective-permute-done | bytes 131104 | tf_op jit(solution)/shard_map/ppermute | solution.py:258
  77.9 1.8 %collective-permute-done.16.refs_3_ = f32[2,64,256]{2,1,0:T(8,128)S(1)} collective-permute-done((f32[2,64,256]{2,1,0:T(8,128)S(1)}, f32[2,64,256]{2,1,0:T(8,128)S(1)}, u32[]{:S(2)}, u32[]{:S(2)}) %collective-permute-start.16) | collective-permute-done | bytes 131104 | tf_op jit(solution)/shard_map/ppermute | solution.py:258
  79.8 1.3 %collective-permute-start.17 = (f32[64,512]{1,0:T(8,128)S(1)}, f32[64,512]{1,0:T(8,128)S(1)}, u32[]{:S(2)}, u32[]{:S(2)}) collective-permute-start(f32[64,512]{1,0:T(8,128)S(1)} %bitcast.8), channel_id=1, source_target_pairs={{0,4},{1,5},{2,6},{3,7},{4,0},{5,1},{6,2},{7,3},{8,12},{9,13},{10,... | collective-permute-start | bytes 393224 | tf_op jit(solution)/shard_map/ppermute | solution.py:258
  81.1 0.0 collective-permute-done.19.refs_6_
  81.1 1.9 %text_near.3.refs_2_ = f32[512,512]{1,0:T(8,128)S(1)} custom-call(f32[8,512]{1,0:T(8,128)S(1)} %hop.5.refs_0_.refs_2_, f32[1024,512]{1,0:T(8,128)S(1)} %get-tuple-element.62.refs_1_, f32[1024,512]{1,0:T(8,128)S(1)} %get-tuple-element.63.refs_2_, bf16[1024,512]{1,0:T(8,128)(2,1)S(1)} %get-tuple-element.74.refs_3_, ...), custom_call_target="tpu_custom_call" | custom-call | tf_op jit(solution)/shard_map/text_near/pallas_call | solution.py:52
  83.0 4.2 %collective-permute-done.17.refs_1_ = f32[64,512]{1,0:T(8,128)S(1)} collective-permute-done((f32[64,512]{1,0:T(8,128)S(1)}, f32[64,512]{1,0:T(8,128)S(1)}, u32[]{:S(2)}, u32[]{:S(2)}) %collective-permute-start.17) | collective-permute-done | bytes 131104 | tf_op jit(solution)/shard_map/ppermute | solution.py:258
  87.1 0.0 collective-permute-done.21.refs_3_
  87.1 1.1 %add.7 = (f32[512,512]{1,0:T(8,128)}, f32[64,512]{1,0:T(8,128)}) custom-call(f32[64,512]{1,0:T(8,128)S(1)} %bitcast.7, f32[64,512]{1,0:T(8,128)S(1)} %collective-permute-done.17.refs_1_, f32[512,512]{1,0:T(8,128)S(1)} %text_near.3.refs_2_, f32[512,512]{1,0:T(8,128)S(1)} %collective-permute-done.21.refs_3_), custom_call_target="tpu_custom_call" | custom-call | flops 99999997952 | tf_op jit(solution)/shard_map/add/pallas_call | solution.py:52
  (16 shorter events, 0.2 us)
Async XLA Ops:
  0.6 11.1 %copy-start = (f32[512,512]{1,0:T(8,128)S(1)}, f32[512,512]{1,0:T(8,128)}, u32[]{:S(2)}) copy-start(f32[512,512]{1,0:T(8,128)} %refs_1_.1) | copy-start | bytes 3145732
  0.6 6.1 %copy-start.1 = (f32[2048]{0:T(1024)S(1)}, f32[2048]{0:T(1024)}, u32[]{:S(2)}) copy-start(f32[2048]{0:T(1024)} %param.6) | copy-start | bytes 24580
  0.7 4.1 %collective-permute-start = (f32[512,512]{1,0:T(8,128)}, f32[512,512]{1,0:T(8,128)S(1)}, u32[]{:S(2)}, u32[]{:S(2)}) collective-permute-start(f32[512,512]{1,0:T(8,128)} %refs_1_.1), channel_id=1, source_target_pairs={{0,8},{8,0},{16,24},{24,16},{1,9},{9,1},{17,25},{25,17},{2,10},{10... | collective-permute-start | bytes 3145736 | tf_op jit(solution)/shard_map/ppermute | solution.py:258
  1.2 30.9 %collective-permute-start.8 = (f32[512,512]{1,0:T(8,128)}, f32[512,512]{1,0:T(8,128)}, u32[]{:S(2)}, u32[]{:S(2)}) collective-permute-start(f32[512,512]{1,0:T(8,128)} %refs_1_.1), channel_id=1, source_target_pairs={{0,16},{8,24},{16,0},{24,8},{1,17},{9,25},{17,1},{25,9},{2,18},{10... | collective-permute-start | bytes 3145736 | tf_op jit(solution)/shard_map/ppermute | solution.py:258
  4.8 12.8 %collective-permute-start.2 = (f32[128,512]{1,0:T(8,128)S(1)}, f32[128,512]{1,0:T(8,128)S(1)}, u32[]{:S(2)}, u32[]{:S(2)}) collective-permute-start(f32[128,512]{1,0:T(8,128)S(1)} %copy.9.refs_1_), channel_id=1, source_target_pairs={{0,2},{1,3},{2,0},{3,1},{4,6},{5,7},{6,4},{7,5},{8,10},{9,11},{10,... | collective-permute-start | bytes 786440 | tf_op jit(solution)/shard_map/ppermute | solution.py:258
  6.7 14.4 %collective-permute-start.1 = (f32[128,512]{1,0:T(8,128)S(1)}, f32[128,512]{1,0:T(8,128)S(1)}, u32[]{:S(2)}, u32[]{:S(2)}) collective-permute-start(f32[128,512]{1,0:T(8,128)S(1)} %copy.9.refs_1_), channel_id=1, source_target_pairs={{0,1},{1,0},{2,3},{3,2},{4,5},{5,4},{6,7},{7,6},{8,9},{9,8},{10,11... | collective-permute-start | bytes 786440 | tf_op jit(solution)/shard_map/ppermute | solution.py:258
  8.2 14.4 %collective-permute-start.4 = (f32[128,512]{1,0:T(8,128)S(1)}, f32[128,512]{1,0:T(8,128)S(1)}, u32[]{:S(2)}, u32[]{:S(2)}) collective-permute-start(f32[128,512]{1,0:T(8,128)S(1)} %copy.9.refs_1_), channel_id=1, source_target_pairs={{0,4},{1,5},{2,6},{3,7},{4,0},{5,1},{6,2},{7,3},{8,12},{9,13},{10,... | collective-permute-start | bytes 786440 | tf_op jit(solution)/shard_map/ppermute | solution.py:258
  17.6 9.8 %collective-permute-start.3 = (f32[128,512]{1,0:T(8,128)S(1)}, f32[128,512]{1,0:T(8,128)S(1)}, u32[]{:S(2)}, u32[]{:S(2)}) collective-permute-start(f32[128,512]{1,0:T(8,128)S(1)} %collective-permute-done.2.refs_3_.refs_2_), channel_id=1, source_target_pairs={{0,1},{1,0},{2,3},{3,2},{4,5},{5,4},{6,7},{7,6},{8,9},{9,8},{10,11... | collective-permute-start | bytes 786440 | tf_op jit(solution)/shard_map/ppermute | solution.py:258
  22.6 7.3 %collective-permute-start.6 = (f32[128,512]{1,0:T(8,128)S(1)}, f32[128,512]{1,0:T(8,128)S(1)}, u32[]{:S(2)}, u32[]{:S(2)}) collective-permute-start(f32[128,512]{1,0:T(8,128)S(1)} %copy.10), channel_id=1, source_target_pairs={{0,2},{1,3},{2,0},{3,1},{4,6},{5,7},{6,4},{7,5},{8,10},{9,11},{10,... | collective-permute-start | bytes 786440 | tf_op jit(solution)/shard_map/ppermute | solution.py:258
  22.7 12.0 %collective-permute-start.5 = (f32[128,512]{1,0:T(8,128)S(1)}, f32[128,512]{1,0:T(8,128)S(1)}, u32[]{:S(2)}, u32[]{:S(2)}) collective-permute-start(f32[128,512]{1,0:T(8,128)S(1)} %collective-permute-done.4.refs_0_.refs_4_), channel_id=1, source_target_pairs={{0,1},{1,0},{2,3},{3,2},{4,5},{5,4},{6,7},{7,6},{8,9},{9,8},{10,11... | collective-permute-start | bytes 786440 | tf_op jit(solution)/shard_map/ppermute | solution.py:258
  29.9 7.4 %collective-permute-start.7 = (f32[128,512]{1,0:T(8,128)S(1)}, f32[128,512]{1,0:T(8,128)S(1)}, u32[]{:S(2)}, u32[]{:S(2)}) collective-permute-start(f32[128,512]{1,0:T(8,128)S(1)} %copy.11), channel_id=1, source_target_pairs={{0,1},{1,0},{2,3},{3,2},{4,5},{5,4},{6,7},{7,6},{8,9},{9,8},{10,11... | collective-permute-start | bytes 786440 | tf_op jit(solution)/shard_map/ppermute | solution.py:258
  32.0 8.2 %collective-permute-start.9 = (f32[512,512]{1,0:T(8,128)}, f32[512,512]{1,0:T(8,128)S(1)}, u32[]{:S(2)}, u32[]{:S(2)}) collective-permute-start(f32[512,512]{1,0:T(8,128)} %collective-permute-done.8.refs_1_), channel_id=1, source_target_pairs={{0,8},{8,0},{16,24},{24,16},{1,9},{9,1},{17,25},{25,17},{2,10},{10... | collective-permute-start | bytes 3145736 | tf_op jit(solution)/shard_map/ppermute | solution.py:258
  44.0 3.8 %collective-permute-start.10 = (f32[8,512]{1,0:T(8,128)S(1)}, f32[8,512]{1,0:T(8,128)S(1)}, u32[]{:S(2)}, u32[]{:S(2)}) collective-permute-start(f32[8,512]{1,0:T(8,128)S(1)} %get-tuple-element.61.refs_0_.refs_5_.refs_1_), channel_id=1, source_target_pairs={{0,1},{1,0},{2,3},{3,2},{4,5},{5,4},{6,7},{7,6},{8,9},{9,8},{10,11... | collective-permute-start | bytes 49160 | tf_op jit(solution)/shard_map/ppermute | solution.py:258
  47.8 3.8 %collective-permute-start.11 = (f32[8,512]{1,0:T(8,128)S(1)}, f32[8,512]{1,0:T(8,128)S(1)}, u32[]{:S(2)}, u32[]{:S(2)}) collective-permute-start(f32[8,512]{1,0:T(8,128)S(1)} %hop.3.refs_6_.refs_0_), channel_id=1, source_target_pairs={{0,2},{1,3},{2,0},{3,1},{4,6},{5,7},{6,4},{7,5},{8,10},{9,11},{10,... | collective-permute-start | bytes 49160 | tf_op jit(solution)/shard_map/ppermute | solution.py:258
  51.6 4.9 %collective-permute-start.12 = (f32[8,512]{1,0:T(8,128)S(1)}, f32[8,512]{1,0:T(8,128)S(1)}, u32[]{:S(2)}, u32[]{:S(2)}) collective-permute-start(f32[8,512]{1,0:T(8,128)S(1)} %hop.4.refs_6_.refs_0_.refs_3_), channel_id=1, source_target_pairs={{0,4},{1,5},{2,6},{3,7},{4,0},{5,1},{6,2},{7,3},{8,12},{9,13},{10,... | collective-permute-start | bytes 49160 | tf_op jit(solution)/shard_map/ppermute | solution.py:258
  58.4 2.7 %collective-permute-start.20 = (f32[512,512]{1,0:T(8,128)S(1)}, f32[512,512]{1,0:T(8,128)S(1)}, u32[]{:S(2)}, u32[]{:S(2)}) collective-permute-start(f32[512,512]{1,0:T(8,128)S(1)} %text_far.2.refs_8_.refs_5_), channel_id=1, source_target_pairs={{0,8},{8,0},{16,24},{24,16},{1,9},{9,1},{17,25},{25,17},{2,10},{10... | collective-permute-start | bytes 3145736 | tf_op jit(solution)/shard_map/ppermute | solution.py:258
  61.3 25.8 %collective-permute-start.21 = (f32[512,512]{1,0:T(8,128)S(1)}, f32[512,512]{1,0:T(8,128)S(1)}, u32[]{:S(2)}, u32[]{:S(2)}) collective-permute-start(f32[512,512]{1,0:T(8,128)S(1)} %add.4.refs_7_), channel_id=1, source_target_pairs={{0,16},{8,24},{16,0},{24,8},{1,17},{9,25},{17,1},{25,9},{2,18},{10... | collective-permute-start | bytes 3145736 | tf_op jit(solution)/shard_map/ppermute | solution.py:258
  64.7 8.1 %collective-permute-start.13 = (f32[4,64,256]{2,1,0:T(8,128)S(1)}, f32[4,64,256]{2,1,0:T(8,128)S(1)}, u32[]{:S(2)}, u32[]{:S(2)}) collective-permute-start(f32[4,64,256]{2,1,0:T(8,128)S(1)} %get-tuple-element.77), channel_id=1, source_target_pairs={{0,1},{1,0},{2,3},{3,2},{4,5},{5,4},{6,7},{7,6},{8,9},{9,8},{10,11... | collective-permute-start | bytes 786440 | tf_op jit(solution)/shard_map/ppermute | solution.py:258
  66.5 8.2 %collective-permute-start.15 = (f32[4,64,256]{2,1,0:T(8,128)S(1)}, f32[4,64,256]{2,1,0:T(8,128)S(1)}, u32[]{:S(2)}, u32[]{:S(2)}) collective-permute-start(f32[4,64,256]{2,1,0:T(8,128)S(1)} %get-tuple-element.81), channel_id=1, source_target_pairs={{0,2},{1,3},{2,0},{3,1},{4,6},{5,7},{6,4},{7,5},{8,10},{9,11},{10,... | collective-permute-start | bytes 786440 | tf_op jit(solution)/shard_map/ppermute | solution.py:258
  70.1 11.0 %collective-permute-start.18 = (f32[256,512]{1,0:T(8,128)S(1)}, f32[256,512]{1,0:T(8,128)S(1)}, u32[]{:S(2)}, u32[]{:S(2)}) collective-permute-start(f32[256,512]{1,0:T(8,128)S(1)} %get-tuple-element.86), channel_id=1, source_target_pairs={{0,8},{8,0},{16,24},{24,16},{1,9},{9,1},{17,25},{25,17},{2,10},{10... | collective-permute-start | bytes 1572872 | tf_op jit(solution)/shard_map/ppermute | solution.py:258
  70.2 10.9 %collective-permute-start.19 = (f32[256,512]{1,0:T(8,128)S(1)}, f32[256,512]{1,0:T(8,128)S(1)}, u32[]{:S(2)}, u32[]{:S(2)}) collective-permute-start(f32[256,512]{1,0:T(8,128)S(1)} %get-tuple-element.87), channel_id=1, source_target_pairs={{0,8},{8,0},{16,24},{24,16},{1,9},{9,1},{17,25},{25,17},{2,10},{10... | collective-permute-start | bytes 1572872 | tf_op jit(solution)/shard_map/ppermute | solution.py:258
  72.9 5.0 %collective-permute-start.14 = (f32[2,64,256]{2,1,0:T(8,128)S(1)}, f32[2,64,256]{2,1,0:T(8,128)S(1)}, u32[]{:S(2)}, u32[]{:S(2)}) collective-permute-start(f32[2,64,256]{2,1,0:T(8,128)S(1)} %get-tuple-element.79), channel_id=1, source_target_pairs={{0,2},{1,3},{2,0},{3,1},{4,6},{5,7},{6,4},{7,5},{8,10},{9,11},{10,... | collective-permute-start | bytes 393224 | tf_op jit(solution)/shard_map/ppermute | solution.py:258
  74.7 5.0 %collective-permute-start.16 = (f32[2,64,256]{2,1,0:T(8,128)S(1)}, f32[2,64,256]{2,1,0:T(8,128)S(1)}, u32[]{:S(2)}, u32[]{:S(2)}) collective-permute-start(f32[2,64,256]{2,1,0:T(8,128)S(1)} %get-tuple-element.83), channel_id=1, source_target_pairs={{0,1},{1,0},{2,3},{3,2},{4,5},{5,4},{6,7},{7,6},{8,9},{9,8},{10,11... | collective-permute-start | bytes 393224 | tf_op jit(solution)/shard_map/ppermute | solution.py:258
  79.8 7.3 %collective-permute-start.17 = (f32[64,512]{1,0:T(8,128)S(1)}, f32[64,512]{1,0:T(8,128)S(1)}, u32[]{:S(2)}, u32[]{:S(2)}) collective-permute-start(f32[64,512]{1,0:T(8,128)S(1)} %bitcast.8), channel_id=1, source_target_pairs={{0,4},{1,5},{2,6},{3,7},{4,0},{5,1},{6,2},{7,3},{8,12},{9,13},{10,... | collective-permute-start | bytes 393224 | tf_op jit(solution)/shard_map/ppermute | solution.py:258

commit v4 on v3

--- a/solution.py
+++ b/solution.py
@@ -14,7 +14,7 @@
     "plan_late": 3 * SHORT,
     "plan_part": SHORT,
     "plan_more": SHORT,
-    "moments": 3 * SHORT,
+    "moments": 6 * SHORT,
     "frames_first": SHORT,
     "split": SHORT,
     "offsets": SHORT // 10,
@@ -117,6 +117,17 @@
     for r in range(count):
         row = pot[pl.ds(place[1] ^ r, 1), :]
         out[r * rows : (r + 1) * rows, :] = jnp.broadcast_to(row, (out.shape[1], rows)).T
+
+
+def row_of(sums, i):
+    count = sums.shape[0] // 2
+    return jnp.concatenate([sums[i * count + j : i * count + j + 1, :] for j in range(count)], axis=1)
+
+
+def add_to_row(sums, i, row):
+    count, lanes = sums.shape[0] // 2, sums.shape[1]
+    for j in range(count):
+        sums[i * count + j : i * count + j + 1, :] += row[:, j * lanes : (j + 1) * lanes]
 
 
 def plan_rows(scale, first, pot, blocks, left, partials, plan_out, dots_out, sums_out):
@@ -138,8 +149,8 @@
         grad_dots = product[:, frames:]
         plan_out[here, :] = plan
         dots_out[here, :] = grad_dots
-        sums_out[0:1, :] += jnp.sum(plan, axis=0, keepdims=True)
-        sums_out[1:2, :] += jnp.sum(plan * grad_dots, axis=0, keepdims=True)
+        add_to_row(sums_out, 0, jnp.sum(plan, axis=0, keepdims=True))
+        add_to_row(sums_out, 1, jnp.sum(plan * grad_dots, axis=0, keepdims=True))
 
 
 def part_kernel(n_chunks, group, place, *refs):
@@ -185,9 +196,9 @@
 
 
 def weights(sums, plan, grad_dots, scale):
-    mass = sums[0:1, :]
+    mass = row_of(sums, 0)
     shared = plan / mass
-    weighted = scale * (shared * (grad_dots - sums[1:2, :] / mass))
+    weighted = scale * (shared * (grad_dots - row_of(sums, 1) / mass))
     return (shared, weighted)
 
 
@@ -209,16 +220,16 @@
     *total, out = refs
     here = slice(first, first + rows)
     tile = plan[here, :]
-    centred = tile * (grad_dots[here, :] - estimate[1:2, :] / estimate[0:1, :])
+    centred = tile * (grad_dots[here, :] - row_of(estimate, 1) / row_of(estimate, 0))
     term = dot3((high[...], low[...]), halves(jnp.concatenate([tile, centred], axis=1)))
     out[...] = total[0][...] + term if total else term
 
 
 def finish_kernel(n_text, scale, firsts, place, estimate, sums, total, plan, grad_dots, *refs):
     blocks, outs, terms = refs[: 2 * len(firsts)], refs[2 * len(firsts) : -1], refs[-1]
-    frames = sums.shape[1]
-    mass = sums[0:1, :]
-    drift = sums[1:2, :] / mass - estimate[1:2, :] / estimate[0:1, :]
+    frames = total.shape[1] // 2
+    mass = row_of(sums, 0)
+    drift = row_of(sums, 1) / mass - row_of(estimate, 1) / row_of(estimate, 0)
     for i, first in enumerate(firsts):
         high, low = blocks[2 * i : 2 * i + 2]
         here = slice(first, first + high.shape[1])
@@ -309,7 +320,8 @@
 
     half = n_speech // 2
     tile = ((half * rows, frames), jnp.float32)
-    outs = [tile, tile, ((8, frames), jnp.float32)]
+    sums_shape = ((2 * frames // LANES, LANES), jnp.float32)
+    outs = [tile, tile, sums_shape]
     left_shape = ((feats, 2 * frames), jnp.bfloat16)
     plan_early, dots_early, sums, *left = call(
         functools.partial(early_kernel, n_text - known, len(partials[:half]), group, scale),
@@ -350,7 +362,7 @@
                     before=[sums],
                 )
             crossing = swap(sums, "text", step)
-            sums = call(add_kernel, "hop", [sums, crossing], ((8, frames), jnp.float32), before=total)
+            sums = call(add_kernel, "hop", [sums, crossing], sums_shape, before=total)
             step *= 2
     while step < n_text:
         sums = sums + swap(sums, "text", step)

time: 88.5 us -> 88.4 us (level)
  transfers between devices with their start and end apart: 22 -> 22, of which waited for: 11 -> 10; matrix products, arithmetic and copies ran while one was open for 1% -> 1% of each run, Pallas kernels for 29% -> 29%
where the time goes in v4:
time: 88.4 us; the launch traced here: 88.2 us
  Pallas kernels  32.4 us (37%)
  starting transfers between devices  28.1 us (32%)
  waiting for transfers between devices  25.5 us (29%)
  other arithmetic  1.27 us (1%)
  between operations  0.91 us (1%)
    pallas_call x28, Pallas kernels, call(): pl.pallas_call(body, in_specs=[IN_SMEM] * places + [IN_VMEM] * (count - p...  32.4 us
    ppermute x22, starting transfers between devices, swap(): return lax.ppermute(value, axis, [(i, i ^ k) for i in range(count)])  28.1 us
    ppermute x22, waiting for transfers between devices, swap(): return lax.ppermute(value, axis, [(i, i ^ k) for i in range(count)])  25.5 us
  transfers between devices with their start and end apart: 22, of which 10 were waited for; matrix products, arithmetic and copies ran while one was open for 1% of the time, Pallas kernels for 29%

profile of v4, /device:TPU:0, one launch (start us, length us, event | category | flops | bytes accessed | tf_op | source)
XLA Modules:
  0.0 88.2 jit_solution(18416572484768404458)
XLA Ops:
  0.7 0.5 collective-permute-start
  1.2 2.6 %collective-permute-start.8 = (f32[512,512]{1,0:T(8,128)}, f32[512,512]{1,0:T(8,128)}, u32[]{:S(2)}, u32[]{:S(2)}) collective-permute-start(f32[512,512]{1,0:T(8,128)} %refs_1_.1), channel_id=1, source_target_pairs={{0,16},{8,24},{16,0},{24,8},{1,17},{9,25},{17,1},{25,9},{2,18},{10... | collective-permute-start | bytes 3145736 | tf_op jit(solution)/shard_map/ppermute | solution.py:269
  3.8 1.0 %pad_maximum_fusion.refs_0_ = f32[128,512]{1,0:T(8,128)S(1)} fusion(f32[64,512]{1,0:T(8,128)} %bitcast.9, f32[64,512]{1,0:T(8,128)} %bitcast.10), kind=kLoop, calls=%fused_computation | loop fusion | flops 65536 | bytes 524288 | tf_op jit(solution)/shard_map/concatenate | solution.py:287
  4.8 0.0 collective-permute-done.refs_1_
  4.8 1.9 %collective-permute-start.2 = (f32[128,512]{1,0:T(8,128)S(1)}, f32[128,512]{1,0:T(8,128)S(1)}, u32[]{:S(2)}, u32[]{:S(2)}) collective-permute-start(f32[128,512]{1,0:T(8,128)S(1)} %copy.9.refs_1_), channel_id=1, source_target_pairs={{0,2},{1,3},{2,0},{3,1},{4,6},{5,7},{6,4},{7,5},{8,10},{9,11},{10,... | collective-permute-start | bytes 786440 | tf_op jit(solution)/shard_map/ppermute | solution.py:269
  6.7 1.5 %collective-permute-start.1 = (f32[128,512]{1,0:T(8,128)S(1)}, f32[128,512]{1,0:T(8,128)S(1)}, u32[]{:S(2)}, u32[]{:S(2)}) collective-permute-start(f32[128,512]{1,0:T(8,128)S(1)} %copy.9.refs_1_), channel_id=1, source_target_pairs={{0,1},{1,0},{2,3},{3,2},{4,5},{5,4},{6,7},{7,6},{8,9},{9,8},{10,11... | collective-permute-start | bytes 786440 | tf_op jit(solution)/shard_map/ppermute | solution.py:269
  8.2 2.6 %collective-permute-start.4 = (f32[128,512]{1,0:T(8,128)S(1)}, f32[128,512]{1,0:T(8,128)S(1)}, u32[]{:S(2)}, u32[]{:S(2)}) collective-permute-start(f32[128,512]{1,0:T(8,128)S(1)} %copy.9.refs_1_), channel_id=1, source_target_pairs={{0,4},{1,5},{2,6},{3,7},{4,0},{5,1},{6,2},{7,3},{8,12},{9,13},{10,... | collective-permute-start | bytes 786440 | tf_op jit(solution)/shard_map/ppermute | solution.py:269
  10.8 0.1 pad_add_fusion.refs_0_
  10.9 0.9 offsets.1.refs_3_.refs_1_.refs_0_
  11.8 0.9 %split.4 = (bf16[512,512]{1,0:T(8,128)(2,1)S(1)}, bf16[512,512]{1,0:T(8,128)(2,1)S(1)}, bf16[512,512]{1,0:T(8,128)(2,1)S(1)}, bf16[512,512]{1,0:T(8,128)(2,1)S(1)}) custom-call(s32[2]{0:T(128)S(1)} %pad_add_fusion.refs_0_, f32[512,512]{1,0:T(8,128)S(1)} %copy-done), custom_call_target="tpu_custom_call" | custom-call | flops 1000000000 | tf_op jit(solution)/shard_map/split/pallas_call | solution.py:52
  12.7 4.9 %collective-permute-done.2.refs_3_.refs_2_ = f32[128,512]{1,0:T(8,128)S(1)} collective-permute-done((f32[128,512]{1,0:T(8,128)S(1)}, f32[128,512]{1,0:T(8,128)S(1)}, u32[]{:S(2)}, u32[]{:S(2)}) %collective-permute-start.2) | collective-permute-done | bytes 262176 | tf_op jit(solution)/shard_map/ppermute | solution.py:269
  17.6 2.6 %collective-permute-start.3 = (f32[128,512]{1,0:T(8,128)S(1)}, f32[128,512]{1,0:T(8,128)S(1)}, u32[]{:S(2)}, u32[]{:S(2)}) collective-permute-start(f32[128,512]{1,0:T(8,128)S(1)} %collective-permute-done.2.refs_3_.refs_2_), channel_id=1, source_target_pairs={{0,1},{1,0},{2,3},{3,2},{4,5},{5,4},{6,7},{7,6},{8,9},{9,8},{10,11... | collective-permute-start | bytes 786440 | tf_op jit(solution)/shard_map/ppermute | solution.py:269
  20.2 0.9 %split.5 = (bf16[512,512]{1,0:T(8,128)(2,1)S(1)}, bf16[512,512]{1,0:T(8,128)(2,1)S(1)}, bf16[512,512]{1,0:T(8,128)(2,1)S(1)}, bf16[512,512]{1,0:T(8,128)(2,1)S(1)}) custom-call(s32[2]{0:T(128)S(1)} %pad_add_fusion.refs_0_, f32[512,512]{1,0:T(8,128)S(1)} %collective-permute-done.refs_1_), custom_call_target="tpu_custom_call" | custom-call | flops 1000000000 | tf_op jit(solution)/shard_map/split/pallas_call | solution.py:52
  21.1 0.0 collective-permute-done.1.refs_2_.refs_1_
  21.1 1.4 %collective-permute-done.4.refs_0_.refs_4_ = f32[128,512]{1,0:T(8,128)S(1)} collective-permute-done((f32[128,512]{1,0:T(8,128)S(1)}, f32[128,512]{1,0:T(8,128)S(1)}, u32[]{:S(2)}, u32[]{:S(2)}) %collective-permute-start.4) | collective-permute-done | bytes 262176 | tf_op jit(solution)/shard_map/ppermute | solution.py:269
  22.6 0.1 collective-permute-start.6
  22.7 0.7 collective-permute-start.5
  23.4 4.0 %collective-permute-done.3.refs_4_ = f32[128,512]{1,0:T(8,128)S(1)} collective-permute-done((f32[128,512]{1,0:T(8,128)S(1)}, f32[128,512]{1,0:T(8,128)S(1)}, u32[]{:S(2)}, u32[]{:S(2)}) %collective-permute-start.3) | collective-permute-done | bytes 262176 | tf_op jit(solution)/shard_map/ppermute | solution.py:269
  27.4 2.5 %plan_part.1 = (f32[512,1024]{1,0:T(8,128)S(1)}, f32[512,1024]{1,0:T(8,128)S(1)}, bf16[256,1024]{1,0:T(8,128)(2,1)S(1)}, bf16[256,1024]{1,0:T(8,128)(2,1)S(1)}) custom-call(s32[2]{0:T(128)S(1)} %pad_add_fusion.refs_0_, f32[128,512]{1,0:T(8,128)S(1)} %copy.9.refs_1_, f32[128,512]{1,0:T(8,128)S(1)} %collective-permute-done.1.refs_2_.refs_1_, ...), custom_call_target="tpu_custom_call" | custom-call | flops 1000000000 | tf_op jit(solution)/shard_map/plan_part/pallas_call | solution.py:52
  29.9 0.0 collective-permute-done.6.refs_0_.refs_6_
  29.9 2.1 %collective-permute-start.7 = (f32[128,512]{1,0:T(8,128)S(1)}, f32[128,512]{1,0:T(8,128)S(1)}, u32[]{:S(2)}, u32[]{:S(2)}) collective-permute-start(f32[128,512]{1,0:T(8,128)S(1)} %copy.11), channel_id=1, source_target_pairs={{0,1},{1,0},{2,3},{3,2},{4,5},{5,4},{6,7},{7,6},{8,9},{9,8},{10,11... | collective-permute-start | bytes 786440 | tf_op jit(solution)/shard_map/ppermute | solution.py:269
  32.0 0.0 collective-permute-done.8.refs_1_
  32.0 0.0 collective-permute-start.9
  32.0 1.6 %split.6 = (bf16[512,512]{1,0:T(8,128)(2,1)S(1)}, bf16[512,512]{1,0:T(8,128)(2,1)S(1)}, bf16[512,512]{1,0:T(8,128)(2,1)S(1)}, bf16[512,512]{1,0:T(8,128)(2,1)S(1)}) custom-call(s32[2]{0:T(128)S(1)} %pad_add_fusion.refs_0_, f32[512,512]{1,0:T(8,128)} %collective-permute-done.8.refs_1_), custom_call_target="tpu_custom_call" | custom-call | flops 1000000000 | tf_op jit(solution)/shard_map/split/pallas_call | solution.py:52
  33.6 1.0 %plan_more.1.refs_4_ = f32[512,1024]{1,0:T(8,128)S(1)} custom-call(bf16[256,1024]{1,0:T(8,128)(2,1)S(1)} %get-tuple-element.50.refs_1_.refs_2_.refs_0_, bf16[256,1024]{1,0:T(8,128)(2,1)S(1)} %get-tuple-element.51.refs_3_.refs_1_, bf16[512,512]{1,0:T(8,128)(2,1)S(1)} %get-tuple-element.57.refs_2_.refs_5_, bf16[512,512]{1,0:T(8,128)(2,1)S(1)} %get-tuple-element.58.refs_3_.refs_7_), custom_call_target="tpu_custom_call" | custom-call | flops 1000000000 | tf_op jit(solution)/shard_map/plan_more/pallas_call | solution.py:52
  34.6 0.0 collective-permute-done.5.refs_5_
  34.6 2.7 %collective-permute-done.7.refs_7_ = f32[128,512]{1,0:T(8,128)S(1)} collective-permute-done((f32[128,512]{1,0:T(8,128)S(1)}, f32[128,512]{1,0:T(8,128)S(1)}, u32[]{:S(2)}, u32[]{:S(2)}) %collective-permute-start.7) | collective-permute-done | bytes 262176 | tf_op jit(solution)/shard_map/ppermute | solution.py:269
  37.3 3.0 %plan_early.1 = (f32[1024,512]{1,0:T(8,128)S(1)}, f32[1024,512]{1,0:T(8,128)S(1)}, f32[8,128]{1,0:T(8,128)S(1)}, bf16[512,1024]{1,0:T(8,128)(2,1)S(1)}, bf16[512,1024]{1,0:T(8,128)(2,1)S(1)}) custom-call(s32[2]{0:T(128)S(1)} %pad_add_fusion.refs_0_, f32[2048,128]{1,0:T(8,128)S(1)} %offsets.1.refs_3_.refs_1_.refs_0_, ...), custom_call_target="tpu_custom_call" | custom-call | flops 99999997952 | tf_op jit(solution)/shard_map/plan_early/pallas_call | solution.py:52
  40.3 0.0 collective-permute-done.9.refs_1_
  40.3 0.9 %split.7 = (bf16[512,512]{1,0:T(8,128)(2,1)S(1)}, bf16[512,512]{1,0:T(8,128)(2,1)S(1)}, bf16[512,512]{1,0:T(8,128)(2,1)S(1)}, bf16[512,512]{1,0:T(8,128)(2,1)S(1)}) custom-call(s32[2]{0:T(128)S(1)} %pad_add_fusion.refs_0_, f32[512,512]{1,0:T(8,128)S(1)} %collective-permute-done.9.refs_1_), custom_call_target="tpu_custom_call" | custom-call | flops 1000000000 | tf_op jit(solution)/shard_map/split/pallas_call | solution.py:52
  41.2 2.8 %plan_late.1 = (f32[1024,512]{1,0:T(8,128)S(1)}, f32[1024,512]{1,0:T(8,128)S(1)}, f32[8,128]{1,0:T(8,128)S(1)}) custom-call(f32[2048,128]{1,0:T(8,128)S(1)} %offsets.1.refs_3_.refs_1_.refs_0_, f32[8,128]{1,0:T(8,128)S(1)} %get-tuple-element.54.refs_1_, bf16[512,1024]{1,0:T(8,128)(2,1)S(1)} %get-tuple-element.55.refs_2_.refs_1_, ...), custom_call_target="tpu_custom_call" | custom-call | flops 3000000000 | tf_op jit(solution)/shard_map/plan_late/pallas_call | solution.py:52
  44.1 1.8 %collective-permute-start.10 = (f32[8,128]{1,0:T(8,128)S(1)}, f32[8,128]{1,0:T(8,128)S(1)}, u32[]{:S(2)}, u32[]{:S(2)}) collective-permute-start(f32[8,128]{1,0:T(8,128)S(1)} %get-tuple-element.61.refs_0_.refs_5_.refs_1_), channel_id=1, source_target_pairs={{0,1},{1,0},{2,3},{3,2},{4,5},{5,4},{6,7},{7,6},{8,9},{9,8},{10,11... | collective-permute-start | bytes 12296 | tf_op jit(solution)/shard_map/ppermute | solution.py:269
  45.9 1.9 %moments.3.refs_2_.refs_5_ = f32[512,1024]{1,0:T(8,128)S(1)} custom-call(f32[8,128]{1,0:T(8,128)S(1)} %get-tuple-element.61.refs_0_.refs_5_.refs_1_, f32[1024,512]{1,0:T(8,128)S(1)} %get-tuple-element.62.refs_1_, f32[1024,512]{1,0:T(8,128)S(1)} %get-tuple-element.63.refs_2_, bf16[512,512]{1,0:T(8,128)(2,1)S(1)} %get-tuple-element.64.refs_3_, ...), custom_call_target="tpu_custom_call" | custom-call | flops 6000000000 | tf_op jit(solution)/shard_map/moments/pallas_call | solution.py:52
  47.7 0.0 collective-permute-done.10.refs_1_
  47.7 0.1 collective-permute-start.11
  47.8 1.9 %moments.4.refs_2_.refs_5_ = f32[512,1024]{1,0:T(8,128)S(1)} custom-call(f32[8,128]{1,0:T(8,128)S(1)} %get-tuple-element.61.refs_0_.refs_5_.refs_1_, f32[1024,512]{1,0:T(8,128)S(1)} %get-tuple-element.62.refs_1_, f32[1024,512]{1,0:T(8,128)S(1)} %get-tuple-element.63.refs_2_, bf16[512,512]{1,0:T(8,128)(2,1)S(1)} %get-tuple-element.66.refs_3_, ...), custom_call_target="tpu_custom_call" | custom-call | flops 6000000000 | tf_op jit(solution)/shard_map/moments/pallas_call | solution.py:52
  49.7 1.8 %collective-permute-done.11.refs_1_ = f32[8,128]{1,0:T(8,128)S(1)} collective-permute-done((f32[8,128]{1,0:T(8,128)S(1)}, f32[8,128]{1,0:T(8,128)S(1)}, u32[]{:S(2)}, u32[]{:S(2)}) %collective-permute-start.11) | collective-permute-done | bytes 4128 | tf_op jit(solution)/shard_map/ppermute | solution.py:269
  51.5 1.3 %collective-permute-start.12 = (f32[8,128]{1,0:T(8,128)S(1)}, f32[8,128]{1,0:T(8,128)S(1)}, u32[]{:S(2)}, u32[]{:S(2)}) collective-permute-start(f32[8,128]{1,0:T(8,128)S(1)} %hop.4.refs_6_.refs_0_.refs_3_), channel_id=1, source_target_pairs={{0,4},{1,5},{2,6},{3,7},{4,0},{5,1},{6,2},{7,3},{8,12},{9,13},{10,... | collective-permute-start | bytes 12296 | tf_op jit(solution)/shard_map/ppermute | solution.py:269
  52.8 2.1 %moments.5.refs_2_.refs_3_ = f32[512,1024]{1,0:T(8,128)S(1)} custom-call(f32[8,128]{1,0:T(8,128)S(1)} %get-tuple-element.61.refs_0_.refs_5_.refs_1_, f32[1024,512]{1,0:T(8,128)S(1)} %get-tuple-element.68.refs_1_.refs_4_, f32[1024,512]{1,0:T(8,128)S(1)} %get-tuple-element.69.refs_2_.refs_5_, bf16[512,512]{1,0:T(8,128)(2,1)S(1)} %get-tuple-element.70.refs_3_, ...), custom_call_target="tpu_custom_call" | custom-call | flops 6000000000 | tf_op jit(solution)/shard_map/moments/pallas_call | solution.py:52
  54.9 1.5 %frames_first.1 = (bf16[1024,512]{1,0:T(8,128)(2,1)S(1)}, bf16[1024,512]{1,0:T(8,128)(2,1)S(1)}) custom-call(s32[2]{0:T(128)S(1)} %pad_add_fusion.refs_0_, bf16[512,1024]{1,0:T(8,128)(2,1)S(1)} %get-tuple-element.55.refs_2_.refs_1_, bf16[512,1024]{1,0:T(8,128)(2,1)S(1)} %get-tuple-element.56.refs_3_.refs_2_, f32[8,128]{1,0:T(8,128)S(1)} %hop.4.refs_6_.refs_0_.refs_3_), custom_call_target="tpu_custom_call" | custom-call | flops 1000000000 | tf_op jit(solution)/shard_map/frames_first/pallas_call | solution.py:52
  56.4 0.0 collective-permute-done.12.refs_1_
  56.4 1.9 %text_far.2.refs_8_.refs_5_ = f32[512,512]{1,0:T(8,128)S(1)} custom-call(f32[8,128]{1,0:T(8,128)S(1)} %hop.5.refs_0_.refs_2_, f32[1024,512]{1,0:T(8,128)S(1)} %get-tuple-element.68.refs_1_.refs_4_, f32[1024,512]{1,0:T(8,128)S(1)} %get-tuple-element.69.refs_2_.refs_5_, bf16[1024,512]{1,0:T(8,128)(2,1)S(1)} %get-tuple-element.74.refs_3_, ...), custom_call_target="tpu_custom_call" | custom-call | tf_op jit(solution)/shard_map/text_far/pallas_call | solution.py:52
  58.3 0.1 collective-permute-start.20
  58.4 1.9 %text_far.3 = f32[512,512]{1,0:T(8,128)S(1)} custom-call(f32[8,128]{1,0:T(8,128)S(1)} %hop.5.refs_0_.refs_2_, f32[1024,512]{1,0:T(8,128)S(1)} %get-tuple-element.68.refs_1_.refs_4_, f32[1024,512]{1,0:T(8,128)S(1)} %get-tuple-element.69.refs_2_.refs_5_, bf16[1024,512]{1,0:T(8,128)(2,1)S(1)} %get-tuple-element.74.refs_3_, ...), custom_call_target="tpu_custom_call" | custom-call | tf_op jit(solution)/shard_map/text_far/pallas_call | solution.py:52
  60.3 0.8 collective-permute-done.20
  61.0 0.2 add.4.refs_7_
  61.2 1.6 %collective-permute-start.21 = (f32[512,512]{1,0:T(8,128)S(1)}, f32[512,512]{1,0:T(8,128)S(1)}, u32[]{:S(2)}, u32[]{:S(2)}) collective-permute-start(f32[512,512]{1,0:T(8,128)S(1)} %add.4.refs_7_), channel_id=1, source_target_pairs={{0,16},{8,24},{16,0},{24,8},{1,17},{9,25},{17,1},{25,9},{2,18},{10... | collective-permute-start | bytes 3145736 | tf_op jit(solution)/shard_map/ppermute | solution.py:269
  62.8 1.8 %finish.1 = (f32[4,64,256]{2,1,0:T(8,128)S(1)}, f32[4,64,256]{2,1,0:T(8,128)S(1)}, f32[4,64,256]{2,1,0:T(8,128)S(1)}, f32[4,64,256]{2,1,0:T(8,128)S(1)}) custom-call(s32[2]{0:T(128)S(1)} %pad_add_fusion.refs_0_, f32[8,128]{1,0:T(8,128)S(1)} %get-tuple-element.61.refs_0_.refs_5_.refs_1_, f32[8,128]{1,0:T(8,128)S(1)} %hop.5.refs_0_.refs_2_, ...), custom_call_target="tpu_custom_call" | custom-call | tf_op jit(solution)/shard_map/finish/pallas_call | solution.py:52
  64.7 1.7 %collective-permute-start.13 = (f32[4,64,256]{2,1,0:T(8,128)S(1)}, f32[4,64,256]{2,1,0:T(8,128)S(1)}, u32[]{:S(2)}, u32[]{:S(2)}) collective-permute-start(f32[4,64,256]{2,1,0:T(8,128)S(1)} %get-tuple-element.77), channel_id=1, source_target_pairs={{0,1},{1,0},{2,3},{3,2},{4,5},{5,4},{6,7},{7,6},{8,9},{9,8},{10,11... | collective-permute-start | bytes 786440 | tf_op jit(solution)/shard_map/ppermute | solution.py:269
  66.4 1.7 %collective-permute-start.15 = (f32[4,64,256]{2,1,0:T(8,128)S(1)}, f32[4,64,256]{2,1,0:T(8,128)S(1)}, u32[]{:S(2)}, u32[]{:S(2)}) collective-permute-start(f32[4,64,256]{2,1,0:T(8,128)S(1)} %get-tuple-element.81), channel_id=1, source_target_pairs={{0,2},{1,3},{2,0},{3,1},{4,6},{5,7},{6,4},{7,5},{8,10},{9,11},{10,... | collective-permute-start | bytes 786440 | tf_op jit(solution)/shard_map/ppermute | solution.py:269
  68.0 1.9 %text_near.2 = (f32[256,512]{1,0:T(8,128)S(1)}, f32[256,512]{1,0:T(8,128)S(1)}) custom-call(f32[8,128]{1,0:T(8,128)S(1)} %hop.5.refs_0_.refs_2_, f32[1024,512]{1,0:T(8,128)S(1)} %get-tuple-element.62.refs_1_, f32[1024,512]{1,0:T(8,128)S(1)} %get-tuple-element.63.refs_2_, bf16[1024,512]{1,0:T(8,128)(2,1)S(1)} %get-tuple-element.74.refs_3_, ...), custom_call_target="tpu_custom_call" | custom-call | tf_op jit(solution)/shard_map/text_near/pallas_call | solution.py:52
  69.9 0.1 collective-permute-start.18
  70.0 0.5 collective-permute-start.19
  70.5 2.3 %collective-permute-done.13.refs_1_ = f32[4,64,256]{2,1,0:T(8,128)S(1)} collective-permute-done((f32[4,64,256]{2,1,0:T(8,128)S(1)}, f32[4,64,256]{2,1,0:T(8,128)S(1)}, u32[]{:S(2)}, u32[]{:S(2)}) %collective-permute-start.13) | collective-permute-done | bytes 262176 | tf_op jit(solution)/shard_map/ppermute | solution.py:269
  72.8 1.8 %collective-permute-start.14 = (f32[2,64,256]{2,1,0:T(8,128)S(1)}, f32[2,64,256]{2,1,0:T(8,128)S(1)}, u32[]{:S(2)}, u32[]{:S(2)}) collective-permute-start(f32[2,64,256]{2,1,0:T(8,128)S(1)} %get-tuple-element.79), channel_id=1, source_target_pairs={{0,2},{1,3},{2,0},{3,1},{4,6},{5,7},{6,4},{7,5},{8,10},{9,11},{10,... | collective-permute-start | bytes 393224 | tf_op jit(solution)/shard_map/ppermute | solution.py:269
  74.6 0.0 collective-permute-done.15.refs_1_
  74.6 1.7 %collective-permute-start.16 = (f32[2,64,256]{2,1,0:T(8,128)S(1)}, f32[2,64,256]{2,1,0:T(8,128)S(1)}, u32[]{:S(2)}, u32[]{:S(2)}) collective-permute-start(f32[2,64,256]{2,1,0:T(8,128)S(1)} %get-tuple-element.83), channel_id=1, source_target_pairs={{0,1},{1,0},{2,3},{3,2},{4,5},{5,4},{6,7},{7,6},{8,9},{9,8},{10,11... | collective-permute-start | bytes 393224 | tf_op jit(solution)/shard_map/ppermute | solution.py:269
  76.3 1.5 %collective-permute-done.14.refs_1_ = f32[2,64,256]{2,1,0:T(8,128)S(1)} collective-permute-done((f32[2,64,256]{2,1,0:T(8,128)S(1)}, f32[2,64,256]{2,1,0:T(8,128)S(1)}, u32[]{:S(2)}, u32[]{:S(2)}) %collective-permute-start.14) | collective-permute-done | bytes 131104 | tf_op jit(solution)/shard_map/ppermute | solution.py:269
  77.9 1.8 %collective-permute-done.16.refs_3_ = f32[2,64,256]{2,1,0:T(8,128)S(1)} collective-permute-done((f32[2,64,256]{2,1,0:T(8,128)S(1)}, f32[2,64,256]{2,1,0:T(8,128)S(1)}, u32[]{:S(2)}, u32[]{:S(2)}) %collective-permute-start.16) | collective-permute-done | bytes 131104 | tf_op jit(solution)/shard_map/ppermute | solution.py:269
  79.7 1.2 %collective-permute-start.17 = (f32[64,512]{1,0:T(8,128)S(1)}, f32[64,512]{1,0:T(8,128)S(1)}, u32[]{:S(2)}, u32[]{:S(2)}) collective-permute-start(f32[64,512]{1,0:T(8,128)S(1)} %bitcast.8), channel_id=1, source_target_pairs={{0,4},{1,5},{2,6},{3,7},{4,0},{5,1},{6,2},{7,3},{8,12},{9,13},{10,... | collective-permute-start | bytes 393224 | tf_op jit(solution)/shard_map/ppermute | solution.py:269
  80.9 0.0 collective-permute-done.18.refs_5_
  80.9 1.9 %text_near.3.refs_2_ = f32[512,512]{1,0:T(8,128)S(1)} custom-call(f32[8,128]{1,0:T(8,128)S(1)} %hop.5.refs_0_.refs_2_, f32[1024,512]{1,0:T(8,128)S(1)} %get-tuple-element.62.refs_1_, f32[1024,512]{1,0:T(8,128)S(1)} %get-tuple-element.63.refs_2_, bf16[1024,512]{1,0:T(8,128)(2,1)S(1)} %get-tuple-element.74.refs_3_, ...), custom_call_target="tpu_custom_call" | custom-call | tf_op jit(solution)/shard_map/text_near/pallas_call | solution.py:52
  82.8 4.3 %collective-permute-done.17.refs_1_ = f32[64,512]{1,0:T(8,128)S(1)} collective-permute-done((f32[64,512]{1,0:T(8,128)S(1)}, f32[64,512]{1,0:T(8,128)S(1)}, u32[]{:S(2)}, u32[]{:S(2)}) %collective-permute-start.17) | collective-permute-done | bytes 131104 | tf_op jit(solution)/shard_map/ppermute | solution.py:269
  87.0 1.2 %add.7 = (f32[512,512]{1,0:T(8,128)}, f32[64,512]{1,0:T(8,128)}) custom-call(f32[64,512]{1,0:T(8,128)S(1)} %bitcast.7, f32[64,512]{1,0:T(8,128)S(1)} %collective-permute-done.17.refs_1_, f32[512,512]{1,0:T(8,128)S(1)} %text_near.3.refs_2_, f32[512,512]{1,0:T(8,128)S(1)} %collective-permute-done.21.refs_3_), custom_call_target="tpu_custom_call" | custom-call | flops 99999997952 | tf_op jit(solution)/shard_map/add/pallas_call | solution.py:52
  (16 shorter events, 0.2 us)
Async XLA Ops:
  0.6 11.1 %copy-start = (f32[512,512]{1,0:T(8,128)S(1)}, f32[512,512]{1,0:T(8,128)}, u32[]{:S(2)}) copy-start(f32[512,512]{1,0:T(8,128)} %refs_1_.1) | copy-start | bytes 3145732
  0.6 6.1 %copy-start.1 = (f32[2048]{0:T(1024)S(1)}, f32[2048]{0:T(1024)}, u32[]{:S(2)}) copy-start(f32[2048]{0:T(1024)} %param.6) | copy-start | bytes 24580
  0.7 4.1 %collective-permute-start = (f32[512,512]{1,0:T(8,128)}, f32[512,512]{1,0:T(8,128)S(1)}, u32[]{:S(2)}, u32[]{:S(2)}) collective-permute-start(f32[512,512]{1,0:T(8,128)} %refs_1_.1), channel_id=1, source_target_pairs={{0,8},{8,0},{16,24},{24,16},{1,9},{9,1},{17,25},{25,17},{2,10},{10... | collective-permute-start | bytes 3145736 | tf_op jit(solution)/shard_map/ppermute | solution.py:269
  1.2 30.9 %collective-permute-start.8 = (f32[512,512]{1,0:T(8,128)}, f32[512,512]{1,0:T(8,128)}, u32[]{:S(2)}, u32[]{:S(2)}) collective-permute-start(f32[512,512]{1,0:T(8,128)} %refs_1_.1), channel_id=1, source_target_pairs={{0,16},{8,24},{16,0},{24,8},{1,17},{9,25},{17,1},{25,9},{2,18},{10... | collective-permute-start | bytes 3145736 | tf_op jit(solution)/shard_map/ppermute | solution.py:269
  4.8 12.8 %collective-permute-start.2 = (f32[128,512]{1,0:T(8,128)S(1)}, f32[128,512]{1,0:T(8,128)S(1)}, u32[]{:S(2)}, u32[]{:S(2)}) collective-permute-start(f32[128,512]{1,0:T(8,128)S(1)} %copy.9.refs_1_), channel_id=1, source_target_pairs={{0,2},{1,3},{2,0},{3,1},{4,6},{5,7},{6,4},{7,5},{8,10},{9,11},{10,... | collective-permute-start | bytes 786440 | tf_op jit(solution)/shard_map/ppermute | solution.py:269
  6.7 14.4 %collective-permute-start.1 = (f32[128,512]{1,0:T(8,128)S(1)}, f32[128,512]{1,0:T(8,128)S(1)}, u32[]{:S(2)}, u32[]{:S(2)}) collective-permute-start(f32[128,512]{1,0:T(8,128)S(1)} %copy.9.refs_1_), channel_id=1, source_target_pairs={{0,1},{1,0},{2,3},{3,2},{4,5},{5,4},{6,7},{7,6},{8,9},{9,8},{10,11... | collective-permute-start | bytes 786440 | tf_op jit(solution)/shard_map/ppermute | solution.py:269
  8.2 14.4 %collective-permute-start.4 = (f32[128,512]{1,0:T(8,128)S(1)}, f32[128,512]{1,0:T(8,128)S(1)}, u32[]{:S(2)}, u32[]{:S(2)}) collective-permute-start(f32[128,512]{1,0:T(8,128)S(1)} %copy.9.refs_1_), channel_id=1, source_target_pairs={{0,4},{1,5},{2,6},{3,7},{4,0},{5,1},{6,2},{7,3},{8,12},{9,13},{10,... | collective-permute-start | bytes 786440 | tf_op jit(solution)/shard_map/ppermute | solution.py:269
  17.6 9.8 %collective-permute-start.3 = (f32[128,512]{1,0:T(8,128)S(1)}, f32[128,512]{1,0:T(8,128)S(1)}, u32[]{:S(2)}, u32[]{:S(2)}) collective-permute-start(f32[128,512]{1,0:T(8,128)S(1)} %collective-permute-done.2.refs_3_.refs_2_), channel_id=1, source_target_pairs={{0,1},{1,0},{2,3},{3,2},{4,5},{5,4},{6,7},{7,6},{8,9},{9,8},{10,11... | collective-permute-start | bytes 786440 | tf_op jit(solution)/shard_map/ppermute | solution.py:269
  22.6 7.3 %collective-permute-start.6 = (f32[128,512]{1,0:T(8,128)S(1)}, f32[128,512]{1,0:T(8,128)S(1)}, u32[]{:S(2)}, u32[]{:S(2)}) collective-permute-start(f32[128,512]{1,0:T(8,128)S(1)} %copy.10), channel_id=1, source_target_pairs={{0,2},{1,3},{2,0},{3,1},{4,6},{5,7},{6,4},{7,5},{8,10},{9,11},{10,... | collective-permute-start | bytes 786440 | tf_op jit(solution)/shard_map/ppermute | solution.py:269
  22.7 12.0 %collective-permute-start.5 = (f32[128,512]{1,0:T(8,128)S(1)}, f32[128,512]{1,0:T(8,128)S(1)}, u32[]{:S(2)}, u32[]{:S(2)}) collective-permute-start(f32[128,512]{1,0:T(8,128)S(1)} %collective-permute-done.4.refs_0_.refs_4_), channel_id=1, source_target_pairs={{0,1},{1,0},{2,3},{3,2},{4,5},{5,4},{6,7},{7,6},{8,9},{9,8},{10,11... | collective-permute-start | bytes 786440 | tf_op jit(solution)/shard_map/ppermute | solution.py:269
  29.9 7.4 %collective-permute-start.7 = (f32[128,512]{1,0:T(8,128)S(1)}, f32[128,512]{1,0:T(8,128)S(1)}, u32[]{:S(2)}, u32[]{:S(2)}) collective-permute-start(f32[128,512]{1,0:T(8,128)S(1)} %copy.11), channel_id=1, source_target_pairs={{0,1},{1,0},{2,3},{3,2},{4,5},{5,4},{6,7},{7,6},{8,9},{9,8},{10,11... | collective-permute-start | bytes 786440 | tf_op jit(solution)/shard_map/ppermute | solution.py:269
  32.0 8.2 %collective-permute-start.9 = (f32[512,512]{1,0:T(8,128)}, f32[512,512]{1,0:T(8,128)S(1)}, u32[]{:S(2)}, u32[]{:S(2)}) collective-permute-start(f32[512,512]{1,0:T(8,128)} %collective-permute-done.8.refs_1_), channel_id=1, source_target_pairs={{0,8},{8,0},{16,24},{24,16},{1,9},{9,1},{17,25},{25,17},{2,10},{10... | collective-permute-start | bytes 3145736 | tf_op jit(solution)/shard_map/ppermute | solution.py:269
  44.1 3.7 %collective-permute-start.10 = (f32[8,128]{1,0:T(8,128)S(1)}, f32[8,128]{1,0:T(8,128)S(1)}, u32[]{:S(2)}, u32[]{:S(2)}) collective-permute-start(f32[8,128]{1,0:T(8,128)S(1)} %get-tuple-element.61.refs_0_.refs_5_.refs_1_), channel_id=1, source_target_pairs={{0,1},{1,0},{2,3},{3,2},{4,5},{5,4},{6,7},{7,6},{8,9},{9,8},{10,11... | collective-permute-start | bytes 12296 | tf_op jit(solution)/shard_map/ppermute | solution.py:269
  47.7 3.7 %collective-permute-start.11 = (f32[8,128]{1,0:T(8,128)S(1)}, f32[8,128]{1,0:T(8,128)S(1)}, u32[]{:S(2)}, u32[]{:S(2)}) collective-permute-start(f32[8,128]{1,0:T(8,128)S(1)} %hop.3.refs_6_.refs_0_), channel_id=1, source_target_pairs={{0,2},{1,3},{2,0},{3,1},{4,6},{5,7},{6,4},{7,5},{8,10},{9,11},{10,... | collective-permute-start | bytes 12296 | tf_op jit(solution)/shard_map/ppermute | solution.py:269
  51.5 5.0 %collective-permute-start.12 = (f32[8,128]{1,0:T(8,128)S(1)}, f32[8,128]{1,0:T(8,128)S(1)}, u32[]{:S(2)}, u32[]{:S(2)}) collective-permute-start(f32[8,128]{1,0:T(8,128)S(1)} %hop.4.refs_6_.refs_0_.refs_3_), channel_id=1, source_target_pairs={{0,4},{1,5},{2,6},{3,7},{4,0},{5,1},{6,2},{7,3},{8,12},{9,13},{10,... | collective-permute-start | bytes 12296 | tf_op jit(solution)/shard_map/ppermute | solution.py:269
  58.3 2.7 %collective-permute-start.20 = (f32[512,512]{1,0:T(8,128)S(1)}, f32[512,512]{1,0:T(8,128)S(1)}, u32[]{:S(2)}, u32[]{:S(2)}) collective-permute-start(f32[512,512]{1,0:T(8,128)S(1)} %text_far.2.refs_8_.refs_5_), channel_id=1, source_target_pairs={{0,8},{8,0},{16,24},{24,16},{1,9},{9,1},{17,25},{25,17},{2,10},{10... | collective-permute-start | bytes 3145736 | tf_op jit(solution)/shard_map/ppermute | solution.py:269
  61.2 25.8 %collective-permute-start.21 = (f32[512,512]{1,0:T(8,128)S(1)}, f32[512,512]{1,0:T(8,128)S(1)}, u32[]{:S(2)}, u32[]{:S(2)}) collective-permute-start(f32[512,512]{1,0:T(8,128)S(1)} %add.4.refs_7_), channel_id=1, source_target_pairs={{0,16},{8,24},{16,0},{24,8},{1,17},{9,25},{17,1},{25,9},{2,18},{10... | collective-permute-start | bytes 3145736 | tf_op jit(solution)/shard_map/ppermute | solution.py:269
  64.7 8.1 %collective-permute-start.13 = (f32[4,64,256]{2,1,0:T(8,128)S(1)}, f32[4,64,256]{2,1,0:T(8,128)S(1)}, u32[]{:S(2)}, u32[]{:S(2)}) collective-permute-start(f32[4,64,256]{2,1,0:T(8,128)S(1)} %get-tuple-element.77), channel_id=1, source_target_pairs={{0,1},{1,0},{2,3},{3,2},{4,5},{5,4},{6,7},{7,6},{8,9},{9,8},{10,11... | collective-permute-start | bytes 786440 | tf_op jit(solution)/shard_map/ppermute | solution.py:269
  66.4 8.2 %collective-permute-start.15 = (f32[4,64,256]{2,1,0:T(8,128)S(1)}, f32[4,64,256]{2,1,0:T(8,128)S(1)}, u32[]{:S(2)}, u32[]{:S(2)}) collective-permute-start(f32[4,64,256]{2,1,0:T(8,128)S(1)} %get-tuple-element.81), channel_id=1, source_target_pairs={{0,2},{1,3},{2,0},{3,1},{4,6},{5,7},{6,4},{7,5},{8,10},{9,11},{10,... | collective-permute-start | bytes 786440 | tf_op jit(solution)/shard_map/ppermute | solution.py:269
  69.9 11.0 %collective-permute-start.18 = (f32[256,512]{1,0:T(8,128)S(1)}, f32[256,512]{1,0:T(8,128)S(1)}, u32[]{:S(2)}, u32[]{:S(2)}) collective-permute-start(f32[256,512]{1,0:T(8,128)S(1)} %get-tuple-element.86), channel_id=1, source_target_pairs={{0,8},{8,0},{16,24},{24,16},{1,9},{9,1},{17,25},{25,17},{2,10},{10... | collective-permute-start | bytes 1572872 | tf_op jit(solution)/shard_map/ppermute | solution.py:269
  70.0 10.9 %collective-permute-start.19 = (f32[256,512]{1,0:T(8,128)S(1)}, f32[256,512]{1,0:T(8,128)S(1)}, u32[]{:S(2)}, u32[]{:S(2)}) collective-permute-start(f32[256,512]{1,0:T(8,128)S(1)} %get-tuple-element.87), channel_id=1, source_target_pairs={{0,8},{8,0},{16,24},{24,16},{1,9},{9,1},{17,25},{25,17},{2,10},{10... | collective-permute-start | bytes 1572872 | tf_op jit(solution)/shard_map/ppermute | solution.py:269
  72.8 5.0 %collective-permute-start.14 = (f32[2,64,256]{2,1,0:T(8,128)S(1)}, f32[2,64,256]{2,1,0:T(8,128)S(1)}, u32[]{:S(2)}, u32[]{:S(2)}) collective-permute-start(f32[2,64,256]{2,1,0:T(8,128)S(1)} %get-tuple-element.79), channel_id=1, source_target_pairs={{0,2},{1,3},{2,0},{3,1},{4,6},{5,7},{6,4},{7,5},{8,10},{9,11},{10,... | collective-permute-start | bytes 393224 | tf_op jit(solution)/shard_map/ppermute | solution.py:269
  74.6 5.0 %collective-permute-start.16 = (f32[2,64,256]{2,1,0:T(8,128)S(1)}, f32[2,64,256]{2,1,0:T(8,128)S(1)}, u32[]{:S(2)}, u32[]{:S(2)}) collective-permute-start(f32[2,64,256]{2,1,0:T(8,128)S(1)} %get-tuple-element.83), channel_id=1, source_target_pairs={{0,1},{1,0},{2,3},{3,2},{4,5},{5,4},{6,7},{7,6},{8,9},{9,8},{10,11... | collective-permute-start | bytes 393224 | tf_op jit(solution)/shard_map/ppermute | solution.py:269
  79.7 7.3 %collective-permute-start.17 = (f32[64,512]{1,0:T(8,128)S(1)}, f32[64,512]{1,0:T(8,128)S(1)}, u32[]{:S(2)}, u32[]{:S(2)}) collective-permute-start(f32[64,512]{1,0:T(8,128)S(1)} %bitcast.8), channel_id=1, source_target_pairs={{0,4},{1,5},{2,6},{3,7},{4,0},{5,1},{6,2},{7,3},{8,12},{9,13},{10,... | collective-permute-start | bytes 393224 | tf_op jit(solution)/shard_map/ppermute | solution.py:269

commit v5 on v4

--- a/solution.py
+++ b/solution.py
@@ -230,12 +230,11 @@
     frames = total.shape[1] // 2
     mass = row_of(sums, 0)
     drift = row_of(sums, 1) / mass - row_of(estimate, 1) / row_of(estimate, 0)
-    for i, first in enumerate(firsts):
-        high, low = blocks[2 * i : 2 * i + 2]
-        here = slice(first, first + high.shape[1])
-        _, weighted = weights(sums, plan[here, :], grad_dots[here, :], scale)
-        term = dot3((high[...], low[...]), halves(weighted))
-        terms[...] = terms[...] + term if i else term
+    rows = blocks[0].shape[1]
+    here = slice(firsts[0], firsts[0] + len(firsts) * rows)
+    _, weighted = weights(sums, plan[here, :], grad_dots[here, :], scale)
+    text = [jnp.concatenate([block[...] for block in part], axis=1) for part in (blocks[::2], blocks[1::2])]
+    terms[...] = dot3(text, halves(weighted))
     width = total.shape[0] // n_text
     for k in range(n_text):
         here = pl.ds(pl.multiple_of((place[0] ^ k) * width, width), width)
@@ -341,7 +340,7 @@
     total = []
     step = 1
     for r in range(n_speech):
-        if r < n_speech - 1:
+        if r < n_speech - 2:
             total = [
                 call(
                     functools.partial(moments_kernel, r % half * rows, rows),
@@ -380,7 +379,7 @@
 
     shape = ((n_text // 2, width, frames // 2), jnp.float32)
 
-    direct = range(n_speech - 1, n_speech)
+    direct = range(n_speech - 2, n_speech)
     others = []
     for r in range(2, n_speech, 2):
         (term,) = text_part(r + 1, "text_far", [])

time: 88.4 us -> 88.2 us (level)
  waiting for transfers between devices: 25.5 us -> 29.3 us
  starting transfers between devices: 28.1 us -> 25.3 us
  Pallas kernels: 32.4 us -> 31.2 us
    ppermute x22, waiting for transfers between devices: 25.5 us -> 29.3 us  [swap(): return lax.ppermute(value, axis, [(i, i ^ k) for i in range(count)])]
    ppermute x22, starting transfers between devices: 28.1 us -> 25.3 us  [swap(): return lax.ppermute(value, axis, [(i, i ^ k) for i in range(count)])]
    pallas_call x28 -> x27, Pallas kernels: 32.4 us -> 31.2 us  [call(): pl.pallas_call(body, in_specs=[IN_SMEM] * places + [IN_VMEM] * (count - p...]
  transfers between devices with their start and end apart: 22 -> 22, of which waited for: 10 -> 12; matrix products, arithmetic and copies ran while one was open for 1% -> 1% of each run, Pallas kernels for 29% -> 28%
where the time goes in v5:
time: 88.2 us; the launch traced here: 88.1 us
  Pallas kernels  31.2 us (35%)
  waiting for transfers between devices  29.3 us (33%)
  starting transfers between devices  25.3 us (29%)
  other arithmetic  1.27 us (1%)
  between operations  0.9 us (1%)
    pallas_call x27, Pallas kernels, call(): pl.pallas_call(body, in_specs=[IN_SMEM] * places + [IN_VMEM] * (count - p...  31.2 us
    ppermute x22, waiting for transfers between devices, swap(): return lax.ppermute(value, axis, [(i, i ^ k) for i in range(count)])  29.3 us
    ppermute x22, starting transfers between devices, swap(): return lax.ppermute(value, axis, [(i, i ^ k) for i in range(count)])  25.3 us
  transfers between devices with their start and end apart: 22, of which 12 were waited for; matrix products, arithmetic and copies ran while one was open for 1% of the time, Pallas kernels for 28%

profile of v5, /device:TPU:0, one launch (start us, length us, event | category | flops | bytes accessed | tf_op | source)
XLA Modules:
  0.0 88.1 jit_solution(2316096772176611184)
XLA Ops:
  0.7 0.5 collective-permute-start
  1.2 2.6 %collective-permute-start.8 = (f32[512,512]{1,0:T(8,128)}, f32[512,512]{1,0:T(8,128)}, u32[]{:S(2)}, u32[]{:S(2)}) collective-permute-start(f32[512,512]{1,0:T(8,128)} %refs_1_.1), channel_id=1, source_target_pairs={{0,16},{8,24},{16,0},{24,8},{1,17},{9,25},{17,1},{25,9},{2,18},{10... | collective-permute-start | bytes 3145736 | tf_op jit(solution)/shard_map/ppermute | solution.py:268
  3.8 1.0 %pad_maximum_fusion.refs_0_ = f32[128,512]{1,0:T(8,128)S(1)} fusion(f32[64,512]{1,0:T(8,128)} %bitcast.9, f32[64,512]{1,0:T(8,128)} %bitcast.10), kind=kLoop, calls=%fused_computation | loop fusion | flops 65536 | bytes 524288 | tf_op jit(solution)/shard_map/concatenate | solution.py:286
  4.8 0.0 collective-permute-done.refs_1_
  4.8 1.9 %collective-permute-start.2 = (f32[128,512]{1,0:T(8,128)S(1)}, f32[128,512]{1,0:T(8,128)S(1)}, u32[]{:S(2)}, u32[]{:S(2)}) collective-permute-start(f32[128,512]{1,0:T(8,128)S(1)} %copy.9.refs_1_), channel_id=1, source_target_pairs={{0,2},{1,3},{2,0},{3,1},{4,6},{5,7},{6,4},{7,5},{8,10},{9,11},{10,... | collective-permute-start | bytes 786440 | tf_op jit(solution)/shard_map/ppermute | solution.py:268
  6.7 1.5 %collective-permute-start.1 = (f32[128,512]{1,0:T(8,128)S(1)}, f32[128,512]{1,0:T(8,128)S(1)}, u32[]{:S(2)}, u32[]{:S(2)}) collective-permute-start(f32[128,512]{1,0:T(8,128)S(1)} %copy.9.refs_1_), channel_id=1, source_target_pairs={{0,1},{1,0},{2,3},{3,2},{4,5},{5,4},{6,7},{7,6},{8,9},{9,8},{10,11... | collective-permute-start | bytes 786440 | tf_op jit(solution)/shard_map/ppermute | solution.py:268
  8.2 2.6 %collective-permute-start.4 = (f32[128,512]{1,0:T(8,128)S(1)}, f32[128,512]{1,0:T(8,128)S(1)}, u32[]{:S(2)}, u32[]{:S(2)}) collective-permute-start(f32[128,512]{1,0:T(8,128)S(1)} %copy.9.refs_1_), channel_id=1, source_target_pairs={{0,4},{1,5},{2,6},{3,7},{4,0},{5,1},{6,2},{7,3},{8,12},{9,13},{10,... | collective-permute-start | bytes 786440 | tf_op jit(solution)/shard_map/ppermute | solution.py:268
  10.8 0.1 pad_add_fusion.refs_0_
  10.9 0.9 offsets.1.refs_3_.refs_1_.refs_0_
  11.8 0.9 %split.4 = (bf16[512,512]{1,0:T(8,128)(2,1)S(1)}, bf16[512,512]{1,0:T(8,128)(2,1)S(1)}, bf16[512,512]{1,0:T(8,128)(2,1)S(1)}, bf16[512,512]{1,0:T(8,128)(2,1)S(1)}) custom-call(s32[2]{0:T(128)S(1)} %pad_add_fusion.refs_0_, f32[512,512]{1,0:T(8,128)S(1)} %copy-done), custom_call_target="tpu_custom_call" | custom-call | flops 1000000000 | tf_op jit(solution)/shard_map/split/pallas_call | solution.py:52
  12.7 4.9 %collective-permute-done.2.refs_3_.refs_2_ = f32[128,512]{1,0:T(8,128)S(1)} collective-permute-done((f32[128,512]{1,0:T(8,128)S(1)}, f32[128,512]{1,0:T(8,128)S(1)}, u32[]{:S(2)}, u32[]{:S(2)}) %collective-permute-start.2) | collective-permute-done | bytes 262176 | tf_op jit(solution)/shard_map/ppermute | solution.py:268
  17.6 2.6 %collective-permute-start.3 = (f32[128,512]{1,0:T(8,128)S(1)}, f32[128,512]{1,0:T(8,128)S(1)}, u32[]{:S(2)}, u32[]{:S(2)}) collective-permute-start(f32[128,512]{1,0:T(8,128)S(1)} %collective-permute-done.2.refs_3_.refs_2_), channel_id=1, source_target_pairs={{0,1},{1,0},{2,3},{3,2},{4,5},{5,4},{6,7},{7,6},{8,9},{9,8},{10,11... | collective-permute-start | bytes 786440 | tf_op jit(solution)/shard_map/ppermute | solution.py:268
  20.2 0.9 %split.5 = (bf16[512,512]{1,0:T(8,128)(2,1)S(1)}, bf16[512,512]{1,0:T(8,128)(2,1)S(1)}, bf16[512,512]{1,0:T(8,128)(2,1)S(1)}, bf16[512,512]{1,0:T(8,128)(2,1)S(1)}) custom-call(s32[2]{0:T(128)S(1)} %pad_add_fusion.refs_0_, f32[512,512]{1,0:T(8,128)S(1)} %collective-permute-done.refs_1_), custom_call_target="tpu_custom_call" | custom-call | flops 1000000000 | tf_op jit(solution)/shard_map/split/pallas_call | solution.py:52
  21.1 0.0 collective-permute-done.1.refs_2_.refs_1_
  21.1 1.4 %collective-permute-done.4.refs_0_.refs_4_ = f32[128,512]{1,0:T(8,128)S(1)} collective-permute-done((f32[128,512]{1,0:T(8,128)S(1)}, f32[128,512]{1,0:T(8,128)S(1)}, u32[]{:S(2)}, u32[]{:S(2)}) %collective-permute-start.4) | collective-permute-done | bytes 262176 | tf_op jit(solution)/shard_map/ppermute | solution.py:268
  22.6 0.1 collective-permute-start.6
  22.7 0.7 collective-permute-start.5
  23.4 4.0 %collective-permute-done.3.refs_4_ = f32[128,512]{1,0:T(8,128)S(1)} collective-permute-done((f32[128,512]{1,0:T(8,128)S(1)}, f32[128,512]{1,0:T(8,128)S(1)}, u32[]{:S(2)}, u32[]{:S(2)}) %collective-permute-start.3) | collective-permute-done | bytes 262176 | tf_op jit(solution)/shard_map/ppermute | solution.py:268
  27.4 2.5 %plan_part.1 = (f32[512,1024]{1,0:T(8,128)S(1)}, f32[512,1024]{1,0:T(8,128)S(1)}, bf16[256,1024]{1,0:T(8,128)(2,1)S(1)}, bf16[256,1024]{1,0:T(8,128)(2,1)S(1)}) custom-call(s32[2]{0:T(128)S(1)} %pad_add_fusion.refs_0_, f32[128,512]{1,0:T(8,128)S(1)} %copy.9.refs_1_, f32[128,512]{1,0:T(8,128)S(1)} %collective-permute-done.1.refs_2_.refs_1_, ...), custom_call_target="tpu_custom_call" | custom-call | flops 1000000000 | tf_op jit(solution)/shard_map/plan_part/pallas_call | solution.py:52
  29.9 0.0 collective-permute-done.6.refs_0_.refs_6_
  29.9 2.1 %collective-permute-start.7 = (f32[128,512]{1,0:T(8,128)S(1)}, f32[128,512]{1,0:T(8,128)S(1)}, u32[]{:S(2)}, u32[]{:S(2)}) collective-permute-start(f32[128,512]{1,0:T(8,128)S(1)} %copy.11), channel_id=1, source_target_pairs={{0,1},{1,0},{2,3},{3,2},{4,5},{5,4},{6,7},{7,6},{8,9},{9,8},{10,11... | collective-permute-start | bytes 786440 | tf_op jit(solution)/shard_map/ppermute | solution.py:268
  32.0 0.0 collective-permute-done.8.refs_1_
  32.0 0.0 collective-permute-start.9
  32.0 1.6 %split.6 = (bf16[512,512]{1,0:T(8,128)(2,1)S(1)}, bf16[512,512]{1,0:T(8,128)(2,1)S(1)}, bf16[512,512]{1,0:T(8,128)(2,1)S(1)}, bf16[512,512]{1,0:T(8,128)(2,1)S(1)}) custom-call(s32[2]{0:T(128)S(1)} %pad_add_fusion.refs_0_, f32[512,512]{1,0:T(8,128)} %collective-permute-done.8.refs_1_), custom_call_target="tpu_custom_call" | custom-call | flops 1000000000 | tf_op jit(solution)/shard_map/split/pallas_call | solution.py:52
  33.7 1.0 %plan_more.1.refs_4_ = f32[512,1024]{1,0:T(8,128)S(1)} custom-call(bf16[256,1024]{1,0:T(8,128)(2,1)S(1)} %get-tuple-element.50.refs_1_.refs_2_.refs_0_, bf16[256,1024]{1,0:T(8,128)(2,1)S(1)} %get-tuple-element.51.refs_3_.refs_1_, bf16[512,512]{1,0:T(8,128)(2,1)S(1)} %get-tuple-element.57.refs_2_.refs_5_, bf16[512,512]{1,0:T(8,128)(2,1)S(1)} %get-tuple-element.58.refs_3_.refs_7_), custom_call_target="tpu_custom_call" | custom-call | flops 1000000000 | tf_op jit(solution)/shard_map/plan_more/pallas_call | solution.py:52
  34.6 0.0 collective-permute-done.5.refs_5_
  34.6 2.7 %collective-permute-done.7.refs_7_ = f32[128,512]{1,0:T(8,128)S(1)} collective-permute-done((f32[128,512]{1,0:T(8,128)S(1)}, f32[128,512]{1,0:T(8,128)S(1)}, u32[]{:S(2)}, u32[]{:S(2)}) %collective-permute-start.7) | collective-permute-done | bytes 262176 | tf_op jit(solution)/shard_map/ppermute | solution.py:268
  37.3 2.9 %plan_early.1 = (f32[1024,512]{1,0:T(8,128)S(1)}, f32[1024,512]{1,0:T(8,128)S(1)}, f32[8,128]{1,0:T(8,128)S(1)}, bf16[512,1024]{1,0:T(8,128)(2,1)S(1)}, bf16[512,1024]{1,0:T(8,128)(2,1)S(1)}) custom-call(s32[2]{0:T(128)S(1)} %pad_add_fusion.refs_0_, f32[2048,128]{1,0:T(8,128)S(1)} %offsets.1.refs_3_.refs_1_.refs_0_, ...), custom_call_target="tpu_custom_call" | custom-call | flops 99999997952 | tf_op jit(solution)/shard_map/plan_early/pallas_call | solution.py:52
  40.3 0.0 collective-permute-done.9.refs_1_
  40.3 0.9 %split.7 = (bf16[512,512]{1,0:T(8,128)(2,1)S(1)}, bf16[512,512]{1,0:T(8,128)(2,1)S(1)}, bf16[512,512]{1,0:T(8,128)(2,1)S(1)}, bf16[512,512]{1,0:T(8,128)(2,1)S(1)}) custom-call(s32[2]{0:T(128)S(1)} %pad_add_fusion.refs_0_, f32[512,512]{1,0:T(8,128)S(1)} %collective-permute-done.9.refs_1_), custom_call_target="tpu_custom_call" | custom-call | flops 1000000000 | tf_op jit(solution)/shard_map/split/pallas_call | solution.py:52
  41.2 2.8 %plan_late.1 = (f32[1024,512]{1,0:T(8,128)S(1)}, f32[1024,512]{1,0:T(8,128)S(1)}, f32[8,128]{1,0:T(8,128)S(1)}) custom-call(f32[2048,128]{1,0:T(8,128)S(1)} %offsets.1.refs_3_.refs_1_.refs_0_, f32[8,128]{1,0:T(8,128)S(1)} %get-tuple-element.54.refs_1_, bf16[512,1024]{1,0:T(8,128)(2,1)S(1)} %get-tuple-element.55.refs_2_.refs_1_, ...), custom_call_target="tpu_custom_call" | custom-call | flops 3000000000 | tf_op jit(solution)/shard_map/plan_late/pallas_call | solution.py:52
  44.0 1.8 %collective-permute-start.10 = (f32[8,128]{1,0:T(8,128)S(1)}, f32[8,128]{1,0:T(8,128)S(1)}, u32[]{:S(2)}, u32[]{:S(2)}) collective-permute-start(f32[8,128]{1,0:T(8,128)S(1)} %get-tuple-element.61.refs_0_.refs_5_.refs_1_), channel_id=1, source_target_pairs={{0,1},{1,0},{2,3},{3,2},{4,5},{5,4},{6,7},{7,6},{8,9},{9,8},{10,11... | collective-permute-start | bytes 12296 | tf_op jit(solution)/shard_map/ppermute | solution.py:268
  45.8 1.9 %moments.2.refs_2_.refs_5_ = f32[512,1024]{1,0:T(8,128)S(1)} custom-call(f32[8,128]{1,0:T(8,128)S(1)} %get-tuple-element.61.refs_0_.refs_5_.refs_1_, f32[1024,512]{1,0:T(8,128)S(1)} %get-tuple-element.62.refs_1_, f32[1024,512]{1,0:T(8,128)S(1)} %get-tuple-element.63.refs_2_, bf16[512,512]{1,0:T(8,128)(2,1)S(1)} %get-tuple-element.64.refs_3_, ...), custom_call_target="tpu_custom_call" | custom-call | flops 6000000000 | tf_op jit(solution)/shard_map/moments/pallas_call | solution.py:52
  47.7 0.0 collective-permute-done.10.refs_1_
  47.8 0.1 collective-permute-start.11
  47.8 1.9 %moments.3.refs_2_.refs_3_ = f32[512,1024]{1,0:T(8,128)S(1)} custom-call(f32[8,128]{1,0:T(8,128)S(1)} %get-tuple-element.61.refs_0_.refs_5_.refs_1_, f32[1024,512]{1,0:T(8,128)S(1)} %get-tuple-element.62.refs_1_, f32[1024,512]{1,0:T(8,128)S(1)} %get-tuple-element.63.refs_2_, bf16[512,512]{1,0:T(8,128)(2,1)S(1)} %get-tuple-element.66.refs_3_, ...), custom_call_target="tpu_custom_call" | custom-call | flops 6000000000 | tf_op jit(solution)/shard_map/moments/pallas_call | solution.py:52
  49.7 1.7 %collective-permute-done.11.refs_1_ = f32[8,128]{1,0:T(8,128)S(1)} collective-permute-done((f32[8,128]{1,0:T(8,128)S(1)}, f32[8,128]{1,0:T(8,128)S(1)}, u32[]{:S(2)}, u32[]{:S(2)}) %collective-permute-start.11) | collective-permute-done | bytes 4128 | tf_op jit(solution)/shard_map/ppermute | solution.py:268
  51.5 1.4 %collective-permute-start.12 = (f32[8,128]{1,0:T(8,128)S(1)}, f32[8,128]{1,0:T(8,128)S(1)}, u32[]{:S(2)}, u32[]{:S(2)}) collective-permute-start(f32[8,128]{1,0:T(8,128)S(1)} %hop.4.refs_0_.refs_3_), channel_id=1, source_target_pairs={{0,4},{1,5},{2,6},{3,7},{4,0},{5,1},{6,2},{7,3},{8,12},{9,13},{10,... | collective-permute-start | bytes 12296 | tf_op jit(solution)/shard_map/ppermute | solution.py:268
  52.9 1.7 %frames_first.1 = (bf16[1024,512]{1,0:T(8,128)(2,1)S(1)}, bf16[1024,512]{1,0:T(8,128)(2,1)S(1)}) custom-call(s32[2]{0:T(128)S(1)} %pad_add_fusion.refs_0_, bf16[512,1024]{1,0:T(8,128)(2,1)S(1)} %get-tuple-element.55.refs_2_.refs_1_, bf16[512,1024]{1,0:T(8,128)(2,1)S(1)} %get-tuple-element.56.refs_3_.refs_2_, f32[8,128]{1,0:T(8,128)S(1)} %hop.4.refs_0_.refs_3_), custom_call_target="tpu_custom_call" | custom-call | flops 1000000000 | tf_op jit(solution)/shard_map/frames_first/pallas_call | solution.py:52
  54.6 1.4 %collective-permute-done.12.refs_1_ = f32[8,128]{1,0:T(8,128)S(1)} collective-permute-done((f32[8,128]{1,0:T(8,128)S(1)}, f32[8,128]{1,0:T(8,128)S(1)}, u32[]{:S(2)}, u32[]{:S(2)}) %collective-permute-start.12) | collective-permute-done | bytes 4128 | tf_op jit(solution)/shard_map/ppermute | solution.py:268
  56.0 1.8 %text_far.2.refs_10_.refs_5_ = f32[512,512]{1,0:T(8,128)S(1)} custom-call(f32[8,128]{1,0:T(8,128)S(1)} %hop.5.refs_0_.refs_2_, f32[1024,512]{1,0:T(8,128)S(1)} %get-tuple-element.68.refs_1_.refs_4_, f32[1024,512]{1,0:T(8,128)S(1)} %get-tuple-element.69.refs_2_.refs_5_, bf16[1024,512]{1,0:T(8,128)(2,1)S(1)} %get-tuple-element.74.refs_3_, ...), custom_call_target="tpu_custom_call" | custom-call | tf_op jit(solution)/shard_map/text_far/pallas_call | solution.py:52
  57.8 0.1 collective-permute-start.20
  57.9 1.8 %text_far.3 = f32[512,512]{1,0:T(8,128)S(1)} custom-call(f32[8,128]{1,0:T(8,128)S(1)} %hop.5.refs_0_.refs_2_, f32[1024,512]{1,0:T(8,128)S(1)} %get-tuple-element.68.refs_1_.refs_4_, f32[1024,512]{1,0:T(8,128)S(1)} %get-tuple-element.69.refs_2_.refs_5_, bf16[1024,512]{1,0:T(8,128)(2,1)S(1)} %get-tuple-element.74.refs_3_, ...), custom_call_target="tpu_custom_call" | custom-call | tf_op jit(solution)/shard_map/text_far/pallas_call | solution.py:52
  59.7 0.8 collective-permute-done.20
  60.5 0.2 add.4.refs_7_
  60.7 1.6 %collective-permute-start.21 = (f32[512,512]{1,0:T(8,128)S(1)}, f32[512,512]{1,0:T(8,128)S(1)}, u32[]{:S(2)}, u32[]{:S(2)}) collective-permute-start(f32[512,512]{1,0:T(8,128)S(1)} %add.4.refs_7_), channel_id=1, source_target_pairs={{0,16},{8,24},{16,0},{24,8},{1,17},{9,25},{17,1},{25,9},{2,18},{10... | collective-permute-start | bytes 3145736 | tf_op jit(solution)/shard_map/ppermute | solution.py:268
  62.3 2.7 %finish.1 = (f32[4,64,256]{2,1,0:T(8,128)S(1)}, f32[4,64,256]{2,1,0:T(8,128)S(1)}, f32[4,64,256]{2,1,0:T(8,128)S(1)}, f32[4,64,256]{2,1,0:T(8,128)S(1)}) custom-call(s32[2]{0:T(128)S(1)} %pad_add_fusion.refs_0_, f32[8,128]{1,0:T(8,128)S(1)} %get-tuple-element.61.refs_0_.refs_5_.refs_1_, f32[8,128]{1,0:T(8,128)S(1)} %hop.5.refs_0_.refs_2_, ...), custom_call_target="tpu_custom_call" | custom-call | tf_op jit(solution)/shard_map/finish/pallas_call | solution.py:52
  65.0 1.7 %collective-permute-start.13 = (f32[4,64,256]{2,1,0:T(8,128)S(1)}, f32[4,64,256]{2,1,0:T(8,128)S(1)}, u32[]{:S(2)}, u32[]{:S(2)}) collective-permute-start(f32[4,64,256]{2,1,0:T(8,128)S(1)} %get-tuple-element.77), channel_id=1, source_target_pairs={{0,1},{1,0},{2,3},{3,2},{4,5},{5,4},{6,7},{7,6},{8,9},{9,8},{10,11... | collective-permute-start | bytes 786440 | tf_op jit(solution)/shard_map/ppermute | solution.py:268
  66.7 0.4 collective-permute-start.15
  67.1 1.8 %text_near.2 = (f32[256,512]{1,0:T(8,128)S(1)}, f32[256,512]{1,0:T(8,128)S(1)}) custom-call(f32[8,128]{1,0:T(8,128)S(1)} %hop.5.refs_0_.refs_2_, f32[1024,512]{1,0:T(8,128)S(1)} %get-tuple-element.62.refs_1_, f32[1024,512]{1,0:T(8,128)S(1)} %get-tuple-element.63.refs_2_, bf16[1024,512]{1,0:T(8,128)(2,1)S(1)} %get-tuple-element.74.refs_3_, ...), custom_call_target="tpu_custom_call" | custom-call | tf_op jit(solution)/shard_map/text_near/pallas_call | solution.py:52
  68.9 0.1 collective-permute-start.18
  69.0 0.5 collective-permute-start.19
  69.5 3.7 %collective-permute-done.13.refs_1_ = f32[4,64,256]{2,1,0:T(8,128)S(1)} collective-permute-done((f32[4,64,256]{2,1,0:T(8,128)S(1)}, f32[4,64,256]{2,1,0:T(8,128)S(1)}, u32[]{:S(2)}, u32[]{:S(2)}) %collective-permute-start.13) | collective-permute-done | bytes 262176 | tf_op jit(solution)/shard_map/ppermute | solution.py:268
  73.2 0.4 collective-permute-start.14
  73.6 0.8 collective-permute-done.15.refs_1_
  74.5 0.8 collective-permute-start.16
  75.3 2.9 %collective-permute-done.14.refs_1_ = f32[2,64,256]{2,1,0:T(8,128)S(1)} collective-permute-done((f32[2,64,256]{2,1,0:T(8,128)S(1)}, f32[2,64,256]{2,1,0:T(8,128)S(1)}, u32[]{:S(2)}, u32[]{:S(2)}) %collective-permute-start.14) | collective-permute-done | bytes 131104 | tf_op jit(solution)/shard_map/ppermute | solution.py:268
  78.2 1.3 %collective-permute-done.16.refs_3_ = f32[2,64,256]{2,1,0:T(8,128)S(1)} collective-permute-done((f32[2,64,256]{2,1,0:T(8,128)S(1)}, f32[2,64,256]{2,1,0:T(8,128)S(1)}, u32[]{:S(2)}, u32[]{:S(2)}) %collective-permute-start.16) | collective-permute-done | bytes 131104 | tf_op jit(solution)/shard_map/ppermute | solution.py:268
  79.5 1.9 %collective-permute-start.17 = (f32[64,512]{1,0:T(8,128)S(1)}, f32[64,512]{1,0:T(8,128)S(1)}, u32[]{:S(2)}, u32[]{:S(2)}) collective-permute-start(f32[64,512]{1,0:T(8,128)S(1)} %bitcast.8), channel_id=1, source_target_pairs={{0,4},{1,5},{2,6},{3,7},{4,0},{5,1},{6,2},{7,3},{8,12},{9,13},{10,... | collective-permute-start | bytes 393224 | tf_op jit(solution)/shard_map/ppermute | solution.py:268
  81.4 0.0 collective-permute-done.18.refs_5_
  81.4 0.0 collective-permute-done.19.refs_6_
  81.4 1.8 %text_near.3.refs_2_ = f32[512,512]{1,0:T(8,128)S(1)} custom-call(f32[8,128]{1,0:T(8,128)S(1)} %hop.5.refs_0_.refs_2_, f32[1024,512]{1,0:T(8,128)S(1)} %get-tuple-element.62.refs_1_, f32[1024,512]{1,0:T(8,128)S(1)} %get-tuple-element.63.refs_2_, bf16[1024,512]{1,0:T(8,128)(2,1)S(1)} %get-tuple-element.74.refs_3_, ...), custom_call_target="tpu_custom_call" | custom-call | tf_op jit(solution)/shard_map/text_near/pallas_call | solution.py:52
  83.3 3.6 %collective-permute-done.17.refs_1_ = f32[64,512]{1,0:T(8,128)S(1)} collective-permute-done((f32[64,512]{1,0:T(8,128)S(1)}, f32[64,512]{1,0:T(8,128)S(1)}, u32[]{:S(2)}, u32[]{:S(2)}) %collective-permute-start.17) | collective-permute-done | bytes 131104 | tf_op jit(solution)/shard_map/ppermute | solution.py:268
  86.9 1.2 %add.7 = (f32[512,512]{1,0:T(8,128)}, f32[64,512]{1,0:T(8,128)}) custom-call(f32[64,512]{1,0:T(8,128)S(1)} %bitcast.7, f32[64,512]{1,0:T(8,128)S(1)} %collective-permute-done.17.refs_1_, f32[512,512]{1,0:T(8,128)S(1)} %text_near.3.refs_2_, f32[512,512]{1,0:T(8,128)S(1)} %collective-permute-done.21.refs_3_), custom_call_target="tpu_custom_call" | custom-call | flops 99999997952 | tf_op jit(solution)/shard_map/add/pallas_call | solution.py:52
  (15 shorter events, 0.2 us)
Async XLA Ops:
  0.6 11.1 %copy-start = (f32[512,512]{1,0:T(8,128)S(1)}, f32[512,512]{1,0:T(8,128)}, u32[]{:S(2)}) copy-start(f32[512,512]{1,0:T(8,128)} %refs_1_.1) | copy-start | bytes 3145732
  0.6 6.1 %copy-start.1 = (f32[2048]{0:T(1024)S(1)}, f32[2048]{0:T(1024)}, u32[]{:S(2)}) copy-start(f32[2048]{0:T(1024)} %param.6) | copy-start | bytes 24580
  0.7 4.1 %collective-permute-start = (f32[512,512]{1,0:T(8,128)}, f32[512,512]{1,0:T(8,128)S(1)}, u32[]{:S(2)}, u32[]{:S(2)}) collective-permute-start(f32[512,512]{1,0:T(8,128)} %refs_1_.1), channel_id=1, source_target_pairs={{0,8},{8,0},{16,24},{24,16},{1,9},{9,1},{17,25},{25,17},{2,10},{10... | collective-permute-start | bytes 3145736 | tf_op jit(solution)/shard_map/ppermute | solution.py:268
  1.2 30.9 %collective-permute-start.8 = (f32[512,512]{1,0:T(8,128)}, f32[512,512]{1,0:T(8,128)}, u32[]{:S(2)}, u32[]{:S(2)}) collective-permute-start(f32[512,512]{1,0:T(8,128)} %refs_1_.1), channel_id=1, source_target_pairs={{0,16},{8,24},{16,0},{24,8},{1,17},{9,25},{17,1},{25,9},{2,18},{10... | collective-permute-start | bytes 3145736 | tf_op jit(solution)/shard_map/ppermute | solution.py:268
  4.8 12.8 %collective-permute-start.2 = (f32[128,512]{1,0:T(8,128)S(1)}, f32[128,512]{1,0:T(8,128)S(1)}, u32[]{:S(2)}, u32[]{:S(2)}) collective-permute-start(f32[128,512]{1,0:T(8,128)S(1)} %copy.9.refs_1_), channel_id=1, source_target_pairs={{0,2},{1,3},{2,0},{3,1},{4,6},{5,7},{6,4},{7,5},{8,10},{9,11},{10,... | collective-permute-start | bytes 786440 | tf_op jit(solution)/shard_map/ppermute | solution.py:268
  6.7 14.4 %collective-permute-start.1 = (f32[128,512]{1,0:T(8,128)S(1)}, f32[128,512]{1,0:T(8,128)S(1)}, u32[]{:S(2)}, u32[]{:S(2)}) collective-permute-start(f32[128,512]{1,0:T(8,128)S(1)} %copy.9.refs_1_), channel_id=1, source_target_pairs={{0,1},{1,0},{2,3},{3,2},{4,5},{5,4},{6,7},{7,6},{8,9},{9,8},{10,11... | collective-permute-start | bytes 786440 | tf_op jit(solution)/shard_map/ppermute | solution.py:268
  8.2 14.4 %collective-permute-start.4 = (f32[128,512]{1,0:T(8,128)S(1)}, f32[128,512]{1,0:T(8,128)S(1)}, u32[]{:S(2)}, u32[]{:S(2)}) collective-permute-start(f32[128,512]{1,0:T(8,128)S(1)} %copy.9.refs_1_), channel_id=1, source_target_pairs={{0,4},{1,5},{2,6},{3,7},{4,0},{5,1},{6,2},{7,3},{8,12},{9,13},{10,... | collective-permute-start | bytes 786440 | tf_op jit(solution)/shard_map/ppermute | solution.py:268
  17.6 9.8 %collective-permute-start.3 = (f32[128,512]{1,0:T(8,128)S(1)}, f32[128,512]{1,0:T(8,128)S(1)}, u32[]{:S(2)}, u32[]{:S(2)}) collective-permute-start(f32[128,512]{1,0:T(8,128)S(1)} %collective-permute-done.2.refs_3_.refs_2_), channel_id=1, source_target_pairs={{0,1},{1,0},{2,3},{3,2},{4,5},{5,4},{6,7},{7,6},{8,9},{9,8},{10,11... | collective-permute-start | bytes 786440 | tf_op jit(solution)/shard_map/ppermute | solution.py:268
  22.6 7.3 %collective-permute-start.6 = (f32[128,512]{1,0:T(8,128)S(1)}, f32[128,512]{1,0:T(8,128)S(1)}, u32[]{:S(2)}, u32[]{:S(2)}) collective-permute-start(f32[128,512]{1,0:T(8,128)S(1)} %copy.10), channel_id=1, source_target_pairs={{0,2},{1,3},{2,0},{3,1},{4,6},{5,7},{6,4},{7,5},{8,10},{9,11},{10,... | collective-permute-start | bytes 786440 | tf_op jit(solution)/shard_map/ppermute | solution.py:268
  22.7 12.0 %collective-permute-start.5 = (f32[128,512]{1,0:T(8,128)S(1)}, f32[128,512]{1,0:T(8,128)S(1)}, u32[]{:S(2)}, u32[]{:S(2)}) collective-permute-start(f32[128,512]{1,0:T(8,128)S(1)} %collective-permute-done.4.refs_0_.refs_4_), channel_id=1, source_target_pairs={{0,1},{1,0},{2,3},{3,2},{4,5},{5,4},{6,7},{7,6},{8,9},{9,8},{10,11... | collective-permute-start | bytes 786440 | tf_op jit(solution)/shard_map/ppermute | solution.py:268
  29.9 7.4 %collective-permute-start.7 = (f32[128,512]{1,0:T(8,128)S(1)}, f32[128,512]{1,0:T(8,128)S(1)}, u32[]{:S(2)}, u32[]{:S(2)}) collective-permute-start(f32[128,512]{1,0:T(8,128)S(1)} %copy.11), channel_id=1, source_target_pairs={{0,1},{1,0},{2,3},{3,2},{4,5},{5,4},{6,7},{7,6},{8,9},{9,8},{10,11... | collective-permute-start | bytes 786440 | tf_op jit(solution)/shard_map/ppermute | solution.py:268
  32.0 8.2 %collective-permute-start.9 = (f32[512,512]{1,0:T(8,128)}, f32[512,512]{1,0:T(8,128)S(1)}, u32[]{:S(2)}, u32[]{:S(2)}) collective-permute-start(f32[512,512]{1,0:T(8,128)} %collective-permute-done.8.refs_1_), channel_id=1, source_target_pairs={{0,8},{8,0},{16,24},{24,16},{1,9},{9,1},{17,25},{25,17},{2,10},{10... | collective-permute-start | bytes 3145736 | tf_op jit(solution)/shard_map/ppermute | solution.py:268
  44.0 3.7 %collective-permute-start.10 = (f32[8,128]{1,0:T(8,128)S(1)}, f32[8,128]{1,0:T(8,128)S(1)}, u32[]{:S(2)}, u32[]{:S(2)}) collective-permute-start(f32[8,128]{1,0:T(8,128)S(1)} %get-tuple-element.61.refs_0_.refs_5_.refs_1_), channel_id=1, source_target_pairs={{0,1},{1,0},{2,3},{3,2},{4,5},{5,4},{6,7},{7,6},{8,9},{9,8},{10,11... | collective-permute-start | bytes 12296 | tf_op jit(solution)/shard_map/ppermute | solution.py:268
  47.8 3.7 %collective-permute-start.11 = (f32[8,128]{1,0:T(8,128)S(1)}, f32[8,128]{1,0:T(8,128)S(1)}, u32[]{:S(2)}, u32[]{:S(2)}) collective-permute-start(f32[8,128]{1,0:T(8,128)S(1)} %hop.3.refs_6_.refs_0_), channel_id=1, source_target_pairs={{0,2},{1,3},{2,0},{3,1},{4,6},{5,7},{6,4},{7,5},{8,10},{9,11},{10,... | collective-permute-start | bytes 12296 | tf_op jit(solution)/shard_map/ppermute | solution.py:268
  51.5 4.5 %collective-permute-start.12 = (f32[8,128]{1,0:T(8,128)S(1)}, f32[8,128]{1,0:T(8,128)S(1)}, u32[]{:S(2)}, u32[]{:S(2)}) collective-permute-start(f32[8,128]{1,0:T(8,128)S(1)} %hop.4.refs_0_.refs_3_), channel_id=1, source_target_pairs={{0,4},{1,5},{2,6},{3,7},{4,0},{5,1},{6,2},{7,3},{8,12},{9,13},{10,... | collective-permute-start | bytes 12296 | tf_op jit(solution)/shard_map/ppermute | solution.py:268
  57.8 2.7 %collective-permute-start.20 = (f32[512,512]{1,0:T(8,128)S(1)}, f32[512,512]{1,0:T(8,128)S(1)}, u32[]{:S(2)}, u32[]{:S(2)}) collective-permute-start(f32[512,512]{1,0:T(8,128)S(1)} %text_far.2.refs_10_.refs_5_), channel_id=1, source_target_pairs={{0,8},{8,0},{16,24},{24,16},{1,9},{9,1},{17,25},{25,17},{2,10},{10... | collective-permute-start | bytes 3145736 | tf_op jit(solution)/shard_map/ppermute | solution.py:268
  60.7 26.1 %collective-permute-start.21 = (f32[512,512]{1,0:T(8,128)S(1)}, f32[512,512]{1,0:T(8,128)S(1)}, u32[]{:S(2)}, u32[]{:S(2)}) collective-permute-start(f32[512,512]{1,0:T(8,128)S(1)} %add.4.refs_7_), channel_id=1, source_target_pairs={{0,16},{8,24},{16,0},{24,8},{1,17},{9,25},{17,1},{25,9},{2,18},{10... | collective-permute-start | bytes 3145736 | tf_op jit(solution)/shard_map/ppermute | solution.py:268
  65.0 8.1 %collective-permute-start.13 = (f32[4,64,256]{2,1,0:T(8,128)S(1)}, f32[4,64,256]{2,1,0:T(8,128)S(1)}, u32[]{:S(2)}, u32[]{:S(2)}) collective-permute-start(f32[4,64,256]{2,1,0:T(8,128)S(1)} %get-tuple-element.77), channel_id=1, source_target_pairs={{0,1},{1,0},{2,3},{3,2},{4,5},{5,4},{6,7},{7,6},{8,9},{9,8},{10,11... | collective-permute-start | bytes 786440 | tf_op jit(solution)/shard_map/ppermute | solution.py:268
  66.7 7.8 %collective-permute-start.15 = (f32[4,64,256]{2,1,0:T(8,128)S(1)}, f32[4,64,256]{2,1,0:T(8,128)S(1)}, u32[]{:S(2)}, u32[]{:S(2)}) collective-permute-start(f32[4,64,256]{2,1,0:T(8,128)S(1)} %get-tuple-element.81), channel_id=1, source_target_pairs={{0,2},{1,3},{2,0},{3,1},{4,6},{5,7},{6,4},{7,5},{8,10},{9,11},{10,... | collective-permute-start | bytes 786440 | tf_op jit(solution)/shard_map/ppermute | solution.py:268
  68.9 12.6 %collective-permute-start.18 = (f32[256,512]{1,0:T(8,128)S(1)}, f32[256,512]{1,0:T(8,128)S(1)}, u32[]{:S(2)}, u32[]{:S(2)}) collective-permute-start(f32[256,512]{1,0:T(8,128)S(1)} %get-tuple-element.86), channel_id=1, source_target_pairs={{0,8},{8,0},{16,24},{24,16},{1,9},{9,1},{17,25},{25,17},{2,10},{10... | collective-permute-start | bytes 1572872 | tf_op jit(solution)/shard_map/ppermute | solution.py:268
  69.0 12.5 %collective-permute-start.19 = (f32[256,512]{1,0:T(8,128)S(1)}, f32[256,512]{1,0:T(8,128)S(1)}, u32[]{:S(2)}, u32[]{:S(2)}) collective-permute-start(f32[256,512]{1,0:T(8,128)S(1)} %get-tuple-element.87), channel_id=1, source_target_pairs={{0,8},{8,0},{16,24},{24,16},{1,9},{9,1},{17,25},{25,17},{2,10},{10... | collective-permute-start | bytes 1572872 | tf_op jit(solution)/shard_map/ppermute | solution.py:268
  73.2 5.0 %collective-permute-start.14 = (f32[2,64,256]{2,1,0:T(8,128)S(1)}, f32[2,64,256]{2,1,0:T(8,128)S(1)}, u32[]{:S(2)}, u32[]{:S(2)}) collective-permute-start(f32[2,64,256]{2,1,0:T(8,128)S(1)} %get-tuple-element.79), channel_id=1, source_target_pairs={{0,2},{1,3},{2,0},{3,1},{4,6},{5,7},{6,4},{7,5},{8,10},{9,11},{10,... | collective-permute-start | bytes 393224 | tf_op jit(solution)/shard_map/ppermute | solution.py:268
  74.5 5.0 %collective-permute-start.16 = (f32[2,64,256]{2,1,0:T(8,128)S(1)}, f32[2,64,256]{2,1,0:T(8,128)S(1)}, u32[]{:S(2)}, u32[]{:S(2)}) collective-permute-start(f32[2,64,256]{2,1,0:T(8,128)S(1)} %get-tuple-element.83), channel_id=1, source_target_pairs={{0,1},{1,0},{2,3},{3,2},{4,5},{5,4},{6,7},{7,6},{8,9},{9,8},{10,11... | collective-permute-start | bytes 393224 | tf_op jit(solution)/shard_map/ppermute | solution.py:268
  79.5 7.3 %collective-permute-start.17 = (f32[64,512]{1,0:T(8,128)S(1)}, f32[64,512]{1,0:T(8,128)S(1)}, u32[]{:S(2)}, u32[]{:S(2)}) collective-permute-start(f32[64,512]{1,0:T(8,128)S(1)} %bitcast.8), channel_id=1, source_target_pairs={{0,4},{1,5},{2,6},{3,7},{4,0},{5,1},{6,2},{7,3},{8,12},{9,13},{10,... | collective-permute-start | bytes 393224 | tf_op jit(solution)/shard_map/ppermute | solution.py:268
